TPU v7x, 128 devices: a whole 4x4x4 slice. The times are simulated.
128 devices in a mesh: gx: 8 (over y, core), gy: 16 (over x, z).
Axes of the slice: x: 4, y: 4, z: 4, core: 2. Of those that a mesh axis runs over, the one named last changes fastest.
Arguments:
- parent: float32 [5, 20, 256, 2048], P(None, None, 'gx', 'gy'), may hold values from -6 to 6
- metric: float32 [256, 2048], P('gx', 'gy'), may hold values from 0.5 to 1.5
- buoyancy: float32 [20], replicated, may hold values from 0.1 to 0.9
- nest: float32 [5, 20, 192, 2048], P(None, None, 'gx', 'gy'), may hold values from -6 to 6
- nest_metric: float32 [192, 2048], P('gx', 'gy'), may hold values from 0.5 to 1.5
- strip_col: int32 [131072], P(('gx', 'gy')), may hold values from 0 to 4095
- strip_dest: int32 [131072, 1], P(('gx', 'gy')), may hold values from 0 to 127; in each aligned block of 1024 rows (0 to 1023, 1024 to 2047, ...) at most 32 rows name the same one
- strip_pos: int32 [131072], P(('gx', 'gy')), may hold values from 0 to 3071
- panel_src: int32 [131072], P(('gx', 'gy')), may hold values from 0 to 3071
- panel_dest: int32 [131072, 1], P(('gx', 'gy')), may hold values from 0 to 127; in each aligned block of 1024 rows (0 to 1023, 1024 to 2047, ...) at most 32 rows name the same one
- panel_col: int32 [131072], P(('gx', 'gy')), may hold values from 0 to 4095
Outputs:
- parent_out: float32 [5, 20, 256, 2048], P(None, None, 'gx', 'gy')
- nest_out: float32 [5, 20, 192, 2048], P(None, None, 'gx', 'gy')
Inputs may be any that keep to these rules, and one draw needn't show every extreme that they name: `strip_dest`: among the 1024 rows of one device no device is named more than 32 times. `panel_dest`: among the 1024 rows of one device no device is named more than 32 times.
All inputs are finite; a program needn't handle non-finite values.
Results may differ from a plain program's by a relative error of at most 0.00002.
Values sent between devices are 32-bit elements; how exact they have to be, the bound alone decides.
No kernel may reach another device: no remote copies, remote signals or barrier semaphores. Data moves between devices by JAX's collectives and lax.ppermute only.
A program may use at most 128 MiB of HBM per device.

v0:
```python
import functools

import jax
import jax.numpy as jnp
from jax import lax
from jax.experimental import pallas as pl
from jax.experimental.pallas import tpu as pltpu
from jax.sharding import PartitionSpec as P

CAP = 32
NSP = 4
NSN = 6
COURANT = 0.35
WIDTH = NSP

ROW = 128
SPOT = 100
TALLY = 101
DEPTH = 256
VMEM_BYTES = 48 * 1024 * 1024


def slot_rows(dest):
    groups = dest.shape[0]
    dest = dest.astype(jnp.float32)
    shape = (ROW, ROW)
    earlier = lax.broadcasted_iota(jnp.int32, shape, 0) < lax.broadcasted_iota(jnp.int32, shape, 1)
    counts = [jnp.zeros((8, ROW), jnp.float32) for _ in range(groups)]
    for a in range(groups):
        column = jnp.broadcast_to(dest[a : a + 1], shape).T
        for b in range(a, groups):
            same = column == dest[b : b + 1]
            if a == b:
                same = same & earlier
            ones = jnp.where(same, 1.0, 0.0)
            counts[b] = counts[b] + jnp.sum(ones.reshape(ROW // 8, 8, ROW), axis=0)
    rank = jnp.concatenate([jnp.sum(c, axis=0, keepdims=True) for c in counts], 0)
    return (dest * CAP + rank).astype(jnp.int32)


def to_rows(fields, rows, channels, size_x):
    tail_row = lax.broadcasted_iota(jnp.int32, (ROW - channels, ROW), 0)
    tail = jnp.where(tail_row == TALLY - channels, 1.0, 0.0)
    for i in range(size_x):
        block = fields[pl.ds(i, channels, stride=size_x), :]
        rows[i * ROW : (i + 1) * ROW, :] = jnp.concatenate([block, tail], 0).T


def pack_rows(rows, picks, spots, slots, packed):
    lane = lax.broadcasted_iota(jnp.int32, (1, ROW), 1)
    empty = jnp.where(lane == SPOT, -1.0, 0.0)
    packed[...] = jnp.broadcast_to(empty, packed.shape)
    groups = slots.shape[0]

    def group(a, carry):
        def move(b, carry):
            r = a * ROW + b
            spot = jnp.full((1, ROW), spots[r], jnp.int32).astype(jnp.float32)
            row = rows[pl.ds(picks[r], 1), :]
            packed[pl.ds(slots[a, b], 1), :] = jnp.where(lane == SPOT, spot, row)
            return carry

        return lax.fori_loop(0, ROW, move, carry, unroll=16)

    lax.fori_loop(0, groups, group, 0)


def add_rows(moved, sums, size_x):
    sums[...] = jnp.zeros(sums.shape, jnp.float32)
    lane = lax.broadcasted_iota(jnp.int32, (16, 2 * ROW), 1)
    pick = jnp.where((lane == SPOT) | (lane == SPOT + ROW), 1.0, 0.0).astype(jnp.bfloat16)
    north = lax.broadcasted_iota(jnp.int32, (ROW, DEPTH), 0)
    step = 8

    def tile(t, carry):
        values = moved[pl.ds(pl.multiple_of(t * DEPTH, DEPTH), DEPTH), :]
        high = values.astype(jnp.bfloat16)
        low = (values - high.astype(jnp.float32)).astype(jnp.bfloat16)
        both = jnp.concatenate([high, low], 1)
        spot = lax.dot_general(
            pick, both, (((1,), (1,)), ((), ())), preferred_element_type=jnp.float32
        ).astype(jnp.int32)
        east, within = spot >> 7, spot & (ROW - 1)
        column = jnp.where(north == within[0:1], 1.0, 0.0).astype(jnp.bfloat16)
        column = column.reshape(ROW // 16, 16, DEPTH)
        for g in range(size_x // step):
            parts = []
            for i in range(g * step, (g + 1) * step):
                here = jnp.where(east == i, 1.0, 0.0).astype(jnp.bfloat16)
                parts.append((column * here[None]).reshape(ROW, DEPTH))
            block = slice(g * step * ROW, (g + 1) * step * ROW)
            sums[block, :] += jnp.dot(
                jnp.concatenate(parts, 0), both, preferred_element_type=jnp.float32
            )
        return carry

    lax.fori_loop(0, moved.shape[0] // DEPTH, tile, 0)


def relax(fields, sums, out, channels, size_x):
    for i in range(size_x):
        block = slice(i * ROW, (i + 1) * ROW)
        total = (sums[block, :ROW] + sums[block, ROW:]).T
        share = 1.0 / (1.0 + total[TALLY : TALLY + 1])
        where = pl.ds(i, channels, stride=size_x)
        out[where, :] = (fields[where, :] + total[:channels]) * share


def nest_step(state, metric, buoyancy, levels, size_x):
    shape = (size_x, ROW)
    row = lax.broadcasted_iota(jnp.int32, shape, 0)
    lane = lax.broadcasted_iota(jnp.int32, shape, 1)
    scaled = COURANT * metric[...]

    def at(field, k):
        start = (field * levels + k) * size_x
        return slice(start, start + size_x)

    w_below = jnp.zeros(shape, jnp.float32)
    p = state[at(4, 0), :]
    for k in range(levels):
        n = COURANT * buoyancy[k]
        p_above = state[at(4, k + 1), :] if k + 1 < levels else jnp.zeros(shape, jnp.float32)
        p_east = jnp.where(row == size_x - 1, 0.0, pltpu.roll(p, size_x - 1, 0))
        p_north = jnp.where(lane == ROW - 1, 0.0, pltpu.roll(p, ROW - 1, 1))
        u = state[at(0, k), :] - COURANT * (p_east - p)
        v = state[at(1, k), :] - COURANT * (p_north - p)
        edge = -COURANT * p
        u_west = jnp.where(row == 0, edge, pltpu.roll(u, 1, 0))
        v_south = jnp.where(lane == 0, edge, pltpu.roll(v, 1, 1))
        theta = state[at(3, k), :]
        w = state[at(2, k), :] - COURANT * (p_above - p) + n * theta
        state[at(0, k), :] = u
        state[at(1, k), :] = v
        state[at(2, k), :] = w
        state[at(3, k), :] = theta - n * w
        state[at(4, k), :] = p - scaled * ((u - u_west) + (v - v_south) + (w - w_below))
        w_below = w
        p = p_above


def strip_kernel(parent, dest, picks, spots, packed, rows, slots_v, slots, *, size_x):
    channels = parent.shape[0] // size_x
    slots_v[...] = slot_rows(dest[...])
    pltpu.sync_copy(slots_v, slots)
    to_rows(parent, rows, channels, size_x)
    pack_rows(rows, picks, spots, slots, packed)


def nest_kernel(
    moved, nest, metric, dest, buoyancy, picks, spots, out, packed, sums, rows, slots_v, slots,
    *, size_x
):
    channels = nest.shape[0] // size_x
    slots_v[...] = slot_rows(dest[...])
    pltpu.sync_copy(slots_v, slots)
    add_rows(moved, sums, size_x)
    relax(nest, sums, out, channels, size_x)

    def step(_, carry):
        nest_step(out, metric, buoyancy, channels // 5, size_x)
        return carry

    lax.fori_loop(0, NSN, step, 0)
    to_rows(out, rows, channels, size_x)
    pack_rows(rows, picks, spots, slots, packed)


def parent_kernel(edge, buoyancy, parent, rim, side, metric, out, state, scaled):
    channels, size_x = side.shape[0] - 1, metric.shape[0]
    levels = channels // 5
    tall = side.shape[1]
    shape = (tall, 2 * ROW)
    scaled[:size_x, :ROW] = COURANT * metric[...]
    scaled[size_x:, :ROW] = COURANT * rim[channels]
    scaled[:, ROW:] = COURANT * side[channels]

    def fill(c, carry):
        state[c, :size_x, :ROW] = parent[c]
        state[c, size_x:, :ROW] = rim[c]
        state[c, :, ROW:] = side[c]
        return carry

    lax.fori_loop(0, channels, fill, 0)
    row = lax.broadcasted_iota(jnp.int32, shape, 0)
    lane = lax.broadcasted_iota(jnp.int32, shape, 1)
    u_keep = jnp.where((row >= tall - WIDTH) & (edge[0] == 1), 0.0, 1.0)
    v_keep = jnp.where((lane >= 2 * ROW - WIDTH) & (edge[1] == 1), 0.0, 1.0)

    def step(_, carry):
        def level(k, w_below):
            n = COURANT * buoyancy[k]
            p = state[4 * levels + k]
            above = state[4 * levels + jnp.minimum(k + 1, levels - 1)]
            p_above = above * jnp.where(k + 1 < levels, 1.0, 0.0)
            u = state[k] - COURANT * (pltpu.roll(p, tall - 1, 0) - p)
            v = state[levels + k] - COURANT * (pltpu.roll(p, 2 * ROW - 1, 1) - p)
            theta = state[3 * levels + k]
            w = state[2 * levels + k] - COURANT * (p_above - p) + n * theta
            spread = (u - pltpu.roll(u, 1, 0)) + (v - pltpu.roll(v, 1, 1)) + (w - w_below)
            state[k] = u * u_keep
            state[levels + k] = v * v_keep
            state[2 * levels + k] = w
            state[3 * levels + k] = theta - n * w
            state[4 * levels + k] = p - scaled[...] * spread
            return w

        lax.fori_loop(0, levels, level, jnp.zeros(shape, jnp.float32))
        return carry

    lax.fori_loop(0, NSP, step, 0)

    def drain(c, carry):
        out[c] = state[c, :size_x, :ROW]
        return carry

    lax.fori_loop(0, channels, drain, 0)


def final_kernel(moved, parent, out, sums, *, size_x):
    channels = parent.shape[0] // size_x
    add_rows(moved, sums, size_x)
    relax(parent, sums, out, channels, size_x)


def vmem():
    return pl.BlockSpec(memory_space=pltpu.VMEM)


def smem():
    return pl.BlockSpec(memory_space=pltpu.SMEM)


def params():
    return pltpu.CompilerParams(vmem_limit_bytes=VMEM_BYTES)


def exchange(packed, devices):
    moved = lax.all_to_all(
        packed.reshape(devices, CAP, ROW), ("gx", "gy"), split_axis=0, concat_axis=0, tiled=True
    )
    return moved.reshape(devices * CAP, ROW)


def shifted(first, last, axis):
    size = lax.axis_size(axis)
    up = [(i, i + 1) for i in range(size - 1)]
    down = [(j, i) for i, j in up]
    return lax.ppermute(first, axis, down), lax.ppermute(last, axis, up)


def rims(parent, metric):
    channels, size_x, size_y = parent.shape
    first = jnp.concatenate([parent[:, :WIDTH], metric[None, :WIDTH]], 0)
    last = jnp.concatenate([parent[:, size_x - WIDTH :], metric[None, size_x - WIDTH :]], 0)
    after, before = shifted(first, last, "gx")
    rim = jnp.concatenate([after, before], 1)

    def strip(lanes):
        own = jnp.concatenate([parent[:, :, lanes], metric[None, :, lanes]], 0)
        return jnp.concatenate([own, rim[:, :, lanes]], 1)

    after, before = shifted(strip(slice(0, WIDTH)), strip(slice(size_y - WIDTH, size_y)), "gy")
    gap = jnp.zeros(after.shape[:2] + (ROW - 2 * WIDTH,), jnp.float32)
    return rim, jnp.concatenate([after, gap, before], 2)


def on_device(
    parent,
    metric,
    buoyancy,
    nest,
    nest_metric,
    strip_col,
    strip_dest,
    strip_pos,
    panel_src,
    panel_dest,
    panel_col,
):
    devices = lax.axis_size("gx") * lax.axis_size("gy")
    channels = parent.shape[0] * parent.shape[1]
    tile_x, tile_y = parent.shape[2:]
    block_x, block_y = nest.shape[2:]
    slots = strip_col.shape[0]
    packed_type = jax.ShapeDtypeStruct((devices * CAP, ROW), jnp.float32)
    index_scratch = [
        pltpu.VMEM((slots // ROW, ROW), jnp.int32),
        pltpu.SMEM((slots // ROW, ROW), jnp.int32),
    ]

    packed = pl.pallas_call(
        functools.partial(strip_kernel, size_x=tile_x),
        out_shape=packed_type,
        in_specs=[vmem(), vmem(), smem(), smem()],
        out_specs=vmem(),
        scratch_shapes=[pltpu.VMEM((tile_x * tile_y, ROW), jnp.float32)] + index_scratch,
        compiler_params=params(),
        name="pack_strips",
    )(
        parent.reshape(channels * tile_x, tile_y),
        strip_dest.reshape(slots // ROW, ROW),
        strip_col,
        strip_pos,
    )

    packed, late_parent, late_metric = lax.optimization_barrier((packed, parent, metric))
    moved = exchange(packed, devices)
    late_parent = late_parent.reshape(channels, tile_x, tile_y)
    rim, side = rims(late_parent, late_metric)
    edge = jnp.stack([lax.axis_index("gx") == 0, lax.axis_index("gy") == 0]).astype(jnp.int32)
    tall = tile_x + 2 * WIDTH
    parent_state = pl.pallas_call(
        parent_kernel,
        out_shape=jax.ShapeDtypeStruct((channels, tile_x, tile_y), jnp.float32),
        in_specs=[smem(), smem(), vmem(), vmem(), vmem(), vmem()],
        out_specs=vmem(),
        scratch_shapes=[
            pltpu.VMEM((channels, tall, 2 * ROW), jnp.float32),
            pltpu.VMEM((tall, 2 * ROW), jnp.float32),
        ],
        compiler_params=params(),
        cost_estimate=pl.CostEstimate(flops=20_000_000, bytes_accessed=8_000_000, transcendentals=0),
        name="step_parent",
    )(edge, buoyancy, late_parent, rim, side, late_metric)

    nest_out, packed = pl.pallas_call(
        functools.partial(nest_kernel, size_x=block_x),
        out_shape=(
            jax.ShapeDtypeStruct((channels * block_x, block_y), jnp.float32),
            packed_type,
        ),
        in_specs=[vmem(), vmem(), vmem(), vmem(), smem(), smem(), smem()],
        out_specs=(vmem(), vmem()),
        scratch_shapes=[
            pltpu.VMEM((block_x * block_y, 2 * ROW), jnp.float32),
            pltpu.VMEM((block_x * block_y, ROW), jnp.float32),
        ]
        + index_scratch,
        compiler_params=params(),
        name="step_nest",
    )(
        moved,
        nest.reshape(channels * block_x, block_y),
        nest_metric,
        panel_dest.reshape(slots // ROW, ROW),
        buoyancy,
        panel_src,
        panel_col,
    )
    moved = exchange(packed, devices)

    parent_out = pl.pallas_call(
        functools.partial(final_kernel, size_x=tile_x),
        out_shape=jax.ShapeDtypeStruct((channels * tile_x, tile_y), jnp.float32),
        in_specs=[vmem(), vmem()],
        out_specs=vmem(),
        scratch_shapes=[pltpu.VMEM((tile_x * tile_y, 2 * ROW), jnp.float32)],
        compiler_params=params(),
        name="add_panels",
    )(moved, parent_state.reshape(channels * tile_x, tile_y))
    return (parent_out.reshape(parent.shape), nest_out.reshape(nest.shape))


def solution(mesh):
    placed = (
        P(None, None, "gx", "gy"),
        P("gx", "gy"),
        P(),
        P(None, None, "gx", "gy"),
        P("gx", "gy"),
        P(("gx", "gy")),
        P(("gx", "gy"), None),
        P(("gx", "gy")),
        P(("gx", "gy")),
        P(("gx", "gy"), None),
        P(("gx", "gy")),
    )
    return jax.shard_map(
        on_device,
        mesh=mesh,
        in_specs=placed,
        out_specs=(P(None, None, "gx", "gy"), P(None, None, "gx", "gy")),
        check_vma=False,
    )
```

profile of v0, /device:TPU:13, one launch (start us, length us, event | category | flops | bytes accessed | tf_op | source)
XLA Modules:
  0.0 162.5 jit_solution(12059647401767891677)
XLA Ops:
  0.6 1.4 copy-done
  2.1 0.7 copy-done.10
  2.8 0.7 copy-done.11
  3.4 0.7 copy-done.12
  4.1 6.2 %pack_strips.1 = f32[4096,128]{1,0:T(8,128)S(1)} custom-call(f32[3200,128]{1,0:T(8,128)S(1)} %bitcast.22, s32[8,128]{1,0:T(8,128)S(1)} %bitcast.32, s32[1024]{0:T(1024)S(1)} %copy-done.11, s32[1024]{0:T(1024)S(1)} %copy-done.12), custom_call_target="tpu_custom_call" | custom-call | tf_op jit(solution)/shard_map/pack_strips/pallas_call | solution.py:292
  10.4 38.0 %all_to_all.10 = f32[128,32,128]{2,1,0:T(8,128)S(1)} all-to-all(f32[128,32,128]{2,1,0:T(8,128)S(1)} %bitcast.27), channel_id=1, replica_groups=mesh['gx'=8,'gy'=16] {'gx','gy'}, dimensions={0} | all-to-all | bytes 4194304 | tf_op jit(solution)/shard_map/all_to_all | solution.py:239
  48.4 22.0 %step_nest.1 = (f32[2400,128]{1,0:T(8,128)}, f32[4096,128]{1,0:T(8,128)S(1)}) custom-call(f32[4096,128]{1,0:T(8,128)S(1)} %bitcast.26, f32[2400,128]{1,0:T(8,128)S(1)} %bitcast.30, f32[24,128]{1,0:T(8,128)S(1)} %copy-done.6, s32[8,128]{1,0:T(8,128)S(1)} %bitcast.31, f32[20]{0:T(128)S(1)} %copy-done.13, s32[1024]{0:T(1024)S(1)} %copy-done.8, s32[1024]{0:T(1024)S(1)} %copy-done.9), custom_call_target="tpu_custom_call" | custom-call | tf_op jit(solution)/shard_map/step_nest/pallas_call | solution.py:327
  70.3 1.3 copy-done.2
  71.6 8.0 %all-to-all-start.1 = ((f32[128,32,128]{2,1,0:T(8,128)}), f32[128,32,128]{2,1,0:T(8,128)}, u32[]{:S(2)}, u32[]{:S(2)}) async-start(f32[128,32,128]{2,1,0:T(8,128)} %bitcast.29), calls=%async_computation.1 | async-start | bytes 4194304 | tf_op jit(solution)/shard_map/all_to_all | solution.py:239
  79.8 0.7 pad_maximum_fusion.2
  80.5 2.3 %collective-permute-start = (f32[101,4,128]{2,1,0:T(4,128)}, f32[101,4,128]{2,1,0:T(4,128)S(1)}, u32[]{:S(2)}, u32[]{:S(2)}) collective-permute-start(f32[101,4,128]{2,1,0:T(4,128)} %pad_maximum_fusion.2), channel_id=1, source_target_pairs={{16,0},{32,16},{48,32},{64,48},{80,64},{96,80},{112,96},{17,1},{33... | collective-permute-start | bytes 620552 | tf_op jit(solution)/shard_map/ppermute | solution.py:249
  82.8 0.8 pad_maximum_fusion.3
  83.6 3.3 %collective-permute-start.1 = (f32[101,4,128]{2,1,0:T(4,128)}, f32[101,4,128]{2,1,0:T(4,128)}, u32[]{:S(2)}, u32[]{:S(2)}) collective-permute-start(f32[101,4,128]{2,1,0:T(4,128)} %pad_maximum_fusion.3), channel_id=1, source_target_pairs={{0,16},{16,32},{32,48},{48,64},{64,80},{80,96},{96,112},{1,17},{17... | collective-permute-start | bytes 620552 | tf_op jit(solution)/shard_map/ppermute | solution.py:249
  86.8 1.8 %fusion.2 = (f32[100,32,4]{2,1,0:T(8,128)}, f32[100,32,4]{2,1,0:T(8,128)S(1)}) fusion(f32[100,32,128]{2,1,0:T(8,128)S(1)} %bitcast.24), kind=kLoop, calls=%fused_computation.17 | loop fusion | bytes 204800 | tf_op jit(solution)/shard_map/slice | solution.py:260
  88.7 2.9 %copy.18 = f32[100,32,4]{0,1,2:T(8,128)} copy(f32[100,32,4]{2,1,0:T(8,128)} %get-tuple-element.12) | data formatting | bytes 102400 | tf_op jit(solution)/shard_map/slice | solution.py:260
  91.6 1.0 copy.19
  92.6 1.8 %copy.22 = f32[100,32,4]{0,1,2:T(8,128)} copy(f32[100,32,4]{2,1,0:T(8,128)S(1)} %get-tuple-element.13) | data formatting | bytes 102400 | tf_op jit(solution)/shard_map/slice | solution.py:260
  94.3 0.3 copy.23
  94.8 11.0 %collective-permute-done = f32[101,4,128]{2,1,0:T(4,128)S(1)} collective-permute-done((f32[101,4,128]{2,1,0:T(4,128)}, f32[101,4,128]{2,1,0:T(4,128)S(1)}, u32[]{:S(2)}, u32[]{:S(2)}) %collective-permute-start) | collective-permute-done | bytes 206880 | tf_op jit(solution)/shard_map/ppermute | solution.py:249
  105.9 1.3 fusion
  107.2 0.2 copy.20
  107.4 1.0 pad_maximum_fusion.4
  108.4 5.0 %collective-permute-start.2 = (f32[101,40,4]{0,1,2:T(8,128)S(1)}, f32[101,40,4]{0,1,2:T(8,128)S(1)}, u32[]{:S(2)}, u32[]{:S(2)}) collective-permute-start(f32[101,40,4]{0,1,2:T(8,128)S(1)} %pad_maximum_fusion.4), channel_id=1, source_target_pairs={{1,0},{2,1},{3,2},{4,3},{5,4},{6,5},{7,6},{8,7},{9,8},{10,9},{11,1... | collective-permute-start | bytes 193928 | tf_op jit(solution)/shard_map/ppermute | solution.py:249
  113.3 0.2 copy.24
  113.7 2.1 %collective-permute-start.3 = (f32[101,40,4]{0,1,2:T(8,128)S(1)}, f32[101,40,4]{0,1,2:T(8,128)S(1)}, u32[]{:S(2)}, u32[]{:S(2)}) collective-permute-start(f32[101,40,4]{0,1,2:T(8,128)S(1)} %pad_maximum_fusion.5), channel_id=1, source_target_pairs={{0,1},{1,2},{2,3},{3,4},{4,5},{5,6},{6,7},{7,8},{8,9},{9,10},{10,1... | collective-permute-start | bytes 193928 | tf_op jit(solution)/shard_map/ppermute | solution.py:249
  115.8 1.8 %pad_maximum_fusion.1.rim = f32[101,8,128]{2,1,0:T(8,128)} fusion(f32[101,4,128]{2,1,0:T(4,128)} %collective-permute-done.1, f32[101,4,128]{2,1,0:T(4,128)S(1)} %collective-permute-done), kind=kLoop, calls=%fused_computation.3 | loop fusion | flops 103424 | bytes 827392 | tf_op jit(solution)/shard_map/concatenate | solution.py:257
  117.5 2.1 %copy.25 = f32[101,40,4]{2,1,0:T(8,128)} copy(f32[101,40,4]{0,1,2:T(8,128)S(1)} %collective-permute-done.2) | data formatting | bytes 129280 | tf_op jit(solution)/shard_map/ppermute | solution.py:249
  119.6 2.3 %collective-permute-done.3 = f32[101,40,4]{0,1,2:T(8,128)S(1)} collective-permute-done((f32[101,40,4]{0,1,2:T(8,128)S(1)}, f32[101,40,4]{0,1,2:T(8,128)S(1)}, u32[]{:S(2)}, u32[]{:S(2)}) %collective-permute-start.3) | collective-permute-done | bytes 64672 | tf_op jit(solution)/shard_map/ppermute | solution.py:249
  121.9 2.1 %copy.26 = f32[101,40,4]{2,1,0:T(8,128)} copy(f32[101,40,4]{0,1,2:T(8,128)S(1)} %collective-permute-done.3) | data formatting | bytes 129280 | tf_op jit(solution)/shard_map/ppermute | solution.py:249
  124.0 2.9 %pad_maximum_fusion.side = f32[101,40,128]{2,1,0:T(8,128)S(1)} fusion(f32[101,40,4]{2,1,0:T(8,128)} %copy.26, f32[101,40,4]{2,1,0:T(8,128)} %copy.25, f32[128]{0:T(128)S(1)} %pad.1.clone), kind=kLoop, calls=%fused_computation | loop fusion | flops 1034240 | bytes 2198272 | tf_op jit(solution)/shard_map/concatenate | solution.py:265
  126.8 15.2 %step_parent.1 = f32[100,32,128]{2,1,0:T(8,128)S(1)} custom-call(s32[2]{0:T(128)S(1)} %add_convert_fusion.edge, f32[20]{0:T(128)S(1)} %copy-done.13, f32[100,32,128]{2,1,0:T(8,128)S(1)} %bitcast.25, f32[101,8,128]{2,1,0:T(8,128)S(1)} %copy-done.3, f32[101,40,128]{2,1,0:T(8,128)S(1)} %pad_maximum_fusion.side, f32[32,128]{1,0:T(8,128)S(1)} %copy-done.5), custom_call_target="tpu_custom_call" | custom-call | flops 20000000 | bytes 8000000 | tf_op jit(solution)/shard_map/step_parent/pallas_call | solution.py:313
  142.1 20.4 %add_panels.1 = f32[3200,128]{1,0:T(8,128)} custom-call(f32[4096,128]{1,0:T(8,128)} %bitcast.7.moved, f32[3200,128]{1,0:T(8,128)S(1)} %bitcast.28), custom_call_target="tpu_custom_call" | custom-call | tf_op jit(solution)/shard_map/add_panels/pallas_call | solution.py:353
  (35 shorter events, 0.5 us)
Async XLA Ops:
  0.6 1.4 copy-start
  2.1 0.7 copy-start.10
  2.8 0.7 copy-start.11
  3.4 0.7 copy-start.12
  10.3 38.0 %copy-start.4 = (f32[5,20,24,128]{3,2,1,0:T(8,128)S(1)}, f32[5,20,24,128]{3,2,1,0:T(8,128)}, u32[]{:S(2)}) copy-start(f32[5,20,24,128]{3,2,1,0:T(8,128)} %param.14) | copy-start | bytes 3686404
  10.3 38.0 %copy-start.6 = (f32[24,128]{1,0:T(8,128)S(1)}, f32[24,128]{1,0:T(8,128)}, u32[]{:S(2)}) copy-start(f32[24,128]{1,0:T(8,128)} %metric.1) | copy-start | bytes 36868
  10.3 38.0 %copy-start.7 = (s32[1024,1]{0,1:T(1,128)S(1)}, s32[1024,1]{0,1:T(1,128)}, u32[]{:S(2)}) copy-start(s32[1024,1]{0,1:T(1,128)} %param.20) | copy-start | bytes 12292
  10.3 38.0 %copy-start.8 = (s32[1024]{0:T(1024)S(1)}, s32[1024]{0:T(1024)}, u32[]{:S(2)}) copy-start(s32[1024]{0:T(1024)} %picks.3) | copy-start | bytes 12292
  10.4 38.0 %copy-start.9 = (s32[1024]{0:T(1024)S(1)}, s32[1024]{0:T(1024)}, u32[]{:S(2)}) copy-start(s32[1024]{0:T(1024)} %spots.3) | copy-start | bytes 12292
  10.4 38.0 %copy-start.13 = (f32[20]{0:T(128)S(1)}, f32[20]{0:T(128)}, u32[]{:S(2)}) copy-start(f32[20]{0:T(128)} %buoyancy.3) | copy-start | bytes 244
  70.3 1.3 copy-start.2
  71.6 8.1 %copy-start.5 = (f32[32,128]{1,0:T(8,128)S(1)}, f32[32,128]{1,0:T(8,128)}, u32[]{:S(2)}) copy-start(f32[32,128]{1,0:T(8,128)} %metric.2) | copy-start | bytes 49156
  71.6 8.1 %copy-start.1 = (f32[5,20,32,128]{3,2,1,0:T(8,128)S(1)}, f32[5,20,32,128]{3,2,1,0:T(8,128)}, u32[]{:S(2)}) copy-start(f32[5,20,32,128]{3,2,1,0:T(8,128)} %param.11) | copy-start | bytes 4915204
  71.6 70.5 %all-to-all-start.1 = ((f32[128,32,128]{2,1,0:T(8,128)}), f32[128,32,128]{2,1,0:T(8,128)}, u32[]{:S(2)}, u32[]{:S(2)}) async-start(f32[128,32,128]{2,1,0:T(8,128)} %bitcast.29), calls=%async_computation.1 | async-start | bytes 4194304 | tf_op jit(solution)/shard_map/all_to_all | solution.py:239
  80.5 25.3 %collective-permute-start = (f32[101,4,128]{2,1,0:T(4,128)}, f32[101,4,128]{2,1,0:T(4,128)S(1)}, u32[]{:S(2)}, u32[]{:S(2)}) collective-permute-start(f32[101,4,128]{2,1,0:T(4,128)} %pad_maximum_fusion.2), channel_id=1, source_target_pairs={{16,0},{32,16},{48,32},{64,48},{80,64},{96,80},{112,96},{17,1},{33... | collective-permute-start | bytes 620552 | tf_op jit(solution)/shard_map/ppermute | solution.py:249
  83.6 22.3 %collective-permute-start.1 = (f32[101,4,128]{2,1,0:T(4,128)}, f32[101,4,128]{2,1,0:T(4,128)}, u32[]{:S(2)}, u32[]{:S(2)}) collective-permute-start(f32[101,4,128]{2,1,0:T(4,128)} %pad_maximum_fusion.3), channel_id=1, source_target_pairs={{0,16},{16,32},{32,48},{48,64},{64,80},{80,96},{96,112},{1,17},{17... | collective-permute-start | bytes 620552 | tf_op jit(solution)/shard_map/ppermute | solution.py:249
  94.3 19.2 %copy-start.14 = (f32[100,32,4]{0,1,2:T(8,128)S(1)}, f32[100,32,4]{0,1,2:T(8,128)}, u32[]{:S(2)}) copy-start(f32[100,32,4]{0,1,2:T(8,128)} %copy.22) | copy-start | bytes 153604
  108.4 9.2 %collective-permute-start.2 = (f32[101,40,4]{0,1,2:T(8,128)S(1)}, f32[101,40,4]{0,1,2:T(8,128)S(1)}, u32[]{:S(2)}, u32[]{:S(2)}) collective-permute-start(f32[101,40,4]{0,1,2:T(8,128)S(1)} %pad_maximum_fusion.4), channel_id=1, source_target_pairs={{1,0},{2,1},{3,2},{4,3},{5,4},{6,5},{7,6},{8,7},{9,8},{10,9},{11,1... | collective-permute-start | bytes 193928 | tf_op jit(solution)/shard_map/ppermute | solution.py:249
  113.7 8.2 %collective-permute-start.3 = (f32[101,40,4]{0,1,2:T(8,128)S(1)}, f32[101,40,4]{0,1,2:T(8,128)S(1)}, u32[]{:S(2)}, u32[]{:S(2)}) collective-permute-start(f32[101,40,4]{0,1,2:T(8,128)S(1)} %pad_maximum_fusion.5), channel_id=1, source_target_pairs={{0,1},{1,2},{2,3},{3,4},{4,5},{5,6},{6,7},{7,8},{8,9},{9,10},{10,1... | collective-permute-start | bytes 193928 | tf_op jit(solution)/shard_map/ppermute | solution.py:249
  124.0 2.9 %copy-start.3 = (f32[101,8,128]{2,1,0:T(8,128)S(1)}, f32[101,8,128]{2,1,0:T(8,128)}, u32[]{:S(2)}) copy-start(f32[101,8,128]{2,1,0:T(8,128)} %pad_maximum_fusion.1.rim) | copy-start | bytes 1241092
where the time goes:
time: 163 us; the launch traced here: 162 us
  Pallas kernels  63.8 us (39%)
  blocking collectives  38 us (23%)
  starting transfers between devices  20.6 us (13%)
  local copies, waits for them, and re-layouts  17.4 us (11%)
  waiting for transfers between devices  13.3 us (8%)
  other arithmetic  8.6 us (5%)
    all_to_all x1, blocking collectives, exchange(): lax.all_to_all(packed.reshape(devices, CAP, ROW), ('gx', 'gy'), split_axi...  38 us
    pallas_call x1, Pallas kernels, on_device(): pl.pallas_call(functools.partial(nest_kernel, size_x=block_x), out_shape=...  22 us
    pallas_call x1, Pallas kernels, on_device(): pl.pallas_call(functools.partial(final_kernel, size_x=tile_x), out_shape=...  20.4 us
    pallas_call x1, Pallas kernels, on_device(): pl.pallas_call(parent_kernel, out_shape=jax.ShapeDtypeStruct((channels, t...  15.2 us
    ppermute x4, waiting for transfers between devices, shifted(): return (lax.ppermute(first, axis, down), lax.ppermute(last, axis, up))  13.3 us
    ppermute x4, starting transfers between devices, shifted(): return (lax.ppermute(first, axis, down), lax.ppermute(last, axis, up))  12.6 us
    all_to_all x1, starting transfers between devices, exchange(): lax.all_to_all(packed.reshape(devices, CAP, ROW), ('gx', 'gy'), split_axi...  8.04 us
    slice x3, local copies, waits for them, and re-layouts, strip(): own = jnp.concatenate([parent[:, :, lanes], metric[None, :, lanes]], 0)  6.45 us
  transfers between devices with their start and end apart: 5, of which 2 were waited for; matrix products, arithmetic and copies ran while one was open for 13% of the time, Pallas kernels for 9%

commit v1 on v0

--- a/solution.py
+++ b/solution.py
@@ -16,7 +16,7 @@
 ROW = 128
 SPOT = 100
 TALLY = 101
-DEPTH = 256
+DEPTH = 1024
 VMEM_BYTES = 48 * 1024 * 1024
 
 
@@ -50,19 +50,14 @@
     lane = lax.broadcasted_iota(jnp.int32, (1, ROW), 1)
     empty = jnp.where(lane == SPOT, -1.0, 0.0)
     packed[...] = jnp.broadcast_to(empty, packed.shape)
-    groups = slots.shape[0]
-
-    def group(a, carry):
-        def move(b, carry):
-            r = a * ROW + b
-            spot = jnp.full((1, ROW), spots[r], jnp.int32).astype(jnp.float32)
-            row = rows[pl.ds(picks[r], 1), :]
-            packed[pl.ds(slots[a, b], 1), :] = jnp.where(lane == SPOT, spot, row)
-            return carry
-
-        return lax.fori_loop(0, ROW, move, carry, unroll=16)
-
-    lax.fori_loop(0, groups, group, 0)
+
+    def move(r, carry):
+        spot = jnp.full((1, ROW), spots[r], jnp.int32).astype(jnp.float32)
+        row = rows[pl.ds(picks[r], 1), :]
+        packed[pl.ds(slots[r], 1), :] = jnp.where(lane == SPOT, spot, row)
+        return carry
+
+    lax.fori_loop(0, slots.shape[0], move, 0, unroll=32)
 
 
 def add_rows(moved, sums, size_x):
@@ -70,7 +65,7 @@
     lane = lax.broadcasted_iota(jnp.int32, (16, 2 * ROW), 1)
     pick = jnp.where((lane == SPOT) | (lane == SPOT + ROW), 1.0, 0.0).astype(jnp.bfloat16)
     north = lax.broadcasted_iota(jnp.int32, (ROW, DEPTH), 0)
-    step = 8
+    step = 4
 
     def tile(t, carry):
         values = moved[pl.ds(pl.multiple_of(t * DEPTH, DEPTH), DEPTH), :]
@@ -139,21 +134,25 @@
         p = p_above
 
 
-def strip_kernel(parent, dest, picks, spots, packed, rows, slots_v, slots, *, size_x):
+def strip_kernel(parent, dest, picks, spots, packed, rows, slots_v, slots, sems, *, size_x):
     channels = parent.shape[0] // size_x
     slots_v[...] = slot_rows(dest[...])
-    pltpu.sync_copy(slots_v, slots)
+    copies = [
+        pltpu.make_async_copy(slots_v.at[a], slots.at[pl.ds(a * ROW, ROW)], sems.at[a])
+        for a in range(slots_v.shape[0])
+    ]
+    for copy in copies:
+        copy.start()
     to_rows(parent, rows, channels, size_x)
+    for copy in copies:
+        copy.wait()
     pack_rows(rows, picks, spots, slots, packed)
 
 
 def nest_kernel(
-    moved, nest, metric, dest, buoyancy, picks, spots, out, packed, sums, rows, slots_v, slots,
-    *, size_x
+    moved, nest, metric, buoyancy, picks, spots, slots, out, packed, sums, rows, *, size_x
 ):
     channels = nest.shape[0] // size_x
-    slots_v[...] = slot_rows(dest[...])
-    pltpu.sync_copy(slots_v, slots)
     add_rows(moved, sums, size_x)
     relax(nest, sums, out, channels, size_x)
 
@@ -166,33 +165,58 @@
     pack_rows(rows, picks, spots, slots, packed)
 
 
-def parent_kernel(edge, buoyancy, parent, rim, side, metric, out, state, scaled):
-    channels, size_x = side.shape[0] - 1, metric.shape[0]
+def rim_kernel(parent, metric, after, before, dest, first, last, slots):
+    channels, size_x = parent.shape[:2]
+    slots[...] = slot_rows(dest[...])
+    tall = size_x + 2 * WIDTH
+    per = ROW // WIDTH
+    lane = lax.broadcasted_iota(jnp.int32, (tall, ROW), 1) // WIDTH
+    for q in range(pl.cdiv(channels + 1, per)):
+        ahead = jnp.zeros((tall, ROW), jnp.float32)
+        behind = ahead
+        for m in range(min(per, channels + 1 - q * per)):
+            c = q * per + m
+            own = parent[c] if c < channels else metric[...]
+            block = jnp.concatenate([own, jnp.concatenate([after[c], before[c]], 0)], 0)
+            ahead = jnp.where(lane == m, pltpu.roll(block, m * WIDTH, 1), ahead)
+            behind = jnp.where(lane == m, pltpu.roll(block, (m + 1) * WIDTH % ROW, 1), behind)
+        first[q * tall : (q + 1) * tall, :] = ahead
+        last[q * tall : (q + 1) * tall, :] = behind
+
+
+def parent_kernel(
+    edge, buoyancy, parent, metric, after_x, before_x, after_y, before_y, out, state, scaled
+):
+    channels, size_x = parent.shape[:2]
     levels = channels // 5
-    tall = side.shape[1]
+    tall = size_x + 2 * WIDTH
+    per = ROW // WIDTH
     shape = (tall, 2 * ROW)
-    scaled[:size_x, :ROW] = COURANT * metric[...]
-    scaled[size_x:, :ROW] = COURANT * rim[channels]
-    scaled[:, ROW:] = COURANT * side[channels]
-
-    def fill(c, carry):
-        state[c, :size_x, :ROW] = parent[c]
-        state[c, size_x:, :ROW] = rim[c]
-        state[c, :, ROW:] = side[c]
-        return carry
-
-    lax.fori_loop(0, channels, fill, 0)
+    group = lax.broadcasted_iota(jnp.int32, (tall, ROW), 1) // WIDTH
+
+    def extended(c, own):
+        rows = slice(c // per * tall, (c // per + 1) * tall)
+        m = c % per
+        ahead = pltpu.roll(after_y[rows, :], -m * WIDTH % ROW, 1)
+        behind = pltpu.roll(before_y[rows, :], (per - 1 - m) * WIDTH, 1)
+        side = jnp.where(group == 0, ahead, jnp.where(group == per - 1, behind, 0.0))
+        middle = jnp.concatenate([own, jnp.concatenate([after_x[c], before_x[c]], 0)], 0)
+        return jnp.concatenate([middle, side], 1)
+
+    for c in range(channels):
+        state[c] = extended(c, parent[c])
+    scaled[...] = COURANT * extended(channels, metric[...])
     row = lax.broadcasted_iota(jnp.int32, shape, 0)
     lane = lax.broadcasted_iota(jnp.int32, shape, 1)
     u_keep = jnp.where((row >= tall - WIDTH) & (edge[0] == 1), 0.0, 1.0)
     v_keep = jnp.where((lane >= 2 * ROW - WIDTH) & (edge[1] == 1), 0.0, 1.0)
 
     def step(_, carry):
-        def level(k, w_below):
+        w_below = jnp.zeros(shape, jnp.float32)
+        p = state[4 * levels]
+        for k in range(levels):
             n = COURANT * buoyancy[k]
-            p = state[4 * levels + k]
-            above = state[4 * levels + jnp.minimum(k + 1, levels - 1)]
-            p_above = above * jnp.where(k + 1 < levels, 1.0, 0.0)
+            p_above = state[4 * levels + k + 1] if k + 1 < levels else jnp.zeros(shape, jnp.float32)
             u = state[k] - COURANT * (pltpu.roll(p, tall - 1, 0) - p)
             v = state[levels + k] - COURANT * (pltpu.roll(p, 2 * ROW - 1, 1) - p)
             theta = state[3 * levels + k]
@@ -203,18 +227,13 @@
             state[2 * levels + k] = w
             state[3 * levels + k] = theta - n * w
             state[4 * levels + k] = p - scaled[...] * spread
-            return w
-
-        lax.fori_loop(0, levels, level, jnp.zeros(shape, jnp.float32))
+            w_below = w
+            p = p_above
         return carry
 
     lax.fori_loop(0, NSP, step, 0)
-
-    def drain(c, carry):
+    for c in range(channels):
         out[c] = state[c, :size_x, :ROW]
-        return carry
-
-    lax.fori_loop(0, channels, drain, 0)
 
 
 def final_kernel(moved, parent, out, sums, *, size_x):
@@ -249,20 +268,11 @@
     return lax.ppermute(first, axis, down), lax.ppermute(last, axis, up)
 
 
-def rims(parent, metric):
-    channels, size_x, size_y = parent.shape
+def gx_rims(parent, metric):
+    size_x = parent.shape[1]
     first = jnp.concatenate([parent[:, :WIDTH], metric[None, :WIDTH]], 0)
     last = jnp.concatenate([parent[:, size_x - WIDTH :], metric[None, size_x - WIDTH :]], 0)
-    after, before = shifted(first, last, "gx")
-    rim = jnp.concatenate([after, before], 1)
-
-    def strip(lanes):
-        own = jnp.concatenate([parent[:, :, lanes], metric[None, :, lanes]], 0)
-        return jnp.concatenate([own, rim[:, :, lanes]], 1)
-
-    after, before = shifted(strip(slice(0, WIDTH)), strip(slice(size_y - WIDTH, size_y)), "gy")
-    gap = jnp.zeros(after.shape[:2] + (ROW - 2 * WIDTH,), jnp.float32)
-    return rim, jnp.concatenate([after, gap, before], 2)
+    return shifted(first, last, "gx")
 
 
 def on_device(
@@ -284,36 +294,56 @@
     block_x, block_y = nest.shape[2:]
     slots = strip_col.shape[0]
     packed_type = jax.ShapeDtypeStruct((devices * CAP, ROW), jnp.float32)
-    index_scratch = [
-        pltpu.VMEM((slots // ROW, ROW), jnp.int32),
-        pltpu.SMEM((slots // ROW, ROW), jnp.int32),
-    ]
+    groups = slots // ROW
 
     packed = pl.pallas_call(
         functools.partial(strip_kernel, size_x=tile_x),
         out_shape=packed_type,
         in_specs=[vmem(), vmem(), smem(), smem()],
         out_specs=vmem(),
-        scratch_shapes=[pltpu.VMEM((tile_x * tile_y, ROW), jnp.float32)] + index_scratch,
+        scratch_shapes=[
+            pltpu.VMEM((tile_x * tile_y, ROW), jnp.float32),
+            pltpu.VMEM((groups, ROW), jnp.int32),
+            pltpu.SMEM((slots,), jnp.int32),
+            pltpu.SemaphoreType.DMA((groups,)),
+        ],
         compiler_params=params(),
         name="pack_strips",
     )(
         parent.reshape(channels * tile_x, tile_y),
-        strip_dest.reshape(slots // ROW, ROW),
+        strip_dest.reshape(groups, ROW),
         strip_col,
         strip_pos,
     )
 
-    packed, late_parent, late_metric = lax.optimization_barrier((packed, parent, metric))
+    packed, late_parent, late_metric, late_dest = lax.optimization_barrier(
+        (packed, parent, metric, panel_dest)
+    )
     moved = exchange(packed, devices)
     late_parent = late_parent.reshape(channels, tile_x, tile_y)
-    rim, side = rims(late_parent, late_metric)
+    after_x, before_x = gx_rims(late_parent, late_metric)
+    strip_type = jax.ShapeDtypeStruct(
+        (pl.cdiv(channels + 1, ROW // WIDTH) * (tile_x + 2 * WIDTH), ROW), jnp.float32
+    )
+    first, last, panel_slots = pl.pallas_call(
+        rim_kernel,
+        out_shape=(strip_type, strip_type, jax.ShapeDtypeStruct((groups, ROW), jnp.int32)),
+        in_specs=[vmem()] * 5,
+        out_specs=(vmem(),) * 3,
+        compiler_params=params(),
+        cost_estimate=pl.CostEstimate(flops=3_000_000, bytes_accessed=2_000_000, transcendentals=0),
+        name="pack_rims",
+    )(late_parent, late_metric, after_x, before_x, late_dest.reshape(groups, ROW))
+    after_y, before_y = shifted(first, last, "gy")
+    moved, after_x, before_x, after_y, before_y, panel_slots = lax.optimization_barrier(
+        (moved, after_x, before_x, after_y, before_y, panel_slots)
+    )
     edge = jnp.stack([lax.axis_index("gx") == 0, lax.axis_index("gy") == 0]).astype(jnp.int32)
     tall = tile_x + 2 * WIDTH
     parent_state = pl.pallas_call(
         parent_kernel,
         out_shape=jax.ShapeDtypeStruct((channels, tile_x, tile_y), jnp.float32),
-        in_specs=[smem(), smem(), vmem(), vmem(), vmem(), vmem()],
+        in_specs=[smem(), smem()] + [vmem()] * 6,
         out_specs=vmem(),
         scratch_shapes=[
             pltpu.VMEM((channels, tall, 2 * ROW), jnp.float32),
@@ -322,7 +352,7 @@
         compiler_params=params(),
         cost_estimate=pl.CostEstimate(flops=20_000_000, bytes_accessed=8_000_000, transcendentals=0),
         name="step_parent",
-    )(edge, buoyancy, late_parent, rim, side, late_metric)
+    )(edge, buoyancy, late_parent, late_metric, after_x, before_x, after_y, before_y)
 
     nest_out, packed = pl.pallas_call(
         functools.partial(nest_kernel, size_x=block_x),
@@ -330,23 +360,22 @@
             jax.ShapeDtypeStruct((channels * block_x, block_y), jnp.float32),
             packed_type,
         ),
-        in_specs=[vmem(), vmem(), vmem(), vmem(), smem(), smem(), smem()],
+        in_specs=[vmem(), vmem(), vmem(), smem(), smem(), smem(), smem()],
         out_specs=(vmem(), vmem()),
         scratch_shapes=[
             pltpu.VMEM((block_x * block_y, 2 * ROW), jnp.float32),
             pltpu.VMEM((block_x * block_y, ROW), jnp.float32),
-        ]
-        + index_scratch,
+        ],
         compiler_params=params(),
         name="step_nest",
     )(
         moved,
         nest.reshape(channels * block_x, block_y),
         nest_metric,
-        panel_dest.reshape(slots // ROW, ROW),
         buoyancy,
         panel_src,
         panel_col,
+        panel_slots.reshape(slots),
     )
     moved = exchange(packed, devices)
 

time: 163 us -> 133 us (0.82)
  the two profiles are of different devices: /device:TPU:13 before, /device:TPU:1 now
where the time goes in v1:
time: 133 us; the launch traced here: 132 us
  Pallas kernels  44.7 us (34%)
  waiting for transfers between devices  40.7 us (31%)
  starting transfers between devices  36.2 us (27%)
  local copies, waits for them, and re-layouts  9.61 us (7%)
    all_to_all x2, starting transfers between devices, exchange(): lax.all_to_all(packed.reshape(devices, CAP, ROW), ('gx', 'gy'), split_axi...  25.3 us
    ppermute x4, waiting for transfers between devices, shifted(): return (lax.ppermute(first, axis, down), lax.ppermute(last, axis, up))  21.7 us
    all_to_all x2, waiting for transfers between devices, exchange(): lax.all_to_all(packed.reshape(devices, CAP, ROW), ('gx', 'gy'), split_axi...  18.9 us
    pallas_call x1, Pallas kernels, on_device(): pl.pallas_call(functools.partial(final_kernel, size_x=tile_x), out_shape=...  15.7 us
    pallas_call x1, Pallas kernels, on_device(): pl.pallas_call(functools.partial(nest_kernel, size_x=block_x), out_shape=...  15.6 us
    ppermute x4, starting transfers between devices, shifted(): return (lax.ppermute(first, axis, down), lax.ppermute(last, axis, up))  11 us
    unnamed x40, local copies, waits for them, and re-layouts  9.53 us
    pallas_call x1, Pallas kernels, on_device(): pl.pallas_call(parent_kernel, out_shape=jax.ShapeDtypeStruct((channels, t...  7.55 us
  transfers between devices with their start and end apart: 6, of which 3 were waited for; matrix products, arithmetic and copies ran while one was open for 0% of the time, Pallas kernels for 7%

profile of v1, /device:TPU:1, one launch (start us, length us, event | category | flops | bytes accessed | tf_op | source)
XLA Modules:
  0.0 132.3 jit_solution(17162476518921119037)
XLA Ops:
  0.6 0.0 copy-start
  0.6 1.4 %copy-done = f32[5,20,32,128]{3,2,1,0:T(8,128)S(1)} copy-done((f32[5,20,32,128]{3,2,1,0:T(8,128)S(1)}, f32[5,20,32,128]{3,2,1,0:T(8,128)}, u32[]{:S(2)}) %copy-start) | copy-done | bytes 1638424
  2.1 0.7 copy-done.16
  2.8 0.7 copy-done.17
  3.4 0.7 copy-done.18
  4.1 4.4 %pack_strips.1 = f32[4096,128]{1,0:T(8,128)S(1)} custom-call(f32[3200,128]{1,0:T(8,128)S(1)} %bitcast.19, s32[8,128]{1,0:T(8,128)S(1)} %bitcast.29, s32[1024]{0:T(1024)S(1)} %copy-done.17, s32[1024]{0:T(1024)S(1)} %copy-done.18), custom_call_target="tpu_custom_call" | custom-call | tf_op jit(solution)/shard_map/pack_strips/pallas_call | solution.py:299
  8.5 1.3 copy-done.2
  9.8 12.0 %all-to-all-start = ((f32[128,32,128]{2,1,0:T(8,128)}), f32[128,32,128]{2,1,0:T(8,128)}, u32[]{:S(2)}, u32[]{:S(2)}) async-start(f32[128,32,128]{2,1,0:T(8,128)} %bitcast.23), calls=%async_computation | async-start | bytes 4194304 | tf_op jit(solution)/shard_map/all_to_all | solution.py:258
  21.8 0.0 copy-start.13
  21.8 0.1 fusion
  21.9 0.0 copy-start.4
  22.0 0.0 copy-start.15
  22.0 0.0 copy-start.19
  22.0 3.2 %collective-permute-start = (f32[101,4,128]{2,1,0:T(4,128)S(1)}, f32[101,4,128]{2,1,0:T(4,128)S(1)}, u32[]{:S(2)}, u32[]{:S(2)}) collective-permute-start(f32[101,4,128]{2,1,0:T(4,128)S(1)} %pad_maximum_fusion), channel_id=1, source_target_pairs={{16,0},{32,16},{48,32},{64,48},{80,64},{96,80},{112,96},{17,1},{33... | collective-permute-start | bytes 620552 | tf_op jit(solution)/shard_map/ppermute | solution.py:268
  25.3 2.5 %collective-permute-start.1 = (f32[101,4,128]{2,1,0:T(4,128)S(1)}, f32[101,4,128]{2,1,0:T(4,128)S(1)}, u32[]{:S(2)}, u32[]{:S(2)}) collective-permute-start(f32[101,4,128]{2,1,0:T(4,128)S(1)} %pad_maximum_fusion.1), channel_id=1, source_target_pairs={{0,16},{16,32},{32,48},{48,64},{64,80},{80,96},{96,112},{1,17},{17... | collective-permute-start | bytes 620552 | tf_op jit(solution)/shard_map/ppermute | solution.py:268
  27.8 20.3 %collective-permute-done.after.after_x = f32[101,4,128]{2,1,0:T(4,128)S(1)} collective-permute-done((f32[101,4,128]{2,1,0:T(4,128)S(1)}, f32[101,4,128]{2,1,0:T(4,128)S(1)}, u32[]{:S(2)}, u32[]{:S(2)}) %collective-permute-start) | collective-permute-done | bytes 206880 | tf_op jit(solution)/shard_map/ppermute | solution.py:268
  48.1 1.4 %pack_rims.1 = (f32[160,128]{1,0:T(8,128)S(1)}, f32[160,128]{1,0:T(8,128)S(1)}, s32[8,128]{1,0:T(8,128)S(1)}) custom-call(f32[100,32,128]{2,1,0:T(8,128)S(1)} %bitcast.21, f32[32,128]{1,0:T(8,128)S(1)} %copy-done.7, f32[101,4,128]{2,1,0:T(4,128)S(1)} %collective-permute-done.after.after_x, f32[101,4,128]{2,1,0:T(4,128)S(1)} %collective-permute-done.1.before.before_x, ...), custom_call_target="tpu_custom_call" | custom-call | flops 3000000 | bytes 2000000 | tf_op jit(solution)/shard_map/pack_rims/pallas_call | solution.py:328
  49.5 0.0 copy-start.5
  49.5 0.7 copy-done.5
  50.2 1.3 collective-permute-start.2
  51.5 4.0 %collective-permute-start.3 = (f32[160,128]{1,0:T(8,128)S(1)}, f32[160,128]{1,0:T(8,128)S(1)}, u32[]{:S(2)}, u32[]{:S(2)}) collective-permute-start(f32[160,128]{1,0:T(8,128)S(1)} %get-tuple-element.22), channel_id=1, source_target_pairs={{0,1},{1,2},{2,3},{3,4},{4,5},{5,6},{6,7},{7,8},{8,9},{9,10},{10,1... | collective-permute-start | bytes 245768 | tf_op jit(solution)/shard_map/ppermute | solution.py:268
  55.5 1.4 %collective-permute-done.3.before_y = f32[160,128]{1,0:T(8,128)S(1)} collective-permute-done((f32[160,128]{1,0:T(8,128)S(1)}, f32[160,128]{1,0:T(8,128)S(1)}, u32[]{:S(2)}, u32[]{:S(2)}) %collective-permute-start.3) | collective-permute-done | bytes 81952 | tf_op jit(solution)/shard_map/ppermute | solution.py:268
  57.0 15.6 %step_nest.1 = (f32[2400,128]{1,0:T(8,128)}, f32[4096,128]{1,0:T(8,128)S(1)}) custom-call(f32[4096,128]{1,0:T(8,128)} %bitcast.3.moved, f32[2400,128]{1,0:T(8,128)S(1)} %bitcast.26, f32[24,128]{1,0:T(8,128)S(1)} %copy-done.12, f32[20]{0:T(128)S(1)} %copy-done.19, s32[1024]{0:T(1024)S(1)} %copy-done.14, s32[1024]{0:T(1024)S(1)} %copy-done.15, s32[1024]{0:T(1024)S(1)} %bitcast.28), custom_call_target="tpu_custom_call" | custom-call | tf_op jit(solution)/shard_map/step_nest/pallas_call | solution.py:357
  72.6 1.3 copy-done.3
  74.0 13.3 %all-to-all-start.1 = ((f32[128,32,128]{2,1,0:T(8,128)}), f32[128,32,128]{2,1,0:T(8,128)}, u32[]{:S(2)}, u32[]{:S(2)}) async-start(f32[128,32,128]{2,1,0:T(8,128)} %bitcast.25), calls=%async_computation.1 | async-start | bytes 4194304 | tf_op jit(solution)/shard_map/all_to_all | solution.py:258
  87.3 0.1 add_convert_fusion.edge
  87.3 0.9 copy-done.6
  88.3 0.9 copy-done.9
  89.2 0.9 copy-done.11
  90.0 7.5 %step_parent.1 = f32[100,32,128]{2,1,0:T(8,128)S(1)} custom-call(s32[2]{0:T(128)S(1)} %add_convert_fusion.edge, f32[20]{0:T(128)S(1)} %copy-done.19, f32[100,32,128]{2,1,0:T(8,128)S(1)} %bitcast.22, f32[32,128]{1,0:T(8,128)S(1)} %copy-done.7, f32[101,4,128]{2,1,0:T(4,128)S(1)} %collective-permute-done.after.after_x, f32[101,4,128]{2,1,0:T(4,128)S(1)} %copy-done.6, ...), custom_call_target="tpu_custom_call" | custom-call | flops 20000000 | bytes 8000000 | tf_op jit(solution)/shard_map/step_parent/pallas_call | solution.py:343
  97.6 18.9 %all-to-all-done.1 = f32[128,32,128]{2,1,0:T(8,128)} async-done(((f32[128,32,128]{2,1,0:T(8,128)}), f32[128,32,128]{2,1,0:T(8,128)}, u32[]{:S(2)}, u32[]{:S(2)}) %all-to-all-start.1) | async-done | bytes 2097184 | tf_op jit(solution)/shard_map/all_to_all | solution.py:258
  116.5 15.7 %add_panels.1 = f32[3200,128]{1,0:T(8,128)} custom-call(f32[4096,128]{1,0:T(8,128)} %bitcast.11.moved, f32[3200,128]{1,0:T(8,128)S(1)} %bitcast.24), custom_call_target="tpu_custom_call" | custom-call | tf_op jit(solution)/shard_map/add_panels/pallas_call | solution.py:382
  (30 shorter events, 0.2 us)
Async XLA Ops:
  0.6 1.4 %copy-start = (f32[5,20,32,128]{3,2,1,0:T(8,128)S(1)}, f32[5,20,32,128]{3,2,1,0:T(8,128)}, u32[]{:S(2)}) copy-start(f32[5,20,32,128]{3,2,1,0:T(8,128)} %param.11) | copy-start | bytes 4915204
  2.1 0.7 copy-start.16
  2.8 0.7 copy-start.17
  3.4 0.7 copy-start.18
  8.5 1.3 copy-start.2
  9.8 12.0 %copy-start.7 = (f32[32,128]{1,0:T(8,128)S(1)}, f32[32,128]{1,0:T(8,128)}, u32[]{:S(2)}) copy-start(f32[32,128]{1,0:T(8,128)} %metric.3) | copy-start | bytes 49156
  9.8 12.0 %copy-start.1 = (f32[5,20,32,128]{3,2,1,0:T(8,128)S(1)}, f32[5,20,32,128]{3,2,1,0:T(8,128)}, u32[]{:S(2)}) copy-start(f32[5,20,32,128]{3,2,1,0:T(8,128)} %param.11) | copy-start | bytes 4915204
  9.8 47.1 %all-to-all-start = ((f32[128,32,128]{2,1,0:T(8,128)}), f32[128,32,128]{2,1,0:T(8,128)}, u32[]{:S(2)}, u32[]{:S(2)}) async-start(f32[128,32,128]{2,1,0:T(8,128)} %bitcast.23), calls=%async_computation | async-start | bytes 4194304 | tf_op jit(solution)/shard_map/all_to_all | solution.py:258
  21.8 26.3 %copy-start.13 = (s32[1024,1]{0,1:T(1,128)S(1)}, s32[1024,1]{0,1:T(1,128)}, u32[]{:S(2)}) copy-start(s32[1024,1]{0,1:T(1,128)} %param.20) | copy-start | bytes 12292
  21.9 35.0 %copy-start.4 = (f32[5,20,24,128]{3,2,1,0:T(8,128)S(1)}, f32[5,20,24,128]{3,2,1,0:T(8,128)}, u32[]{:S(2)}) copy-start(f32[5,20,24,128]{3,2,1,0:T(8,128)} %param.14) | copy-start | bytes 3686404
  21.9 35.0 %copy-start.12 = (f32[24,128]{1,0:T(8,128)S(1)}, f32[24,128]{1,0:T(8,128)}, u32[]{:S(2)}) copy-start(f32[24,128]{1,0:T(8,128)} %metric.2) | copy-start | bytes 36868
  21.9 35.0 %copy-start.14 = (s32[1024]{0:T(1024)S(1)}, s32[1024]{0:T(1024)}, u32[]{:S(2)}) copy-start(s32[1024]{0:T(1024)} %picks.3) | copy-start | bytes 12292
  22.0 35.0 %copy-start.15 = (s32[1024]{0:T(1024)S(1)}, s32[1024]{0:T(1024)}, u32[]{:S(2)}) copy-start(s32[1024]{0:T(1024)} %spots.3) | copy-start | bytes 12292
  22.0 35.0 %copy-start.19 = (f32[20]{0:T(128)S(1)}, f32[20]{0:T(128)}, u32[]{:S(2)}) copy-start(f32[20]{0:T(128)} %buoyancy.3) | copy-start | bytes 244
  22.0 26.1 %collective-permute-start = (f32[101,4,128]{2,1,0:T(4,128)S(1)}, f32[101,4,128]{2,1,0:T(4,128)S(1)}, u32[]{:S(2)}, u32[]{:S(2)}) collective-permute-start(f32[101,4,128]{2,1,0:T(4,128)S(1)} %pad_maximum_fusion), channel_id=1, source_target_pairs={{16,0},{32,16},{48,32},{64,48},{80,64},{96,80},{112,96},{17,1},{33... | collective-permute-start | bytes 620552 | tf_op jit(solution)/shard_map/ppermute | solution.py:268
  25.3 22.8 %collective-permute-start.1 = (f32[101,4,128]{2,1,0:T(4,128)S(1)}, f32[101,4,128]{2,1,0:T(4,128)S(1)}, u32[]{:S(2)}, u32[]{:S(2)}) collective-permute-start(f32[101,4,128]{2,1,0:T(4,128)S(1)} %pad_maximum_fusion.1), channel_id=1, source_target_pairs={{0,16},{16,32},{32,48},{48,64},{64,80},{80,96},{96,112},{1,17},{17... | collective-permute-start | bytes 620552 | tf_op jit(solution)/shard_map/ppermute | solution.py:268
  49.5 0.7 copy-start.5
  50.2 5.3 %collective-permute-start.2 = (f32[160,128]{1,0:T(8,128)S(1)}, f32[160,128]{1,0:T(8,128)S(1)}, u32[]{:S(2)}, u32[]{:S(2)}) collective-permute-start(f32[160,128]{1,0:T(8,128)S(1)} %get-tuple-element.21), channel_id=1, source_target_pairs={{1,0},{2,1},{3,2},{4,3},{5,4},{6,5},{7,6},{8,7},{9,8},{10,9},{11,1... | collective-permute-start | bytes 245768 | tf_op jit(solution)/shard_map/ppermute | solution.py:268
  51.5 5.5 %collective-permute-start.3 = (f32[160,128]{1,0:T(8,128)S(1)}, f32[160,128]{1,0:T(8,128)S(1)}, u32[]{:S(2)}, u32[]{:S(2)}) collective-permute-start(f32[160,128]{1,0:T(8,128)S(1)} %get-tuple-element.22), channel_id=1, source_target_pairs={{0,1},{1,2},{2,3},{3,4},{4,5},{5,6},{6,7},{7,8},{8,9},{9,10},{10,1... | collective-permute-start | bytes 245768 | tf_op jit(solution)/shard_map/ppermute | solution.py:268
  55.5 17.1 %copy-start.8 = (f32[160,128]{1,0:T(8,128)}, f32[160,128]{1,0:T(8,128)S(1)}, u32[]{:S(2)}) copy-start(f32[160,128]{1,0:T(8,128)S(1)} %collective-permute-done.2.after_y) | copy-start | bytes 245764
  57.0 15.7 %copy-start.10 = (f32[160,128]{1,0:T(8,128)}, f32[160,128]{1,0:T(8,128)S(1)}, u32[]{:S(2)}) copy-start(f32[160,128]{1,0:T(8,128)S(1)} %collective-permute-done.3.before_y) | copy-start | bytes 245764
  72.6 1.3 copy-start.3
  74.0 42.6 %all-to-all-start.1 = ((f32[128,32,128]{2,1,0:T(8,128)}), f32[128,32,128]{2,1,0:T(8,128)}, u32[]{:S(2)}, u32[]{:S(2)}) async-start(f32[128,32,128]{2,1,0:T(8,128)} %bitcast.25), calls=%async_computation.1 | async-start | bytes 4194304 | tf_op jit(solution)/shard_map/all_to_all | solution.py:258
  87.3 0.9 copy-start.6
  88.3 0.9 copy-start.9
  89.2 0.9 copy-start.11

commit v2 on v1

v2 whole, which is shorter than its diff:
```python
import functools

import jax
import jax.numpy as jnp
from jax import lax
from jax.experimental import pallas as pl
from jax.experimental.pallas import tpu as pltpu
from jax.sharding import PartitionSpec as P

CAP = 32
NSP = 4
NSN = 6
COURANT = 0.35
WIDTH = NSP

ROW = 128
SPOT = 100
TALLY = 101
FREE = SPOT + 1
PIECE = ROW - FREE
PIECES = 4
KEEP = 26
REST = CAP - KEEP
GROUP = 8
STEP = 4
VMEM_BYTES = 60 * 1024 * 1024


def slot_rows(dest, spot, cells):
    groups = dest.shape[0]
    shape = (ROW, ROW)
    row = lax.broadcasted_iota(jnp.int32, dest.shape, 0)
    lane = lax.broadcasted_iota(jnp.int32, dest.shape, 1)
    high = spot >= cells // 2
    side = jnp.where(high, 1, 0)
    inward = jnp.where(high, cells - 1 - spot, spot)
    least = (dest * 2 + side) << 21
    key = least + (inward << 10) + (row * ROW + lane)
    counts = [jnp.zeros((8, ROW), jnp.float32) for _ in range(groups)]
    for a in range(groups):
        column = jnp.broadcast_to(key[a : a + 1], shape).T
        for b in range(groups):
            before = (column >= least[b : b + 1]) & (column < key[b : b + 1])
            ones = jnp.where(before, 1.0, 0.0)
            counts[b] = counts[b] + jnp.sum(ones.reshape(ROW // 8, 8, ROW), axis=0)
    rank = jnp.concatenate([jnp.sum(c, axis=0, keepdims=True) for c in counts], 0)
    rank = rank.astype(jnp.int32)
    slot = jnp.where(high, CAP - 1 - rank, rank)
    devices = ROW
    spill = devices * KEEP + (slot - KEEP) * devices + dest
    return jnp.where(slot < KEEP, dest * KEEP + slot, spill)


def to_rows(fields, rows, channels, size_x):
    tail = jnp.zeros((ROW - channels, ROW), jnp.float32)
    for i in range(size_x):
        block = fields[pl.ds(i, channels, stride=size_x), :]
        rows[i * ROW : (i + 1) * ROW, :] = jnp.concatenate([block, tail], 0).T


def clear_rows(staged):
    lane = lax.broadcasted_iota(jnp.int32, (1, ROW), 1)
    staged[...] = jnp.broadcast_to(jnp.where(lane == SPOT, -1.0, 0.0), staged.shape)


def pack_rows(rows, picks, spots, slots, staged, packed, sems):
    lane = lax.broadcasted_iota(jnp.int32, (1, ROW), 1)
    devices = packed.shape[0] // KEEP

    def move(r, carry):
        spot = jnp.full((1, ROW), spots[r], jnp.int32).astype(jnp.float32)
        row = rows[pl.ds(picks[r], 1), :]
        staged[pl.ds(slots[r], 1), :] = jnp.where(lane == SPOT, spot, row)
        return carry

    lax.fori_loop(0, slots.shape[0], move, 0, unroll=32)
    parts = sems.shape[0]
    count = devices // parts
    free = lax.broadcasted_iota(jnp.int32, (count, ROW), 1) >= FREE
    copies = []
    for part in range(parts):
        base = part * count
        for a in range(REST):
            start = devices * (KEEP + a) + base
            values = staged[start : start + count, :]
            for b in range(PIECES):
                where = pl.ds(base * KEEP + b * REST + a, count, stride=KEEP)
                piece = pltpu.roll(values, (FREE - b * PIECE) % ROW, 1)
                staged[where, :] = jnp.where(free, piece, staged[where, :])
        block = pl.ds(base * KEEP, count * KEEP)
        copies.append(pltpu.make_async_copy(staged.at[block], packed.at[block], sems.at[part]))
        copies[-1].start()
    return copies


def slot_values(moved, s):
    devices = moved.shape[0] // KEEP
    if s < KEEP:
        return moved[pl.ds(s, devices, stride=KEEP), :]
    lane = lax.broadcasted_iota(jnp.int32, (devices, ROW), 1)
    values = jnp.zeros((devices, ROW), jnp.float32)
    for b in range(PIECES):
        piece = moved[pl.ds(b * REST + s - KEEP, devices, stride=KEEP), :]
        piece = pltpu.roll(piece, (b * PIECE - FREE) % ROW, 1)
        values = jnp.where((lane >= b * PIECE) & (lane < (b + 1) * PIECE), piece, values)
    return values


def add_rows(moved, sums, size_x):
    lane = lax.broadcasted_iota(jnp.int32, (16, 2 * ROW), 1)
    pick = jnp.where((lane == SPOT) | (lane == SPOT + ROW), 1.0, 0.0).astype(jnp.bfloat16)
    depth = moved.shape[0] // KEEP * GROUP
    north = lax.broadcasted_iota(jnp.int32, (ROW, depth), 0)
    tally = lax.broadcasted_iota(jnp.int32, (depth, ROW), 1) == TALLY
    for t in range(CAP // GROUP):
        values = [slot_values(moved, t * GROUP + k) for k in range(GROUP)]
        values = jnp.where(tally, 1.0, jnp.concatenate(values, 0))
        high = values.astype(jnp.bfloat16)
        low = (values - high.astype(jnp.float32)).astype(jnp.bfloat16)
        both = jnp.concatenate([high, low], 1)
        spot = lax.dot_general(
            pick, both, (((1,), (1,)), ((), ())), preferred_element_type=jnp.float32
        )
        whole = spot.astype(jnp.int32)
        east, within = whole >> 7, whole & (ROW - 1)
        used = spot[0:8] >= 0.0
        reach = east[0:8].astype(jnp.float32)
        first = jnp.min(jnp.where(used, reach, float(size_x))).astype(jnp.int32)
        last = jnp.max(jnp.where(used, reach, -1.0)).astype(jnp.int32)
        blocks = jnp.maximum(last - first + STEP, 0) // STEP
        start = jnp.minimum(first, size_x - blocks * STEP)
        column = jnp.where(north == within[0:1], 1.0, 0.0).astype(jnp.bfloat16)
        column = column.reshape(ROW // 16, 16, depth)

        def block(g, carry, start=start, east=east, column=column, both=both):
            here = start + g * STEP
            parts = []
            for k in range(STEP):
                mine = jnp.where(east == here + k, 1.0, 0.0).astype(jnp.bfloat16)
                parts.append((column * mine[None]).reshape(ROW, depth))
            where = pl.ds(pl.multiple_of(here * ROW, ROW), STEP * ROW)
            sums[where, :] += jnp.dot(
                jnp.concatenate(parts, 0), both, preferred_element_type=jnp.float32
            )
            return carry

        lax.fori_loop(0, blocks, block, 0)


def relax(fields, sums, out, channels, size_x, i):
    block = slice(i * ROW, (i + 1) * ROW)
    total = (sums[block, :ROW] + sums[block, ROW:]).T
    share = 1.0 / (1.0 + total[TALLY : TALLY + 1])
    where = pl.ds(i, channels, stride=size_x)
    out[where, :] = (fields[where, :] + total[:channels]) * share


def nest_step(state, metric, buoyancy, levels, size_x):
    shape = (size_x, ROW)
    row = lax.broadcasted_iota(jnp.int32, shape, 0)
    lane = lax.broadcasted_iota(jnp.int32, shape, 1)
    scaled = COURANT * metric[...]

    def at(field, k):
        start = (field * levels + k) * size_x
        return slice(start, start + size_x)

    w_below = jnp.zeros(shape, jnp.float32)
    p = state[at(4, 0), :]
    for k in range(levels):
        n = COURANT * buoyancy[k]
        p_above = state[at(4, k + 1), :] if k + 1 < levels else jnp.zeros(shape, jnp.float32)
        p_east = jnp.where(row == size_x - 1, 0.0, pltpu.roll(p, size_x - 1, 0))
        p_north = jnp.where(lane == ROW - 1, 0.0, pltpu.roll(p, ROW - 1, 1))
        u = state[at(0, k), :] - COURANT * (p_east - p)
        v = state[at(1, k), :] - COURANT * (p_north - p)
        edge = -COURANT * p
        u_west = jnp.where(row == 0, edge, pltpu.roll(u, 1, 0))
        v_south = jnp.where(lane == 0, edge, pltpu.roll(v, 1, 1))
        theta = state[at(3, k), :]
        w = state[at(2, k), :] - COURANT * (p_above - p) + n * theta
        state[at(0, k), :] = u
        state[at(1, k), :] = v
        state[at(2, k), :] = w
        state[at(3, k), :] = theta - n * w
        state[at(4, k), :] = p - scaled * ((u - u_west) + (v - v_south) + (w - w_below))
        w_below = w
        p = p_above


def fetch(pairs, sems):
    copies = [pltpu.make_async_copy(a, b, sems.at[i]) for i, (a, b) in enumerate(pairs)]
    for copy in copies:
        copy.start()
    return copies


def strip_kernel(
    parent, dest, picks, spots, spot_rows, packed,
    tile, dest_v, picks_s, spots_s, spots_v, rows, staged, slots_v, slots, sems, slot_sems, out_sems,
    *, size_x, cells
):
    channels = parent.shape[0] // size_x
    copies = fetch(
        [(dest, dest_v), (spot_rows, spots_v), (parent, tile), (picks, picks_s), (spots, spots_s)],
        sems,
    )
    clear_rows(staged)
    copies[0].wait()
    copies[1].wait()
    slots_v[...] = slot_rows(dest_v[...], spots_v[...], cells)
    moves = fetch(
        [(slots_v.at[a], slots.at[pl.ds(a * ROW, ROW)]) for a in range(slots_v.shape[0])], slot_sems
    )
    copies[2].wait()
    to_rows(tile, rows, channels, size_x)
    for copy in copies[3:] + moves:
        copy.wait()
    for copy in pack_rows(rows, picks_s, spots_s, slots, staged, packed, out_sems):
        copy.wait()


def nest_kernel(
    moved, nest, metric, buoyancy, picks, spots, slots, out, packed,
    came, tile, state, sums, rows, staged, sems, out_sems,
    *, size_x
):
    channels = nest.shape[0] // size_x
    copies = fetch([(moved, came), (nest, tile)], sems)
    sums[...] = jnp.zeros(sums.shape, jnp.float32)
    clear_rows(staged)
    copies[0].wait()
    add_rows(came, sums, size_x)
    copies[1].wait()
    for i in range(size_x):
        relax(tile, sums, state, channels, size_x, i)

    def step(_, carry):
        nest_step(state, metric, buoyancy, channels // 5, size_x)
        return carry

    lax.fori_loop(0, NSN, step, 0)
    result = pltpu.make_async_copy(state, out, sems.at[2])
    result.start()
    to_rows(state, rows, channels, size_x)
    for copy in pack_rows(rows, picks, spots, slots, staged, packed, out_sems):
        copy.wait()
    result.wait()


def rim_kernel(parent, metric, dest, spots, first_x, last_x, first_y, last_y, slots):
    size_x = metric.shape[0]
    channels = parent.shape[0] // size_x
    slots[...] = slot_rows(dest[...], spots[...], size_x * ROW)
    for r in range(WIDTH):
        there = pl.ds(r, channels, stride=WIDTH)
        end = size_x - WIDTH + r
        first_x[there, :] = parent[pl.ds(r, channels, stride=size_x), :]
        last_x[there, :] = parent[pl.ds(end, channels, stride=size_x), :]
        own = channels * WIDTH + r
        first_x[own : own + 1, :] = metric[r : r + 1]
        last_x[own : own + 1, :] = metric[end : end + 1]

    def rows(c):
        return parent[c * size_x : (c + 1) * size_x, :] if c < channels else metric[...]

    gather_lanes(rows, channels + 1, size_x, first_y, last_y, size_x, 0)


def gather_lanes(rows, count, height, first, last, pitch, offset):
    per = ROW // WIDTH
    lane = lax.broadcasted_iota(jnp.int32, (height, ROW), 1) // WIDTH
    for q in range(pl.cdiv(count, per)):
        ahead = jnp.zeros((height, ROW), jnp.float32)
        behind = ahead
        for m in range(min(per, count - q * per)):
            own = rows(q * per + m)
            ahead = jnp.where(lane == m, pltpu.roll(own, m * WIDTH, 1), ahead)
            behind = jnp.where(lane == m, pltpu.roll(own, (m + 1) * WIDTH % ROW, 1), behind)
        where = slice(q * pitch + offset, q * pitch + offset + height)
        first[where, :] = ahead
        last[where, :] = behind


def corner_kernel(own_first, own_last, after, before, first, last):
    count = after.shape[0] // WIDTH
    quarters = pl.cdiv(count, ROW // WIDTH)
    size_x = own_first.shape[0] // quarters
    tall = size_x + 2 * WIDTH
    for q in range(quarters):
        first[q * tall : q * tall + size_x, :] = own_first[q * size_x : (q + 1) * size_x, :]
        last[q * tall : q * tall + size_x, :] = own_last[q * size_x : (q + 1) * size_x, :]

    def rows(c):
        rim = slice(c * WIDTH, (c + 1) * WIDTH)
        return jnp.concatenate([after[rim, :], before[rim, :]], 0)

    gather_lanes(rows, count, 2 * WIDTH, first, last, tall, size_x)


def parent_kernel(
    edge, buoyancy, parent, metric, after_x, before_x, after_y, before_y, out, state, scaled
):
    size_x = metric.shape[0]
    channels = parent.shape[0] // size_x
    levels = channels // 5
    tall = size_x + 2 * WIDTH
    per = ROW // WIDTH
    shape = (tall, 2 * ROW)
    group = lax.broadcasted_iota(jnp.int32, (tall, ROW), 1) // WIDTH

    def extended(c, own):
        m = c % per
        rows = slice(c // per * tall, (c // per + 1) * tall)
        ahead = pltpu.roll(after_y[rows, :], -m * WIDTH % ROW, 1)
        behind = pltpu.roll(before_y[rows, :], (per - 1 - m) * WIDTH, 1)
        side = jnp.where(group == 0, ahead, jnp.where(group == per - 1, behind, 0.0))
        rim = slice(c * WIDTH, (c + 1) * WIDTH)
        beyond = jnp.concatenate([after_x[rim, :], before_x[rim, :]], 0)
        return jnp.concatenate([jnp.concatenate([own, beyond], 0), side], 1)

    for c in range(channels):
        state[c] = extended(c, parent[c * size_x : (c + 1) * size_x, :])
    scaled[...] = COURANT * extended(channels, metric[...])
    row = lax.broadcasted_iota(jnp.int32, shape, 0)
    lane = lax.broadcasted_iota(jnp.int32, shape, 1)
    u_keep = jnp.where((row >= tall - WIDTH) & (edge[0] == 1), 0.0, 1.0)
    v_keep = jnp.where((lane >= 2 * ROW - WIDTH) & (edge[1] == 1), 0.0, 1.0)

    def step(_, carry):
        w_below = jnp.zeros(shape, jnp.float32)
        p = state[4 * levels]
        for k in range(levels):
            n = COURANT * buoyancy[k]
            p_above = state[4 * levels + k + 1] if k + 1 < levels else jnp.zeros(shape, jnp.float32)
            u = state[k] - COURANT * (pltpu.roll(p, tall - 1, 0) - p)
            v = state[levels + k] - COURANT * (pltpu.roll(p, 2 * ROW - 1, 1) - p)
            theta = state[3 * levels + k]
            w = state[2 * levels + k] - COURANT * (p_above - p) + n * theta
            spread = (u - pltpu.roll(u, 1, 0)) + (v - pltpu.roll(v, 1, 1)) + (w - w_below)
            state[k] = u * u_keep
            state[levels + k] = v * v_keep
            state[2 * levels + k] = w
            state[3 * levels + k] = theta - n * w
            state[4 * levels + k] = p - scaled[...] * spread
            w_below = w
            p = p_above
        return carry

    lax.fori_loop(0, NSP, step, 0)
    for c in range(channels):
        out[c * size_x : (c + 1) * size_x, :] = state[c, :size_x, :ROW]


def final_kernel(moved, parent, out, came, tile, sums, sems, *, size_x):
    channels = parent.shape[0] // size_x
    copies = fetch([(moved, came), (parent, tile)], sems)
    sums[...] = jnp.zeros(sums.shape, jnp.float32)
    copies[0].wait()
    add_rows(came, sums, size_x)
    copies[1].wait()
    for i in range(size_x):
        relax(tile, sums, tile, channels, size_x, i)
    result = pltpu.make_async_copy(tile, out, sems.at[2])
    result.start()
    result.wait()


def vmem():
    return pl.BlockSpec(memory_space=pltpu.VMEM)


def smem():
    return pl.BlockSpec(memory_space=pltpu.SMEM)


def anywhere():
    return pl.BlockSpec(memory_space=pltpu.HBM)


def params():
    return pltpu.CompilerParams(vmem_limit_bytes=VMEM_BYTES)


def exchange(packed, devices):
    moved = lax.all_to_all(
        packed.reshape(devices, KEEP * ROW), ("gx", "gy"), split_axis=0, concat_axis=0, tiled=True
    )
    return moved.reshape(devices * KEEP, ROW)


def shifted(first, last, axis):
    size = lax.axis_size(axis)
    up = [(i, i + 1) for i in range(size - 1)]
    down = [(j, i) for i, j in up]
    return lax.ppermute(first, axis, down), lax.ppermute(last, axis, up)


def on_device(
    parent,
    metric,
    buoyancy,
    nest,
    nest_metric,
    strip_col,
    strip_dest,
    strip_pos,
    panel_src,
    panel_dest,
    panel_col,
):
    devices = lax.axis_size("gx") * lax.axis_size("gy")
    channels = parent.shape[0] * parent.shape[1]
    tile_x, tile_y = parent.shape[2:]
    block_x, block_y = nest.shape[2:]
    slots = strip_col.shape[0]
    groups = slots // ROW
    tile_shape = (channels * tile_x, tile_y)
    block_shape = (channels * block_x, block_y)
    packed_shape = (devices * KEEP, ROW)
    parts = 4

    def shape(*dims, dtype=jnp.float32):
        return jax.ShapeDtypeStruct(dims, dtype)

    def index(memory):
        return memory((slots,), jnp.int32)

    listed = pltpu.VMEM((groups, ROW), jnp.int32)
    packed = pl.pallas_call(
        functools.partial(strip_kernel, size_x=tile_x, cells=block_x * block_y),
        out_shape=shape(*packed_shape),
        in_specs=[anywhere()] * 5,
        out_specs=anywhere(),
        scratch_shapes=[
            pltpu.VMEM(tile_shape, jnp.float32),
            listed,
            index(pltpu.SMEM),
            index(pltpu.SMEM),
            listed,
            pltpu.VMEM((tile_x * tile_y, ROW), jnp.float32),
            pltpu.VMEM((devices * CAP, ROW), jnp.float32),
            listed,
            index(pltpu.SMEM),
            pltpu.SemaphoreType.DMA((5,)),
            pltpu.SemaphoreType.DMA((groups,)),
            pltpu.SemaphoreType.DMA((parts,)),
        ],
        compiler_params=params(),
        name="pack_strips",
    )(
        parent.reshape(tile_shape),
        strip_dest.reshape(groups, ROW),
        strip_col,
        strip_pos,
        strip_pos.reshape(groups, ROW),
    )

    packed, late_parent, late_metric, late_dest, late_col = lax.optimization_barrier(
        (packed, parent.reshape(tile_shape), metric, panel_dest, panel_col)
    )
    moved = exchange(packed, devices)
    rim_x = shape((channels + 1) * WIDTH, ROW)
    quarters = pl.cdiv(channels + 1, ROW // WIDTH)
    rim_y = shape(quarters * tile_x, ROW)
    first_x, last_x, own_first, own_last, panel_slots = pl.pallas_call(
        rim_kernel,
        out_shape=(rim_x, rim_x, rim_y, rim_y, shape(groups, ROW, dtype=jnp.int32)),
        in_specs=[vmem()] * 4,
        out_specs=(vmem(),) * 5,
        compiler_params=params(),
        cost_estimate=pl.CostEstimate(flops=3_000_000, bytes_accessed=2_000_000, transcendentals=0),
        name="pack_rims",
    )(late_parent, late_metric, late_dest.reshape(groups, ROW), late_col.reshape(groups, ROW))
    after_x, before_x = shifted(first_x, last_x, "gx")
    moved, after_x, before_x, panel_slots = lax.optimization_barrier(
        (moved, after_x, before_x, panel_slots)
    )
    tall = tile_x + 2 * WIDTH
    tall_y = shape(quarters * tall, ROW)
    first_y, last_y = pl.pallas_call(
        corner_kernel,
        out_shape=(tall_y, tall_y),
        in_specs=[vmem()] * 4,
        out_specs=(vmem(),) * 2,
        compiler_params=params(),
        name="pack_corners",
    )(own_first, own_last, after_x, before_x)
    after_y, before_y = shifted(first_y, last_y, "gy")
    nest_out, packed = pl.pallas_call(
        functools.partial(nest_kernel, size_x=block_x),
        out_shape=(shape(*block_shape), shape(*packed_shape)),
        in_specs=[anywhere(), anywhere(), vmem()] + [smem()] * 4,
        out_specs=(anywhere(), anywhere()),
        scratch_shapes=[
            pltpu.VMEM(packed_shape, jnp.float32),
            pltpu.VMEM(block_shape, jnp.float32),
            pltpu.VMEM(block_shape, jnp.float32),
            pltpu.VMEM((block_x * block_y, 2 * ROW), jnp.float32),
            pltpu.VMEM((block_x * block_y, ROW), jnp.float32),
            pltpu.VMEM((devices * CAP, ROW), jnp.float32),
            pltpu.SemaphoreType.DMA((3,)),
            pltpu.SemaphoreType.DMA((parts,)),
        ],
        compiler_params=params(),
        name="step_nest",
    )(
        moved,
        nest.reshape(block_shape),
        nest_metric,
        buoyancy,
        panel_src,
        panel_col,
        panel_slots.reshape(slots),
    )
    packed, after_y, before_y = lax.optimization_barrier((packed, after_y, before_y))
    moved = exchange(packed, devices)
    edge = jnp.stack([lax.axis_index("gx") == 0, lax.axis_index("gy") == 0]).astype(jnp.int32)
    parent_state = pl.pallas_call(
        parent_kernel,
        out_shape=shape(*tile_shape),
        in_specs=[smem(), smem()] + [vmem()] * 6,
        out_specs=vmem(),
        scratch_shapes=[
            pltpu.VMEM((channels, tall, 2 * ROW), jnp.float32),
            pltpu.VMEM((tall, 2 * ROW), jnp.float32),
        ],
        compiler_params=params(),
        cost_estimate=pl.CostEstimate(flops=20_000_000, bytes_accessed=8_000_000, transcendentals=0),
        name="step_parent",
    )(edge, buoyancy, late_parent, late_metric, after_x, before_x, after_y, before_y)

    parent_out = pl.pallas_call(
        functools.partial(final_kernel, size_x=tile_x),
        out_shape=shape(*tile_shape),
        in_specs=[anywhere(), anywhere()],
        out_specs=anywhere(),
        scratch_shapes=[
            pltpu.VMEM(packed_shape, jnp.float32),
            pltpu.VMEM(tile_shape, jnp.float32),
            pltpu.VMEM((tile_x * tile_y, 2 * ROW), jnp.float32),
            pltpu.SemaphoreType.DMA((3,)),
        ],
        compiler_params=params(),
        name="add_panels",
    )(moved, parent_state)
    return (parent_out.reshape(parent.shape), nest_out.reshape(nest.shape))


def solution(mesh):
    placed = (
        P(None, None, "gx", "gy"),
        P("gx", "gy"),
        P(),
        P(None, None, "gx", "gy"),
        P("gx", "gy"),
        P(("gx", "gy")),
        P(("gx", "gy"), None),
        P(("gx", "gy")),
        P(("gx", "gy")),
        P(("gx", "gy"), None),
        P(("gx", "gy")),
    )
    return jax.shard_map(
        on_device,
        mesh=mesh,
        in_specs=placed,
        out_specs=(P(None, None, "gx", "gy"), P(None, None, "gx", "gy")),
        check_vma=False,
    )
```

time: 133 us -> 119 us (0.89)
  the two profiles are of different devices: /device:TPU:1 before, /device:TPU:10 now
where the time goes in v2:
time: 119 us; the launch traced here: 118 us
  Pallas kernels  51.5 us (43%)
  starting transfers between devices  32.4 us (27%)
  waiting for transfers between devices  30.8 us (26%)
  local copies, waits for them, and re-layouts  1.85 us (2%)
    all_to_all x2, starting transfers between devices, exchange(): lax.all_to_all(packed.reshape(devices, KEEP * ROW), ('gx', 'gy'), split_a...  22.2 us
    all_to_all x2, waiting for transfers between devices, exchange(): lax.all_to_all(packed.reshape(devices, KEEP * ROW), ('gx', 'gy'), split_a...  17.5 us
    pallas_call x1, Pallas kernels, on_device(): pl.pallas_call(functools.partial(final_kernel, size_x=tile_x), out_shape=...  15.8 us
    pallas_call x1, Pallas kernels, on_device(): pl.pallas_call(functools.partial(nest_kernel, size_x=block_x), out_shape=...  13.9 us
    ppermute x4, waiting for transfers between devices, shifted(): return (lax.ppermute(first, axis, down), lax.ppermute(last, axis, up))  13.4 us
    ppermute x4, starting transfers between devices, shifted(): return (lax.ppermute(first, axis, down), lax.ppermute(last, axis, up))  10.1 us
    pallas_call x1, Pallas kernels, on_device(): pl.pallas_call(parent_kernel, out_shape=shape(*tile_shape), in_specs=[sme...  9.77 us
    pallas_call x1, Pallas kernels, on_device(): pl.pallas_call(functools.partial(strip_kernel, size_x=tile_x, cells=block...  5.83 us
  transfers between devices with their start and end apart: 6, of which 4 were waited for; matrix products, arithmetic and copies ran while one was open for 0% of the time, Pallas kernels for 23%

profile of v2, /device:TPU:10, one launch (start us, length us, event | category | flops | bytes accessed | tf_op | source)
XLA Modules:
  0.0 118.1 jit_solution(7766746017584738100)
XLA Ops:
  0.6 5.8 %pack_strips.1 = f32[3328,128]{1,0:T(8,128)} custom-call(f32[3200,128]{1,0:T(8,128)} %bitcast.15, s32[8,128]{1,0:T(8,128)} %bitcast.26, s32[1024]{0:T(1024)} %picks.2, s32[1024]{0:T(1024)} %spots.2, s32[8,128]{1,0:T(8,128)} %bitcast.24), custom_call_target="tpu_custom_call" | custom-call | tf_op jit(solution)/shard_map/pack_strips/pallas_call | solution.py:430
  6.5 10.4 %all-to-all-start = ((f32[128,1,3328]{2,1,0:T(1,128)}), f32[128,1,3328]{2,1,0:T(1,128)S(1)}, u32[]{:S(2)}, u32[]{:S(2)}) async-start(f32[128,1,3328]{2,1,0:T(1,128)} %bitcast.19), calls=%async_computation | async-start | bytes 3407872 | tf_op jit(solution)/shard_map/all_to_all | solution.py:386
  16.9 3.5 %pack_rims.1 = (f32[404,128]{1,0:T(8,128)}, f32[404,128]{1,0:T(8,128)}, f32[128,128]{1,0:T(8,128)}, f32[128,128]{1,0:T(8,128)}, s32[8,128]{1,0:T(8,128)}) custom-call(f32[3200,128]{1,0:T(8,128)} %bitcast.16, f32[32,128]{1,0:T(8,128)} %metric.3, s32[8,128]{1,0:T(8,128)} %bitcast.27, s32[8,128]{1,0:T(8,128)} %bitcast.25), custom_call_target="tpu_custom_call" | custom-call | flops 3000000 | bytes 2000000 | tf_op jit(solution)/shard_map/pack_rims/pallas_call | solution.py:466
  20.4 2.2 %collective-permute-start = (f32[404,128]{1,0:T(8,128)}, f32[404,128]{1,0:T(8,128)S(1)}, u32[]{:S(2)}, u32[]{:S(2)}) collective-permute-start(f32[404,128]{1,0:T(8,128)} %get-tuple-element.28), channel_id=1, source_target_pairs={{16,0},{32,16},{48,32},{64,48},{80,64},{96,80},{112,96},{17,1},{33... | collective-permute-start | bytes 620552 | tf_op jit(solution)/shard_map/ppermute | solution.py:396
  22.6 2.1 %collective-permute-start.1 = (f32[404,128]{1,0:T(8,128)}, f32[404,128]{1,0:T(8,128)S(1)}, u32[]{:S(2)}, u32[]{:S(2)}) collective-permute-start(f32[404,128]{1,0:T(8,128)} %get-tuple-element.29), channel_id=1, source_target_pairs={{0,16},{16,32},{32,48},{48,64},{64,80},{80,96},{96,112},{1,17},{17... | collective-permute-start | bytes 620552 | tf_op jit(solution)/shard_map/ppermute | solution.py:396
  24.8 12.6 %collective-permute-done.after.after_x = f32[404,128]{1,0:T(8,128)S(1)} collective-permute-done((f32[404,128]{1,0:T(8,128)}, f32[404,128]{1,0:T(8,128)S(1)}, u32[]{:S(2)}, u32[]{:S(2)}) %collective-permute-start) | collective-permute-done | bytes 206880 | tf_op jit(solution)/shard_map/ppermute | solution.py:396
  37.4 0.0 copy-start.2
  37.4 0.8 collective-permute-done.1.before.before_x
  38.1 0.0 copy-start.3
  38.2 3.3 %all-to-all-done = f32[128,1,3328]{2,1,0:T(1,128)S(1)} async-done(((f32[128,1,3328]{2,1,0:T(1,128)}), f32[128,1,3328]{2,1,0:T(1,128)S(1)}, u32[]{:S(2)}, u32[]{:S(2)}) %all-to-all-start) | async-done | bytes 1703968 | tf_op jit(solution)/shard_map/all_to_all | solution.py:386
  41.4 0.0 copy-start
  41.4 0.0 copy-done.2
  41.4 0.0 copy-done.3
  41.5 2.7 %pack_corners.1 = (f32[160,128]{1,0:T(8,128)}, f32[160,128]{1,0:T(8,128)}) custom-call(f32[128,128]{1,0:T(8,128)} %get-tuple-element.34.own_first, f32[128,128]{1,0:T(8,128)} %get-tuple-element.35.own_last, f32[404,128]{1,0:T(8,128)} %copy-done.2, f32[404,128]{1,0:T(8,128)} %copy-done.3), custom_call_target="tpu_custom_call" | custom-call | tf_op jit(solution)/shard_map/pack_corners/pallas_call | solution.py:481
  44.1 3.6 %collective-permute-start.2 = (f32[160,128]{1,0:T(8,128)}, f32[160,128]{1,0:T(8,128)S(1)}, u32[]{:S(2)}, u32[]{:S(2)}) collective-permute-start(f32[160,128]{1,0:T(8,128)} %get-tuple-element.38), channel_id=1, source_target_pairs={{1,0},{2,1},{3,2},{4,3},{5,4},{6,5},{7,6},{8,7},{9,8},{10,9},{11,1... | collective-permute-start | bytes 245768 | tf_op jit(solution)/shard_map/ppermute | solution.py:396
  47.7 2.2 %collective-permute-start.3 = (f32[160,128]{1,0:T(8,128)}, f32[160,128]{1,0:T(8,128)S(1)}, u32[]{:S(2)}, u32[]{:S(2)}) collective-permute-start(f32[160,128]{1,0:T(8,128)} %get-tuple-element.39), channel_id=1, source_target_pairs={{0,1},{1,2},{2,3},{3,4},{4,5},{5,6},{6,7},{7,8},{8,9},{9,10},{10,1... | collective-permute-start | bytes 245768 | tf_op jit(solution)/shard_map/ppermute | solution.py:396
  50.0 0.0 copy-done
  50.0 13.9 %step_nest.1 = (f32[2400,128]{1,0:T(8,128)}, f32[3328,128]{1,0:T(8,128)}) custom-call(f32[3328,128]{1,0:T(8,128)} %bitcast.18, f32[2400,128]{1,0:T(8,128)} %bitcast.23, f32[24,128]{1,0:T(8,128)} %metric.2, f32[20]{0:T(128)} %buoyancy.3, s32[1024]{0:T(1024)} %picks.3, s32[1024]{0:T(1024)} %spots.3, s32[1024]{0:T(1024)} %bitcast.28), custom_call_target="tpu_custom_call" | custom-call | tf_op jit(solution)/shard_map/step_nest/pallas_call | solution.py:490
  63.9 0.0 collective-permute-done.2.after_y
  63.9 0.0 copy-start.4
  63.9 0.0 collective-permute-done.3.before_y
  63.9 0.0 copy-start.5
  63.9 0.6 copy-done.4
  64.5 0.0 copy-done.5
  64.6 11.8 %all-to-all-start.1 = ((f32[128,1,3328]{2,1,0:T(1,128)}), f32[128,1,3328]{2,1,0:T(1,128)S(1)}, u32[]{:S(2)}, u32[]{:S(2)}) async-start(f32[128,1,3328]{2,1,0:T(1,128)} %bitcast.21), calls=%async_computation.1 | async-start | bytes 3407872 | tf_op jit(solution)/shard_map/all_to_all | solution.py:386
  76.4 0.6 add_convert_fusion.edge
  77.0 9.8 %step_parent.1.parent = f32[3200,128]{1,0:T(8,128)} custom-call(s32[2]{0:T(128)} %add_convert_fusion.edge, f32[20]{0:T(128)} %buoyancy.3, f32[3200,128]{1,0:T(8,128)} %bitcast.17, f32[32,128]{1,0:T(8,128)} %metric.3, f32[404,128]{1,0:T(8,128)} %copy-done.2, f32[404,128]{1,0:T(8,128)} %copy-done.3, f32[160,128]{1,0:T(8,128)} %copy-done.4, f32[160,128]{1,0:T(8,128)} %copy-done.5), custom_call_target="tpu_custom_call" | custom-call | flops 20000000 | bytes 8000000 | tf_op jit(solution)/shard_map/step_parent/pallas_call | solution.py:519
  86.8 14.2 %all-to-all-done.1 = f32[128,1,3328]{2,1,0:T(1,128)S(1)} async-done(((f32[128,1,3328]{2,1,0:T(1,128)}), f32[128,1,3328]{2,1,0:T(1,128)S(1)}, u32[]{:S(2)}, u32[]{:S(2)}) %all-to-all-start.1) | async-done | bytes 1703968 | tf_op jit(solution)/shard_map/all_to_all | solution.py:386
  100.9 0.0 copy-start.1
  100.9 1.2 %copy-done.1 = f32[128,1,3328]{2,1,0:T(1,128)} copy-done((f32[128,1,3328]{2,1,0:T(1,128)}, f32[128,1,3328]{2,1,0:T(1,128)S(1)}, u32[]{:S(2)}) %copy-start.1) | copy-done | bytes 1703960
  102.1 15.8 %add_panels.1 = f32[3200,128]{1,0:T(8,128)} custom-call(f32[3328,128]{1,0:T(8,128)} %bitcast.20, f32[3200,128]{1,0:T(8,128)} %step_parent.1.parent), custom_call_target="tpu_custom_call" | custom-call | tf_op jit(solution)/shard_map/add_panels/pallas_call | solution.py:533
Async XLA Ops:
  6.5 35.0 %all-to-all-start = ((f32[128,1,3328]{2,1,0:T(1,128)}), f32[128,1,3328]{2,1,0:T(1,128)S(1)}, u32[]{:S(2)}, u32[]{:S(2)}) async-start(f32[128,1,3328]{2,1,0:T(1,128)} %bitcast.19), calls=%async_computation | async-start | bytes 3407872 | tf_op jit(solution)/shard_map/all_to_all | solution.py:386
  20.4 16.9 %collective-permute-start = (f32[404,128]{1,0:T(8,128)}, f32[404,128]{1,0:T(8,128)S(1)}, u32[]{:S(2)}, u32[]{:S(2)}) collective-permute-start(f32[404,128]{1,0:T(8,128)} %get-tuple-element.28), channel_id=1, source_target_pairs={{16,0},{32,16},{48,32},{64,48},{80,64},{96,80},{112,96},{17,1},{33... | collective-permute-start | bytes 620552 | tf_op jit(solution)/shard_map/ppermute | solution.py:396
  22.6 15.5 %collective-permute-start.1 = (f32[404,128]{1,0:T(8,128)}, f32[404,128]{1,0:T(8,128)S(1)}, u32[]{:S(2)}, u32[]{:S(2)}) collective-permute-start(f32[404,128]{1,0:T(8,128)} %get-tuple-element.29), channel_id=1, source_target_pairs={{0,16},{16,32},{32,48},{48,64},{64,80},{80,96},{96,112},{1,17},{17... | collective-permute-start | bytes 620552 | tf_op jit(solution)/shard_map/ppermute | solution.py:396
  37.4 4.1 %copy-start.2 = (f32[404,128]{1,0:T(8,128)}, f32[404,128]{1,0:T(8,128)S(1)}, u32[]{:S(2)}) copy-start(f32[404,128]{1,0:T(8,128)S(1)} %collective-permute-done.after.after_x) | copy-start | bytes 620548
  38.1 3.3 %copy-start.3 = (f32[404,128]{1,0:T(8,128)}, f32[404,128]{1,0:T(8,128)S(1)}, u32[]{:S(2)}) copy-start(f32[404,128]{1,0:T(8,128)S(1)} %collective-permute-done.1.before.before_x) | copy-start | bytes 620548
  41.4 8.5 %copy-start = (f32[128,1,3328]{2,1,0:T(1,128)}, f32[128,1,3328]{2,1,0:T(1,128)S(1)}, u32[]{:S(2)}) copy-start(f32[128,1,3328]{2,1,0:T(1,128)S(1)} %all-to-all-done) | copy-start | bytes 5111812
  44.1 19.8 %collective-permute-start.2 = (f32[160,128]{1,0:T(8,128)}, f32[160,128]{1,0:T(8,128)S(1)}, u32[]{:S(2)}, u32[]{:S(2)}) collective-permute-start(f32[160,128]{1,0:T(8,128)} %get-tuple-element.38), channel_id=1, source_target_pairs={{1,0},{2,1},{3,2},{4,3},{5,4},{6,5},{7,6},{8,7},{9,8},{10,9},{11,1... | collective-permute-start | bytes 245768 | tf_op jit(solution)/shard_map/ppermute | solution.py:396
  47.7 16.2 %collective-permute-start.3 = (f32[160,128]{1,0:T(8,128)}, f32[160,128]{1,0:T(8,128)S(1)}, u32[]{:S(2)}, u32[]{:S(2)}) collective-permute-start(f32[160,128]{1,0:T(8,128)} %get-tuple-element.39), channel_id=1, source_target_pairs={{0,1},{1,2},{2,3},{3,4},{4,5},{5,6},{6,7},{7,8},{8,9},{9,10},{10,1... | collective-permute-start | bytes 245768 | tf_op jit(solution)/shard_map/ppermute | solution.py:396
  63.9 0.6 copy-start.4
  63.9 0.7 copy-start.5
  64.6 36.4 %all-to-all-start.1 = ((f32[128,1,3328]{2,1,0:T(1,128)}), f32[128,1,3328]{2,1,0:T(1,128)S(1)}, u32[]{:S(2)}, u32[]{:S(2)}) async-start(f32[128,1,3328]{2,1,0:T(1,128)} %bitcast.21), calls=%async_computation.1 | async-start | bytes 3407872 | tf_op jit(solution)/shard_map/all_to_all | solution.py:386
  100.9 1.2 %copy-start.1 = (f32[128,1,3328]{2,1,0:T(1,128)}, f32[128,1,3328]{2,1,0:T(1,128)S(1)}, u32[]{:S(2)}) copy-start(f32[128,1,3328]{2,1,0:T(1,128)S(1)} %all-to-all-done.1) | copy-start | bytes 5111812

commit v3 on v2

--- a/solution.py
+++ b/solution.py
@@ -22,8 +22,8 @@
 KEEP = 26
 REST = CAP - KEEP
 GROUP = 8
-STEP = 4
-VMEM_BYTES = 60 * 1024 * 1024
+STEP = 2
+VMEM_BYTES = 65500 * 1024
 
 
 def slot_rows(dest, spot, cells):
@@ -106,45 +106,87 @@
     return values
 
 
-def add_rows(moved, sums, size_x):
+def prepare(moved, weights, columns, easts, size_x):
     lane = lax.broadcasted_iota(jnp.int32, (16, 2 * ROW), 1)
     pick = jnp.where((lane == SPOT) | (lane == SPOT + ROW), 1.0, 0.0).astype(jnp.bfloat16)
-    depth = moved.shape[0] // KEEP * GROUP
+    devices = moved.shape[0] // KEEP
+    depth = devices * GROUP
+    tiles = CAP // GROUP
     north = lax.broadcasted_iota(jnp.int32, (ROW, depth), 0)
-    tally = lax.broadcasted_iota(jnp.int32, (depth, ROW), 1) == TALLY
-    for t in range(CAP // GROUP):
-        values = [slot_values(moved, t * GROUP + k) for k in range(GROUP)]
-        values = jnp.where(tally, 1.0, jnp.concatenate(values, 0))
-        high = values.astype(jnp.bfloat16)
-        low = (values - high.astype(jnp.float32)).astype(jnp.bfloat16)
-        both = jnp.concatenate([high, low], 1)
+    tally = lax.broadcasted_iota(jnp.int32, (devices, ROW), 1) == TALLY
+    reaches = []
+    for t in range(tiles):
+        for k in range(GROUP):
+            values = jnp.where(tally, 1.0, slot_values(moved, t * GROUP + k))
+            high = values.astype(jnp.bfloat16)
+            low = (values - high.astype(jnp.float32)).astype(jnp.bfloat16)
+            where = slice(k * devices, (k + 1) * devices)
+            weights[t, where, :ROW] = high
+            weights[t, where, ROW:] = low
         spot = lax.dot_general(
-            pick, both, (((1,), (1,)), ((), ())), preferred_element_type=jnp.float32
+            pick, weights[t], (((1,), (1,)), ((), ())), preferred_element_type=jnp.float32
         )
         whole = spot.astype(jnp.int32)
         east, within = whole >> 7, whole & (ROW - 1)
+        easts[t] = east
+        columns[t] = jnp.where(north == within[0:1], 1.0, 0.0).astype(jnp.bfloat16)
         used = spot[0:8] >= 0.0
         reach = east[0:8].astype(jnp.float32)
-        first = jnp.min(jnp.where(used, reach, float(size_x))).astype(jnp.int32)
-        last = jnp.max(jnp.where(used, reach, -1.0)).astype(jnp.int32)
-        blocks = jnp.maximum(last - first + STEP, 0) // STEP
-        start = jnp.minimum(first, size_x - blocks * STEP)
-        column = jnp.where(north == within[0:1], 1.0, 0.0).astype(jnp.bfloat16)
-        column = column.reshape(ROW // 16, 16, depth)
-
-        def block(g, carry, start=start, east=east, column=column, both=both):
-            here = start + g * STEP
-            parts = []
-            for k in range(STEP):
-                mine = jnp.where(east == here + k, 1.0, 0.0).astype(jnp.bfloat16)
-                parts.append((column * mine[None]).reshape(ROW, depth))
-            where = pl.ds(pl.multiple_of(here * ROW, ROW), STEP * ROW)
-            sums[where, :] += jnp.dot(
-                jnp.concatenate(parts, 0), both, preferred_element_type=jnp.float32
-            )
-            return carry
-
-        lax.fori_loop(0, blocks, block, 0)
+        first = jnp.min(jnp.where(used, reach, float(size_x)))
+        last = jnp.max(jnp.where(used, reach, -1.0))
+        reaches.append((first.astype(jnp.int32), last.astype(jnp.int32)))
+    return reaches
+
+
+def add_rows(moved, sums, weights, columns, easts, size_x):
+    tiles, depth = easts.shape[0], easts.shape[2]
+    reaches = prepare(moved, weights, columns, easts, size_x)
+
+    def block(t, here):
+        column = columns[t].reshape(ROW // 16, 16, depth)
+        parts = []
+        for k in range(STEP):
+            mine = jnp.where(easts[t] == here + k, 1.0, 0.0).astype(jnp.bfloat16)
+            parts.append((column * mine[None]).reshape(ROW, depth))
+        where = pl.ds(pl.multiple_of(here * ROW, ROW), STEP * ROW)
+        sums[where, :] += jnp.dot(
+            jnp.concatenate(parts, 0), weights[t], preferred_element_type=jnp.float32
+        )
+
+    windows = []
+    for t in range(tiles):
+        share = 9 if t in (0, tiles - 1) else 12
+        windows.append(min(size_x, pl.cdiv(size_x * share, 16 * STEP) * STEP))
+    narrow = functools.reduce(
+        jnp.logical_and, [last - first < width for (first, last), width in zip(reaches, windows)]
+    )
+
+    @pl.when(narrow)
+    def _():
+        for t in range(tiles):
+            start = jnp.minimum(reaches[t][0], size_x - windows[t])
+            for g in range(windows[t] // STEP):
+                block(t, start + g * STEP)
+
+    @pl.when(jnp.logical_not(narrow))
+    def _():
+        for t in range(tiles):
+
+            def whole_tile(g, carry, t=t):
+                block(t, g * STEP)
+                return carry
+
+            lax.fori_loop(0, size_x // STEP, whole_tile, 0)
+
+
+def add_scratch(devices):
+    depth = devices * GROUP
+    tiles = CAP // GROUP
+    return [
+        pltpu.VMEM((tiles, depth, 2 * ROW), jnp.bfloat16),
+        pltpu.VMEM((tiles, ROW, depth), jnp.bfloat16),
+        pltpu.VMEM((tiles, 16, depth), jnp.int32),
+    ]
 
 
 def relax(fields, sums, out, channels, size_x, i):
@@ -195,6 +237,12 @@
     return copies
 
 
+def split(source, target, parts):
+    count = source.shape[0] // parts
+    blocks = [pl.ds(part * count, count) for part in range(parts)]
+    return [(source.at[block], target.at[block]) for block in blocks]
+
+
 def strip_kernel(
     parent, dest, picks, spots, spot_rows, packed,
     tile, dest_v, picks_s, spots_s, spots_v, rows, staged, slots_v, slots, sems, slot_sems, out_sems,
@@ -202,9 +250,9 @@
 ):
     channels = parent.shape[0] // size_x
     copies = fetch(
-        [(dest, dest_v), (spot_rows, spots_v), (parent, tile), (picks, picks_s), (spots, spots_s)],
-        sems,
-    )
+        [(dest, dest_v), (spot_rows, spots_v), (picks, picks_s), (spots, spots_s)], sems
+    )
+    arrivals = fetch(split(parent, tile, out_sems.shape[0]), out_sems)
     clear_rows(staged)
     copies[0].wait()
     copies[1].wait()
@@ -212,9 +260,10 @@
     moves = fetch(
         [(slots_v.at[a], slots.at[pl.ds(a * ROW, ROW)]) for a in range(slots_v.shape[0])], slot_sems
     )
-    copies[2].wait()
+    for copy in arrivals:
+        copy.wait()
     to_rows(tile, rows, channels, size_x)
-    for copy in copies[3:] + moves:
+    for copy in copies[2:] + moves:
         copy.wait()
     for copy in pack_rows(rows, picks_s, spots_s, slots, staged, packed, out_sems):
         copy.wait()
@@ -222,52 +271,84 @@
 
 def nest_kernel(
     moved, nest, metric, buoyancy, picks, spots, slots, out, packed,
-    came, tile, state, sums, rows, staged, sems, out_sems,
+    came, tile, metric_v, buoyancy_s, picks_s, spots_s, slots_s, state, sums, rows, staged,
+    weights, columns, easts, sems, out_sems,
     *, size_x
 ):
     channels = nest.shape[0] // size_x
-    copies = fetch([(moved, came), (nest, tile)], sems)
+    arrivals = fetch(split(moved, came, out_sems.shape[0]), out_sems)
+    copies = fetch(
+        [(nest, tile), (metric, metric_v), (buoyancy, buoyancy_s)]
+        + [(picks, picks_s), (spots, spots_s), (slots, slots_s)],
+        sems,
+    )
     sums[...] = jnp.zeros(sums.shape, jnp.float32)
     clear_rows(staged)
-    copies[0].wait()
-    add_rows(came, sums, size_x)
-    copies[1].wait()
+    for copy in arrivals:
+        copy.wait()
+    add_rows(came, sums, weights, columns, easts, size_x)
+    for copy in copies:
+        copy.wait()
     for i in range(size_x):
         relax(tile, sums, state, channels, size_x, i)
 
     def step(_, carry):
-        nest_step(state, metric, buoyancy, channels // 5, size_x)
+        nest_step(state, metric_v, buoyancy_s, channels // 5, size_x)
         return carry
 
     lax.fori_loop(0, NSN, step, 0)
-    result = pltpu.make_async_copy(state, out, sems.at[2])
+    result = pltpu.make_async_copy(state, out, sems.at[0])
     result.start()
     to_rows(state, rows, channels, size_x)
-    for copy in pack_rows(rows, picks, spots, slots, staged, packed, out_sems):
+    for copy in pack_rows(rows, picks_s, spots_s, slots_s, staged, packed, out_sems):
         copy.wait()
     result.wait()
 
 
-def rim_kernel(parent, metric, dest, spots, first_x, last_x, first_y, last_y, slots):
+def rim_kernel(odd, head, tail, metric, near, far):
+    channels, block = head.shape[:2]
+    head, tail = (ref.reshape(channels * block, ROW) for ref in (head, tail))
+    size_x = metric.shape[0]
+
+    def cut(first, last):
+        for r in range(WIDTH):
+            there = pl.ds(r, channels, stride=WIDTH)
+            end = block - WIDTH + r
+            first[there, :] = head[pl.ds(r, channels, stride=block), :]
+            last[there, :] = tail[pl.ds(end, channels, stride=block), :]
+            own, end = channels * WIDTH + r, size_x - WIDTH + r
+            first[own : own + 1, :] = metric[r : r + 1]
+            last[own : own + 1, :] = metric[end : end + 1]
+
+    @pl.when(odd[0] == 1)
+    def _():
+        cut(near, far)
+
+    @pl.when(odd[0] == 0)
+    def _():
+        cut(far, near)
+
+
+def rim_rows(odd, near, far, c):
+    rim = slice(c * WIDTH, (c + 1) * WIDTH)
+    ours, theirs = near[rim, :], far[rim, :]
+    even = odd[0] == 0
+    return jnp.concatenate([jnp.where(even, ours, theirs), jnp.where(even, theirs, ours)], 0)
+
+
+def strip_rim_kernel(odd, parent, metric, near, far, dest, spots, first, last, slots):
     size_x = metric.shape[0]
     channels = parent.shape[0] // size_x
     slots[...] = slot_rows(dest[...], spots[...], size_x * ROW)
-    for r in range(WIDTH):
-        there = pl.ds(r, channels, stride=WIDTH)
-        end = size_x - WIDTH + r
-        first_x[there, :] = parent[pl.ds(r, channels, stride=size_x), :]
-        last_x[there, :] = parent[pl.ds(end, channels, stride=size_x), :]
-        own = channels * WIDTH + r
-        first_x[own : own + 1, :] = metric[r : r + 1]
-        last_x[own : own + 1, :] = metric[end : end + 1]
 
     def rows(c):
-        return parent[c * size_x : (c + 1) * size_x, :] if c < channels else metric[...]
-
-    gather_lanes(rows, channels + 1, size_x, first_y, last_y, size_x, 0)
-
-
-def gather_lanes(rows, count, height, first, last, pitch, offset):
+        own = parent[c * size_x : (c + 1) * size_x, :] if c < channels else metric[...]
+        return jnp.concatenate([own, rim_rows(odd, near, far, c)], 0)
+
+    gather_lanes(rows, channels + 1, size_x + 2 * WIDTH, first, last)
+
+
+def gather_lanes(rows, count, height, first, last):
     per = ROW // WIDTH
     lane = lax.broadcasted_iota(jnp.int32, (height, ROW), 1) // WIDTH
     for q in range(pl.cdiv(count, per)):
@@ -277,29 +358,13 @@
             own = rows(q * per + m)
             ahead = jnp.where(lane == m, pltpu.roll(own, m * WIDTH, 1), ahead)
             behind = jnp.where(lane == m, pltpu.roll(own, (m + 1) * WIDTH % ROW, 1), behind)
-        where = slice(q * pitch + offset, q * pitch + offset + height)
+        where = slice(q * height, (q + 1) * height)
         first[where, :] = ahead
         last[where, :] = behind
 
 
-def corner_kernel(own_first, own_last, after, before, first, last):
-    count = after.shape[0] // WIDTH
-    quarters = pl.cdiv(count, ROW // WIDTH)
-    size_x = own_first.shape[0] // quarters
-    tall = size_x + 2 * WIDTH
-    for q in range(quarters):
-        first[q * tall : q * tall + size_x, :] = own_first[q * size_x : (q + 1) * size_x, :]
-        last[q * tall : q * tall + size_x, :] = own_last[q * size_x : (q + 1) * size_x, :]
-
-    def rows(c):
-        rim = slice(c * WIDTH, (c + 1) * WIDTH)
-        return jnp.concatenate([after[rim, :], before[rim, :]], 0)
-
-    gather_lanes(rows, count, 2 * WIDTH, first, last, tall, size_x)
-
-
 def parent_kernel(
-    edge, buoyancy, parent, metric, after_x, before_x, after_y, before_y, out, state, scaled
+    odd, edge, buoyancy, parent, metric, near, far, after_y, before_y, out, state, scaled
 ):
     size_x = metric.shape[0]
     channels = parent.shape[0] // size_x
@@ -315,9 +380,8 @@
         ahead = pltpu.roll(after_y[rows, :], -m * WIDTH % ROW, 1)
         behind = pltpu.roll(before_y[rows, :], (per - 1 - m) * WIDTH, 1)
         side = jnp.where(group == 0, ahead, jnp.where(group == per - 1, behind, 0.0))
-        rim = slice(c * WIDTH, (c + 1) * WIDTH)
-        beyond = jnp.concatenate([after_x[rim, :], before_x[rim, :]], 0)
-        return jnp.concatenate([jnp.concatenate([own, beyond], 0), side], 1)
+        middle = jnp.concatenate([own, rim_rows(odd, near, far, c)], 0)
+        return jnp.concatenate([middle, side], 1)
 
     for c in range(channels):
         state[c] = extended(c, parent[c * size_x : (c + 1) * size_x, :])
@@ -352,18 +416,29 @@
         out[c * size_x : (c + 1) * size_x, :] = state[c, :size_x, :ROW]
 
 
-def final_kernel(moved, parent, out, came, tile, sums, sems, *, size_x):
+def final_kernel(
+    moved, parent, out, came, tile, result, sums, weights, columns, easts, sems, out_sems, *, size_x
+):
     channels = parent.shape[0] // size_x
-    copies = fetch([(moved, came), (parent, tile)], sems)
+    arrivals = fetch(split(moved, came, out_sems.shape[0]), out_sems)
+    copies = fetch([(parent, tile)], sems)
     sums[...] = jnp.zeros(sums.shape, jnp.float32)
+    for copy in arrivals:
+        copy.wait()
+    add_rows(came, sums, weights, columns, easts, size_x)
     copies[0].wait()
-    add_rows(came, sums, size_x)
-    copies[1].wait()
-    for i in range(size_x):
-        relax(tile, sums, tile, channels, size_x, i)
-    result = pltpu.make_async_copy(tile, out, sems.at[2])
-    result.start()
-    result.wait()
+    flat = result.reshape(channels * size_x, ROW)
+    parts = out_sems.shape[0]
+    count = size_x // parts
+    copies = []
+    for part in range(parts):
+        for i in range(part * count, (part + 1) * count):
+            relax(tile, sums, flat, channels, size_x, i)
+        block = (slice(None), pl.ds(part * count, count))
+        copies.append(pltpu.make_async_copy(result.at[block], out.at[block], out_sems.at[part]))
+        copies[-1].start()
+    for copy in copies:
+        copy.wait()
 
 
 def vmem():
@@ -387,6 +462,13 @@
         packed.reshape(devices, KEEP * ROW), ("gx", "gy"), split_axis=0, concat_axis=0, tiled=True
     )
     return moved.reshape(devices * KEEP, ROW)
+
+
+def swapped(near, far, axis):
+    size = lax.axis_size(axis)
+    pairs = [[(i, i + 1) for i in range(start, size - 1, 2)] for start in (0, 1)]
+    pairs = [some + [(j, i) for i, j in some] for some in pairs]
+    return lax.ppermute(near, axis, pairs[0]), lax.ppermute(far, axis, pairs[1])
 
 
 def shifted(first, last, axis):
@@ -427,6 +509,24 @@
         return memory((slots,), jnp.int32)
 
     listed = pltpu.VMEM((groups, ROW), jnp.int32)
+    rim_x = shape((channels + 1) * WIDTH, ROW)
+    tile = parent.reshape(channels, tile_x, tile_y)
+    ends = [
+        pl.BlockSpec((channels, GROUP, ROW), lambda i, place=place: (0, place, 0))
+        for place in (0, tile_x // GROUP - 1)
+    ]
+    whole_rim = pl.BlockSpec(rim_x.shape, lambda i: (0, 0))
+    odd = (lax.axis_index("gx") % 2).astype(jnp.int32).reshape(1)
+    near, far = pl.pallas_call(
+        rim_kernel,
+        grid=(1,),
+        out_shape=(rim_x, rim_x),
+        in_specs=[smem()] + ends + [pl.BlockSpec(metric.shape, lambda i: (0, 0))],
+        out_specs=(whole_rim, whole_rim),
+        compiler_params=params(),
+        name="cut_rims",
+    )(odd, tile, tile, metric)
+    near, far = swapped(near, far, "gx")
     packed = pl.pallas_call(
         functools.partial(strip_kernel, size_x=tile_x, cells=block_x * block_y),
         out_shape=shape(*packed_shape),
@@ -442,7 +542,7 @@
             pltpu.VMEM((devices * CAP, ROW), jnp.float32),
             listed,
             index(pltpu.SMEM),
-            pltpu.SemaphoreType.DMA((5,)),
+            pltpu.SemaphoreType.DMA((4,)),
             pltpu.SemaphoreType.DMA((groups,)),
             pltpu.SemaphoreType.DMA((parts,)),
         ],
@@ -456,52 +556,55 @@
         strip_pos.reshape(groups, ROW),
     )
 
-    packed, late_parent, late_metric, late_dest, late_col = lax.optimization_barrier(
-        (packed, parent.reshape(tile_shape), metric, panel_dest, panel_col)
+    packed, near, far, late_parent, late_metric, late_dest, late_col = (
+        lax.optimization_barrier(
+            (packed, near, far, parent.reshape(tile_shape), metric, panel_dest, panel_col)
+        )
     )
     moved = exchange(packed, devices)
-    rim_x = shape((channels + 1) * WIDTH, ROW)
-    quarters = pl.cdiv(channels + 1, ROW // WIDTH)
-    rim_y = shape(quarters * tile_x, ROW)
-    first_x, last_x, own_first, own_last, panel_slots = pl.pallas_call(
-        rim_kernel,
-        out_shape=(rim_x, rim_x, rim_y, rim_y, shape(groups, ROW, dtype=jnp.int32)),
-        in_specs=[vmem()] * 4,
-        out_specs=(vmem(),) * 5,
+    tall = tile_x + 2 * WIDTH
+    rim_y = shape(pl.cdiv(channels + 1, ROW // WIDTH) * tall, ROW)
+    first_y, last_y, panel_slots = pl.pallas_call(
+        strip_rim_kernel,
+        out_shape=(rim_y, rim_y, shape(groups, ROW, dtype=jnp.int32)),
+        in_specs=[smem()] + [vmem()] * 6,
+        out_specs=(vmem(),) * 3,
         compiler_params=params(),
         cost_estimate=pl.CostEstimate(flops=3_000_000, bytes_accessed=2_000_000, transcendentals=0),
         name="pack_rims",
-    )(late_parent, late_metric, late_dest.reshape(groups, ROW), late_col.reshape(groups, ROW))
-    after_x, before_x = shifted(first_x, last_x, "gx")
-    moved, after_x, before_x, panel_slots = lax.optimization_barrier(
-        (moved, after_x, before_x, panel_slots)
-    )
-    tall = tile_x + 2 * WIDTH
-    tall_y = shape(quarters * tall, ROW)
-    first_y, last_y = pl.pallas_call(
-        corner_kernel,
-        out_shape=(tall_y, tall_y),
-        in_specs=[vmem()] * 4,
-        out_specs=(vmem(),) * 2,
-        compiler_params=params(),
-        name="pack_corners",
-    )(own_first, own_last, after_x, before_x)
+    )(
+        odd,
+        late_parent,
+        late_metric,
+        near,
+        far,
+        late_dest.reshape(groups, ROW),
+        late_col.reshape(groups, ROW),
+    )
     after_y, before_y = shifted(first_y, last_y, "gy")
+    moved, after_y, before_y, panel_slots = lax.optimization_barrier(
+        (moved, after_y, before_y, panel_slots)
+    )
     nest_out, packed = pl.pallas_call(
         functools.partial(nest_kernel, size_x=block_x),
         out_shape=(shape(*block_shape), shape(*packed_shape)),
-        in_specs=[anywhere(), anywhere(), vmem()] + [smem()] * 4,
+        in_specs=[anywhere()] * 7,
         out_specs=(anywhere(), anywhere()),
         scratch_shapes=[
             pltpu.VMEM(packed_shape, jnp.float32),
             pltpu.VMEM(block_shape, jnp.float32),
+            pltpu.VMEM((block_x, block_y), jnp.float32),
+            pltpu.SMEM(buoyancy.shape, jnp.float32),
+            index(pltpu.SMEM),
+            index(pltpu.SMEM),
+            index(pltpu.SMEM),
             pltpu.VMEM(block_shape, jnp.float32),
             pltpu.VMEM((block_x * block_y, 2 * ROW), jnp.float32),
             pltpu.VMEM((block_x * block_y, ROW), jnp.float32),
             pltpu.VMEM((devices * CAP, ROW), jnp.float32),
-            pltpu.SemaphoreType.DMA((3,)),
-            pltpu.SemaphoreType.DMA((parts,)),
-        ],
+        ]
+        + add_scratch(devices)
+        + [pltpu.SemaphoreType.DMA((6,)), pltpu.SemaphoreType.DMA((parts,))],
         compiler_params=params(),
         name="step_nest",
     )(
@@ -513,13 +616,12 @@
         panel_col,
         panel_slots.reshape(slots),
     )
-    packed, after_y, before_y = lax.optimization_barrier((packed, after_y, before_y))
     moved = exchange(packed, devices)
     edge = jnp.stack([lax.axis_index("gx") == 0, lax.axis_index("gy") == 0]).astype(jnp.int32)
     parent_state = pl.pallas_call(
         parent_kernel,
         out_shape=shape(*tile_shape),
-        in_specs=[smem(), smem()] + [vmem()] * 6,
+        in_specs=[smem()] * 3 + [vmem()] * 6,
         out_specs=vmem(),
         scratch_shapes=[
             pltpu.VMEM((channels, tall, 2 * ROW), jnp.float32),
@@ -528,19 +630,21 @@
         compiler_params=params(),
         cost_estimate=pl.CostEstimate(flops=20_000_000, bytes_accessed=8_000_000, transcendentals=0),
         name="step_parent",
-    )(edge, buoyancy, late_parent, late_metric, after_x, before_x, after_y, before_y)
+    )(odd, edge, buoyancy, late_parent, late_metric, near, far, after_y, before_y)
 
     parent_out = pl.pallas_call(
         functools.partial(final_kernel, size_x=tile_x),
-        out_shape=shape(*tile_shape),
+        out_shape=shape(channels, tile_x, tile_y),
         in_specs=[anywhere(), anywhere()],
         out_specs=anywhere(),
         scratch_shapes=[
             pltpu.VMEM(packed_shape, jnp.float32),
             pltpu.VMEM(tile_shape, jnp.float32),
+            pltpu.VMEM((channels, tile_x, tile_y), jnp.float32),
             pltpu.VMEM((tile_x * tile_y, 2 * ROW), jnp.float32),
-            pltpu.SemaphoreType.DMA((3,)),
-        ],
+        ]
+        + add_scratch(devices)
+        + [pltpu.SemaphoreType.DMA((1,)), pltpu.SemaphoreType.DMA((parts,))],
         compiler_params=params(),
         name="add_panels",
     )(moved, parent_state)

time: 119 us -> 108 us (0.908)
  the two profiles are of different devices: /device:TPU:10 before, /device:TPU:1 now
where the time goes in v3:
time: 108 us; the launch traced here: 107 us
  Pallas kernels  48.2 us (45%)
  waiting for transfers between devices  30.2 us (28%)
  starting transfers between devices  27.4 us (25%)
    all_to_all x2, waiting for transfers between devices, exchange(): lax.all_to_all(packed.reshape(devices, KEEP * ROW), ('gx', 'gy'), split_a...  18.4 us
    all_to_all x2, starting transfers between devices, exchange(): lax.all_to_all(packed.reshape(devices, KEEP * ROW), ('gx', 'gy'), split_a...  16.9 us
    pallas_call x1, Pallas kernels, on_device(): pl.pallas_call(functools.partial(nest_kernel, size_x=block_x), out_shape=...  14.5 us
    pallas_call x1, Pallas kernels, on_device(): pl.pallas_call(functools.partial(final_kernel, size_x=tile_x), out_shape=...  12.3 us
    ppermute x2, waiting for transfers between devices, shifted(): return (lax.ppermute(first, axis, down), lax.ppermute(last, axis, up))  11.8 us
    pallas_call x1, Pallas kernels, on_device(): pl.pallas_call(parent_kernel, out_shape=shape(*tile_shape), in_specs=[sme...  9.79 us
    pallas_call x1, Pallas kernels, on_device(): pl.pallas_call(functools.partial(strip_kernel, size_x=tile_x, cells=block...  5.98 us
    ppermute x2, starting transfers between devices, shifted(): return (lax.ppermute(first, axis, down), lax.ppermute(last, axis, up))  5.96 us
  transfers between devices with their start and end apart: 6, of which 3 were waited for; matrix products, arithmetic and copies ran while one was open for 1% of the time, Pallas kernels for 18%

profile of v3, /device:TPU:1, one launch (start us, length us, event | category | flops | bytes accessed | tf_op | source)
XLA Modules:
  0.0 107.3 jit_solution(15925561852882282546)
XLA Ops:
  0.6 2.0 %cut_rims.1 = (f32[404,128]{1,0:T(8,128)}, f32[404,128]{1,0:T(8,128)}) custom-call(s32[1]{0:T(128)} %bitcast.3.odd, f32[100,32,128]{2,1,0:T(8,128)} %bitcast.17, f32[100,32,128]{2,1,0:T(8,128)} %bitcast.18, f32[32,128]{1,0:T(8,128)} %metric.5), custom_call_target="tpu_custom_call" | custom-call | tf_op jit(solution)/shard_map/cut_rims/pallas_call | solution.py:520
  2.6 1.4 %collective-permute-start = (f32[404,128]{1,0:T(8,128)}, f32[404,128]{1,0:T(8,128)}, u32[]{:S(2)}, u32[]{:S(2)}) collective-permute-start(f32[404,128]{1,0:T(8,128)} %get-tuple-element.20), channel_id=1, source_target_pairs={{0,16},{32,48},{64,80},{96,112},{16,0},{48,32},{80,64},{112,96},{1... | collective-permute-start | bytes 620552 | tf_op jit(solution)/shard_map/ppermute | solution.py:471
  4.0 3.2 %collective-permute-start.1 = (f32[404,128]{1,0:T(8,128)}, f32[404,128]{1,0:T(8,128)}, u32[]{:S(2)}, u32[]{:S(2)}) collective-permute-start(f32[404,128]{1,0:T(8,128)} %get-tuple-element.21), channel_id=1, source_target_pairs={{16,32},{48,64},{80,96},{32,16},{64,48},{96,80},{17,33},{49,65},{8... | collective-permute-start | bytes 620552 | tf_op jit(solution)/shard_map/ppermute | solution.py:471
  7.2 6.0 %pack_strips.1 = f32[3328,128]{1,0:T(8,128)} custom-call(f32[3200,128]{1,0:T(8,128)} %bitcast.19, s32[8,128]{1,0:T(8,128)} %bitcast.28, s32[1024]{0:T(1024)} %picks.2, s32[1024]{0:T(1024)} %spots.2, s32[8,128]{1,0:T(8,128)} %bitcast.26), custom_call_target="tpu_custom_call" | custom-call | tf_op jit(solution)/shard_map/pack_strips/pallas_call | solution.py:530
  13.2 0.0 collective-permute-done.near
  13.2 0.0 collective-permute-done.1.far
  13.2 10.2 %all-to-all-start = ((f32[128,1,3328]{2,1,0:T(1,128)}), f32[128,1,3328]{2,1,0:T(1,128)}, u32[]{:S(2)}, u32[]{:S(2)}) async-start(f32[128,1,3328]{2,1,0:T(1,128)} %bitcast.22), calls=%async_computation | async-start | bytes 3407872 | tf_op jit(solution)/shard_map/all_to_all | solution.py:461
  23.5 3.6 %pack_rims.1 = (f32[160,128]{1,0:T(8,128)}, f32[160,128]{1,0:T(8,128)}, s32[8,128]{1,0:T(8,128)}) custom-call(s32[1]{0:T(128)} %bitcast.3.odd, f32[3200,128]{1,0:T(8,128)} %bitcast.20, f32[32,128]{1,0:T(8,128)} %metric.5, f32[404,128]{1,0:T(8,128)} %collective-permute-done.near, f32[404,128]{1,0:T(8,128)} %collective-permute-done.1.far, s32[8,128]{1,0:T(8,128)} %bitcast.29, ...), custom_call_target="tpu_custom_call" | custom-call | flops 3000000 | bytes 2000000 | tf_op jit(solution)/shard_map/pack_rims/pallas_call | solution.py:567
  27.1 1.3 %collective-permute-start.2 = (f32[160,128]{1,0:T(8,128)}, f32[160,128]{1,0:T(8,128)}, u32[]{:S(2)}, u32[]{:S(2)}) collective-permute-start(f32[160,128]{1,0:T(8,128)} %get-tuple-element.29), channel_id=1, source_target_pairs={{1,0},{2,1},{3,2},{4,3},{5,4},{6,5},{7,6},{8,7},{9,8},{10,9},{11,1... | collective-permute-start | bytes 245768 | tf_op jit(solution)/shard_map/ppermute | solution.py:478
  28.4 4.7 %collective-permute-start.3 = (f32[160,128]{1,0:T(8,128)}, f32[160,128]{1,0:T(8,128)}, u32[]{:S(2)}, u32[]{:S(2)}) collective-permute-start(f32[160,128]{1,0:T(8,128)} %get-tuple-element.30), channel_id=1, source_target_pairs={{0,1},{1,2},{2,3},{3,4},{4,5},{5,6},{6,7},{7,8},{8,9},{9,10},{10,1... | collective-permute-start | bytes 245768 | tf_op jit(solution)/shard_map/ppermute | solution.py:478
  33.0 11.8 %collective-permute-done.2.after_y = f32[160,128]{1,0:T(8,128)} collective-permute-done((f32[160,128]{1,0:T(8,128)}, f32[160,128]{1,0:T(8,128)}, u32[]{:S(2)}, u32[]{:S(2)}) %collective-permute-start.2) | collective-permute-done | bytes 81952 | tf_op jit(solution)/shard_map/ppermute | solution.py:478
  44.8 0.0 collective-permute-done.3.before_y
  44.8 3.7 %all-to-all-done = f32[128,1,3328]{2,1,0:T(1,128)} async-done(((f32[128,1,3328]{2,1,0:T(1,128)}), f32[128,1,3328]{2,1,0:T(1,128)}, u32[]{:S(2)}, u32[]{:S(2)}) %all-to-all-start) | async-done | bytes 1703968 | tf_op jit(solution)/shard_map/all_to_all | solution.py:461
  48.6 14.5 %step_nest.1 = (f32[2400,128]{1,0:T(8,128)}, f32[3328,128]{1,0:T(8,128)}) custom-call(f32[3328,128]{1,0:T(8,128)} %bitcast.6.moved, f32[2400,128]{1,0:T(8,128)} %bitcast.25, f32[24,128]{1,0:T(8,128)} %metric.4, f32[20]{0:T(128)} %buoyancy.3, s32[1024]{0:T(1024)} %picks.3, s32[1024]{0:T(1024)} %spots.3, s32[1024]{0:T(1024)} %bitcast.30), custom_call_target="tpu_custom_call" | custom-call | tf_op jit(solution)/shard_map/step_nest/pallas_call | solution.py:588
  63.0 6.6 %all-to-all-start.1 = ((f32[128,1,3328]{2,1,0:T(1,128)}), f32[128,1,3328]{2,1,0:T(1,128)}, u32[]{:S(2)}, u32[]{:S(2)}) async-start(f32[128,1,3328]{2,1,0:T(1,128)} %bitcast.23), calls=%async_computation.1 | async-start | bytes 3407872 | tf_op jit(solution)/shard_map/all_to_all | solution.py:461
  69.7 0.7 add_convert_fusion.edge
  70.4 9.8 %step_parent.1.parent = f32[3200,128]{1,0:T(8,128)} custom-call(s32[1]{0:T(128)} %bitcast.3.odd, s32[2]{0:T(128)} %add_convert_fusion.edge, f32[20]{0:T(128)} %buoyancy.3, f32[3200,128]{1,0:T(8,128)} %bitcast.21, f32[32,128]{1,0:T(8,128)} %metric.5, f32[404,128]{1,0:T(8,128)} %collective-permute-done.near, f32[404,128]{1,0:T(8,128)} %collective-permute-done.1.far, ...), custom_call_target="tpu_custom_call" | custom-call | flops 20000000 | bytes 8000000 | tf_op jit(solution)/shard_map/step_parent/pallas_call | solution.py:621
  80.1 14.7 %all-to-all-done.1 = f32[128,1,3328]{2,1,0:T(1,128)} async-done(((f32[128,1,3328]{2,1,0:T(1,128)}), f32[128,1,3328]{2,1,0:T(1,128)}, u32[]{:S(2)}, u32[]{:S(2)}) %all-to-all-start.1) | async-done | bytes 1703968 | tf_op jit(solution)/shard_map/all_to_all | solution.py:461
  94.8 12.3 %add_panels.1 = f32[100,32,128]{2,1,0:T(8,128)} custom-call(f32[3328,128]{1,0:T(8,128)} %bitcast.12.moved, f32[3200,128]{1,0:T(8,128)} %step_parent.1.parent), custom_call_target="tpu_custom_call" | custom-call | tf_op jit(solution)/shard_map/add_panels/pallas_call | solution.py:635
Async XLA Ops:
  2.6 10.6 %collective-permute-start = (f32[404,128]{1,0:T(8,128)}, f32[404,128]{1,0:T(8,128)}, u32[]{:S(2)}, u32[]{:S(2)}) collective-permute-start(f32[404,128]{1,0:T(8,128)} %get-tuple-element.20), channel_id=1, source_target_pairs={{0,16},{32,48},{64,80},{96,112},{16,0},{48,32},{80,64},{112,96},{1... | collective-permute-start | bytes 620552 | tf_op jit(solution)/shard_map/ppermute | solution.py:471
  4.0 9.2 %collective-permute-start.1 = (f32[404,128]{1,0:T(8,128)}, f32[404,128]{1,0:T(8,128)}, u32[]{:S(2)}, u32[]{:S(2)}) collective-permute-start(f32[404,128]{1,0:T(8,128)} %get-tuple-element.21), channel_id=1, source_target_pairs={{16,32},{48,64},{80,96},{32,16},{64,48},{96,80},{17,33},{49,65},{8... | collective-permute-start | bytes 620552 | tf_op jit(solution)/shard_map/ppermute | solution.py:471
  13.2 35.3 %all-to-all-start = ((f32[128,1,3328]{2,1,0:T(1,128)}), f32[128,1,3328]{2,1,0:T(1,128)}, u32[]{:S(2)}, u32[]{:S(2)}) async-start(f32[128,1,3328]{2,1,0:T(1,128)} %bitcast.22), calls=%async_computation | async-start | bytes 3407872 | tf_op jit(solution)/shard_map/all_to_all | solution.py:461
  27.1 17.7 %collective-permute-start.2 = (f32[160,128]{1,0:T(8,128)}, f32[160,128]{1,0:T(8,128)}, u32[]{:S(2)}, u32[]{:S(2)}) collective-permute-start(f32[160,128]{1,0:T(8,128)} %get-tuple-element.29), channel_id=1, source_target_pairs={{1,0},{2,1},{3,2},{4,3},{5,4},{6,5},{7,6},{8,7},{9,8},{10,9},{11,1... | collective-permute-start | bytes 245768 | tf_op jit(solution)/shard_map/ppermute | solution.py:478
  28.4 16.5 %collective-permute-start.3 = (f32[160,128]{1,0:T(8,128)}, f32[160,128]{1,0:T(8,128)}, u32[]{:S(2)}, u32[]{:S(2)}) collective-permute-start(f32[160,128]{1,0:T(8,128)} %get-tuple-element.30), channel_id=1, source_target_pairs={{0,1},{1,2},{2,3},{3,4},{4,5},{5,6},{6,7},{7,8},{8,9},{9,10},{10,1... | collective-permute-start | bytes 245768 | tf_op jit(solution)/shard_map/ppermute | solution.py:478
  63.0 31.8 %all-to-all-start.1 = ((f32[128,1,3328]{2,1,0:T(1,128)}), f32[128,1,3328]{2,1,0:T(1,128)}, u32[]{:S(2)}, u32[]{:S(2)}) async-start(f32[128,1,3328]{2,1,0:T(1,128)} %bitcast.23), calls=%async_computation.1 | async-start | bytes 3407872 | tf_op jit(solution)/shard_map/all_to_all | solution.py:461

commit v4 on v3

--- a/solution.py
+++ b/solution.py
@@ -23,6 +23,7 @@
 REST = CAP - KEEP
 GROUP = 8
 STEP = 2
+MARGINS = (4, 8)
 VMEM_BYTES = 65500 * 1024
 
 
@@ -51,11 +52,19 @@
     return jnp.where(slot < KEEP, dest * KEEP + slot, spill)
 
 
+def padded(channels):
+    return pl.cdiv(channels, 8) * 8
+
+
 def to_rows(fields, rows, channels, size_x):
-    tail = jnp.zeros((ROW - channels, ROW), jnp.float32)
+    height = padded(channels)
+    real = lax.broadcasted_iota(jnp.int32, (8, ROW), 0) < channels - (height - 8)
+    tail = jnp.zeros((ROW - height, ROW), jnp.float32)
     for i in range(size_x):
-        block = fields[pl.ds(i, channels, stride=size_x), :]
-        rows[i * ROW : (i + 1) * ROW, :] = jnp.concatenate([block, tail], 0).T
+        block = fields[pl.ds(i, height, stride=size_x), :]
+        final = jnp.where(real, block[height - 8 :], 0.0)
+        block = jnp.concatenate([block[: height - 8], final, tail], 0)
+        rows[i * ROW : (i + 1) * ROW, :] = block.T
 
 
 def clear_rows(staged):
@@ -93,42 +102,48 @@
     return copies
 
 
-def slot_values(moved, s):
-    devices = moved.shape[0] // KEEP
+def slot_values(moved, s, base, count):
     if s < KEEP:
-        return moved[pl.ds(s, devices, stride=KEEP), :]
-    lane = lax.broadcasted_iota(jnp.int32, (devices, ROW), 1)
-    values = jnp.zeros((devices, ROW), jnp.float32)
+        return moved[pl.ds(base * KEEP + s, count, stride=KEEP), :]
+    lane = lax.broadcasted_iota(jnp.int32, (count, ROW), 1)
+    values = jnp.zeros((count, ROW), jnp.float32)
     for b in range(PIECES):
-        piece = moved[pl.ds(b * REST + s - KEEP, devices, stride=KEEP), :]
-        piece = pltpu.roll(piece, (b * PIECE - FREE) % ROW, 1)
+        where = pl.ds(base * KEEP + b * REST + s - KEEP, count, stride=KEEP)
+        piece = pltpu.roll(moved[where, :], (b * PIECE - FREE) % ROW, 1)
         values = jnp.where((lane >= b * PIECE) & (lane < (b + 1) * PIECE), piece, values)
     return values
 
 
-def prepare(moved, weights, columns, easts, size_x):
+def prepare(moved, arrivals, later, weights, columns, easts, size_x):
     lane = lax.broadcasted_iota(jnp.int32, (16, 2 * ROW), 1)
     pick = jnp.where((lane == SPOT) | (lane == SPOT + ROW), 1.0, 0.0).astype(jnp.bfloat16)
     devices = moved.shape[0] // KEEP
     depth = devices * GROUP
     tiles = CAP // GROUP
+    count = devices // len(arrivals)
     north = lax.broadcasted_iota(jnp.int32, (ROW, depth), 0)
-    tally = lax.broadcasted_iota(jnp.int32, (devices, ROW), 1) == TALLY
+    tally = lax.broadcasted_iota(jnp.int32, (count, ROW), 1) == TALLY
+    for part, arrival in enumerate(arrivals):
+        arrival.wait()
+        base = part * count
+        for s in range(CAP):
+            values = jnp.where(tally, 1.0, slot_values(moved, s, base, count))
+            high = values.astype(jnp.bfloat16)
+            low = (values - high.astype(jnp.float32)).astype(jnp.bfloat16)
+            t, k = s // GROUP, s % GROUP
+            start = t * depth + k * devices + base
+            weights[start : start + count, :ROW] = high
+            weights[start : start + count, ROW:] = low
+    for copy in later:
+        copy.start()
     reaches = []
     for t in range(tiles):
-        for k in range(GROUP):
-            values = jnp.where(tally, 1.0, slot_values(moved, t * GROUP + k))
-            high = values.astype(jnp.bfloat16)
-            low = (values - high.astype(jnp.float32)).astype(jnp.bfloat16)
-            where = slice(k * devices, (k + 1) * devices)
-            weights[t, where, :ROW] = high
-            weights[t, where, ROW:] = low
         spot = lax.dot_general(
-            pick, weights[t], (((1,), (1,)), ((), ())), preferred_element_type=jnp.float32
+            pick, weights[t * depth : (t + 1) * depth, :], (((1,), (1,)), ((), ())), preferred_element_type=jnp.float32
         )
         whole = spot.astype(jnp.int32)
         east, within = whole >> 7, whole & (ROW - 1)
-        easts[t] = east
+        easts[t] = east.astype(jnp.float32).astype(jnp.bfloat16)
         columns[t] = jnp.where(north == within[0:1], 1.0, 0.0).astype(jnp.bfloat16)
         used = spot[0:8] >= 0.0
         reach = east[0:8].astype(jnp.float32)
@@ -138,54 +153,57 @@
     return reaches
 
 
-def add_rows(moved, sums, weights, columns, easts, size_x):
+def add_rows(moved, arrivals, later, sums, weights, columns, easts, size_x):
     tiles, depth = easts.shape[0], easts.shape[2]
-    reaches = prepare(moved, weights, columns, easts, size_x)
+    reaches = prepare(moved, arrivals, later, weights, columns, easts, size_x)
 
     def block(t, here):
         column = columns[t].reshape(ROW // 16, 16, depth)
         parts = []
         for k in range(STEP):
-            mine = jnp.where(easts[t] == here + k, 1.0, 0.0).astype(jnp.bfloat16)
+            place = jnp.asarray(here + k, jnp.float32).astype(jnp.bfloat16)
+            mine = jnp.where(easts[t] == place, 1.0, 0.0).astype(jnp.bfloat16)
             parts.append((column * mine[None]).reshape(ROW, depth))
         where = pl.ds(pl.multiple_of(here * ROW, ROW), STEP * ROW)
         sums[where, :] += jnp.dot(
-            jnp.concatenate(parts, 0), weights[t], preferred_element_type=jnp.float32
+            jnp.concatenate(parts, 0),
+            weights[t * depth : (t + 1) * depth, :],
+            preferred_element_type=jnp.float32,
         )
 
-    windows = []
-    for t in range(tiles):
-        share = 9 if t in (0, tiles - 1) else 12
-        windows.append(min(size_x, pl.cdiv(size_x * share, 16 * STEP) * STEP))
-    narrow = functools.reduce(
-        jnp.logical_and, [last - first < width for (first, last), width in zip(reaches, windows)]
-    )
+    low = [min(size_x, size_x // 2 + margin) for margin in MARGINS]
+    widths = low + low[::-1]
+    fits = [last - first < width for (first, last), width in zip(reaches, widths)]
+    narrow = functools.reduce(jnp.logical_and, fits)
 
     @pl.when(narrow)
     def _():
         for t in range(tiles):
-            start = jnp.minimum(reaches[t][0], size_x - windows[t])
-            for g in range(windows[t] // STEP):
+            start = jnp.minimum(reaches[t][0], size_x - widths[t])
+            for g in range(widths[t] // STEP):
                 block(t, start + g * STEP)
 
     @pl.when(jnp.logical_not(narrow))
     def _():
         for t in range(tiles):
-
-            def whole_tile(g, carry, t=t):
-                block(t, g * STEP)
+            first, last = reaches[t]
+            blocks = jnp.maximum(last - first + STEP, 0) // STEP
+            start = jnp.minimum(first, size_x - blocks * STEP)
+
+            def reached(g, carry, t=t, start=start):
+                block(t, start + g * STEP)
                 return carry
 
-            lax.fori_loop(0, size_x // STEP, whole_tile, 0)
+            lax.fori_loop(0, blocks, reached, 0)
 
 
 def add_scratch(devices):
     depth = devices * GROUP
     tiles = CAP // GROUP
     return [
-        pltpu.VMEM((tiles, depth, 2 * ROW), jnp.bfloat16),
+        pltpu.VMEM((tiles * depth, 2 * ROW), jnp.bfloat16),
         pltpu.VMEM((tiles, ROW, depth), jnp.bfloat16),
-        pltpu.VMEM((tiles, 16, depth), jnp.int32),
+        pltpu.VMEM((tiles, 16, depth), jnp.bfloat16),
     ]
 
 
@@ -193,8 +211,9 @@
     block = slice(i * ROW, (i + 1) * ROW)
     total = (sums[block, :ROW] + sums[block, ROW:]).T
     share = 1.0 / (1.0 + total[TALLY : TALLY + 1])
-    where = pl.ds(i, channels, stride=size_x)
-    out[where, :] = (fields[where, :] + total[:channels]) * share
+    height = padded(channels)
+    where = pl.ds(i, height, stride=size_x)
+    out[where, :] = (fields[where, :] + total[:height]) * share
 
 
 def nest_step(state, metric, buoyancy, levels, size_x):
@@ -230,8 +249,12 @@
         p = p_above
 
 
+def planned(pairs, sems):
+    return [pltpu.make_async_copy(a, b, sems.at[i]) for i, (a, b) in enumerate(pairs)]
+
+
 def fetch(pairs, sems):
-    copies = [pltpu.make_async_copy(a, b, sems.at[i]) for i, (a, b) in enumerate(pairs)]
+    copies = planned(pairs, sems)
     for copy in copies:
         copy.start()
     return copies
@@ -277,16 +300,14 @@
 ):
     channels = nest.shape[0] // size_x
     arrivals = fetch(split(moved, came, out_sems.shape[0]), out_sems)
-    copies = fetch(
-        [(nest, tile), (metric, metric_v), (buoyancy, buoyancy_s)]
+    copies = planned(
+        [(nest, tile.at[pl.ds(0, nest.shape[0])]), (metric, metric_v), (buoyancy, buoyancy_s)]
         + [(picks, picks_s), (spots, spots_s), (slots, slots_s)],
         sems,
     )
     sums[...] = jnp.zeros(sums.shape, jnp.float32)
     clear_rows(staged)
-    for copy in arrivals:
-        copy.wait()
-    add_rows(came, sums, weights, columns, easts, size_x)
+    add_rows(came, arrivals, copies, sums, weights, columns, easts, size_x)
     for copy in copies:
         copy.wait()
     for i in range(size_x):
@@ -297,7 +318,7 @@
         return carry
 
     lax.fori_loop(0, NSN, step, 0)
-    result = pltpu.make_async_copy(state, out, sems.at[0])
+    result = pltpu.make_async_copy(state.at[pl.ds(0, out.shape[0])], out, sems.at[0])
     result.start()
     to_rows(state, rows, channels, size_x)
     for copy in pack_rows(rows, picks_s, spots_s, slots_s, staged, packed, out_sems):
@@ -307,18 +328,18 @@
 
 def rim_kernel(odd, head, tail, metric, near, far):
     channels, block = head.shape[:2]
-    head, tail = (ref.reshape(channels * block, ROW) for ref in (head, tail))
     size_x = metric.shape[0]
 
     def cut(first, last):
-        for r in range(WIDTH):
-            there = pl.ds(r, channels, stride=WIDTH)
-            end = block - WIDTH + r
-            first[there, :] = head[pl.ds(r, channels, stride=block), :]
-            last[there, :] = tail[pl.ds(end, channels, stride=block), :]
-            own, end = channels * WIDTH + r, size_x - WIDTH + r
-            first[own : own + 1, :] = metric[r : r + 1]
-            last[own : own + 1, :] = metric[end : end + 1]
+        for c in range(0, channels, 2):
+            pair = slice(c * WIDTH, (c + 2) * WIDTH)
+            first[pair, :] = jnp.concatenate([head[c, :WIDTH], head[c + 1, :WIDTH]], 0)
+            last[pair, :] = jnp.concatenate(
+                [tail[c, block - WIDTH :], tail[c + 1, block - WIDTH :]], 0
+            )
+        own = slice(channels * WIDTH, (channels + 1) * WIDTH)
+        first[own, :] = metric[:WIDTH]
+        last[own, :] = metric[size_x - WIDTH :]
 
     @pl.when(odd[0] == 1)
     def _():
@@ -421,23 +442,20 @@
 ):
     channels = parent.shape[0] // size_x
     arrivals = fetch(split(moved, came, out_sems.shape[0]), out_sems)
-    copies = fetch([(parent, tile)], sems)
+    copies = planned([(parent, tile.at[pl.ds(0, parent.shape[0])])], sems)
+    flat = result.reshape(padded(channels) * size_x, ROW)
+    count = size_x // out_sems.shape[0]
+    blocks = [(pl.ds(0, channels), pl.ds(start, count)) for start in range(0, size_x, count)]
+    leaving = planned([(result.at[block], out.at[block]) for block in blocks], out_sems)
+
     sums[...] = jnp.zeros(sums.shape, jnp.float32)
-    for copy in arrivals:
-        copy.wait()
-    add_rows(came, sums, weights, columns, easts, size_x)
+    add_rows(came, arrivals, copies, sums, weights, columns, easts, size_x)
     copies[0].wait()
-    flat = result.reshape(channels * size_x, ROW)
-    parts = out_sems.shape[0]
-    count = size_x // parts
-    copies = []
-    for part in range(parts):
-        for i in range(part * count, (part + 1) * count):
-            relax(tile, sums, flat, channels, size_x, i)
-        block = (slice(None), pl.ds(part * count, count))
-        copies.append(pltpu.make_async_copy(result.at[block], out.at[block], out_sems.at[part]))
-        copies[-1].start()
-    for copy in copies:
+    for i in range(size_x):
+        relax(tile, sums, flat, channels, size_x, i)
+        if i % count == count - 1:
+            leaving[i // count].start()
+    for copy in leaving:
         copy.wait()
 
 
@@ -533,7 +551,7 @@
         in_specs=[anywhere()] * 5,
         out_specs=anywhere(),
         scratch_shapes=[
-            pltpu.VMEM(tile_shape, jnp.float32),
+            pltpu.VMEM((padded(channels) * tile_x, tile_y), jnp.float32),
             listed,
             index(pltpu.SMEM),
             index(pltpu.SMEM),
@@ -592,13 +610,13 @@
         out_specs=(anywhere(), anywhere()),
         scratch_shapes=[
             pltpu.VMEM(packed_shape, jnp.float32),
-            pltpu.VMEM(block_shape, jnp.float32),
+            pltpu.VMEM((padded(channels) * block_x, block_y), jnp.float32),
             pltpu.VMEM((block_x, block_y), jnp.float32),
             pltpu.SMEM(buoyancy.shape, jnp.float32),
             index(pltpu.SMEM),
             index(pltpu.SMEM),
             index(pltpu.SMEM),
-            pltpu.VMEM(block_shape, jnp.float32),
+            pltpu.VMEM((padded(channels) * block_x, block_y), jnp.float32),
             pltpu.VMEM((block_x * block_y, 2 * ROW), jnp.float32),
             pltpu.VMEM((block_x * block_y, ROW), jnp.float32),
             pltpu.VMEM((devices * CAP, ROW), jnp.float32),
@@ -639,8 +657,8 @@
         out_specs=anywhere(),
         scratch_shapes=[
             pltpu.VMEM(packed_shape, jnp.float32),
-            pltpu.VMEM(tile_shape, jnp.float32),
-            pltpu.VMEM((channels, tile_x, tile_y), jnp.float32),
+            pltpu.VMEM((padded(channels) * tile_x, tile_y), jnp.float32),
+            pltpu.VMEM((padded(channels), tile_x, tile_y), jnp.float32),
             pltpu.VMEM((tile_x * tile_y, 2 * ROW), jnp.float32),
         ]
         + add_scratch(devices)

time: 108 us -> 108 us (level)
  no operation moved by 1% of the time
where the time goes in v4:
time: 108 us
  Pallas kernels  48.9 us (45%)
  waiting for transfers between devices  30.2 us (28%)
  starting transfers between devices  27.4 us (25%)
    all_to_all x2, waiting for transfers between devices, exchange(): lax.all_to_all(packed.reshape(devices, KEEP * ROW), ('gx', 'gy'), split_a...  18.4 us
    all_to_all x2, starting transfers between devices, exchange(): lax.all_to_all(packed.reshape(devices, KEEP * ROW), ('gx', 'gy'), split_a...  16.9 us
    pallas_call x1, Pallas kernels, on_device(): pl.pallas_call(functools.partial(nest_kernel, size_x=block_x), out_shape=...  14.7 us
    pallas_call x1, Pallas kernels, on_device(): pl.pallas_call(functools.partial(final_kernel, size_x=tile_x), out_shape=...  12.9 us
    ppermute x2, waiting for transfers between devices, shifted(): return (lax.ppermute(first, axis, down), lax.ppermute(last, axis, up))  11.8 us
    pallas_call x1, Pallas kernels, on_device(): pl.pallas_call(parent_kernel, out_shape=shape(*tile_shape), in_specs=[sme...  9.79 us
    pallas_call x1, Pallas kernels, on_device(): pl.pallas_call(functools.partial(strip_kernel, size_x=tile_x, cells=block...  6.02 us
    ppermute x2, starting transfers between devices, shifted(): return (lax.ppermute(first, axis, down), lax.ppermute(last, axis, up))  5.96 us
  transfers between devices with their start and end apart: 6, of which 3 were waited for; matrix products, arithmetic and copies ran while one was open for 1% of the time, Pallas kernels for 18%

profile of v4, /device:TPU:1, one launch (start us, length us, event | category | flops | bytes accessed | tf_op | source)
XLA Modules:
  0.0 108.0 jit_solution(1221278730947056157)
XLA Ops:
  0.6 2.0 %cut_rims.1 = (f32[404,128]{1,0:T(8,128)}, f32[404,128]{1,0:T(8,128)}) custom-call(s32[1]{0:T(128)} %bitcast.3.odd, f32[100,32,128]{2,1,0:T(8,128)} %bitcast.17, f32[100,32,128]{2,1,0:T(8,128)} %bitcast.18, f32[32,128]{1,0:T(8,128)} %metric.5), custom_call_target="tpu_custom_call" | custom-call | tf_op jit(solution)/shard_map/cut_rims/pallas_call | solution.py:538
  2.6 1.4 %collective-permute-start = (f32[404,128]{1,0:T(8,128)}, f32[404,128]{1,0:T(8,128)}, u32[]{:S(2)}, u32[]{:S(2)}) collective-permute-start(f32[404,128]{1,0:T(8,128)} %get-tuple-element.20), channel_id=1, source_target_pairs={{0,16},{32,48},{64,80},{96,112},{16,0},{48,32},{80,64},{112,96},{1... | collective-permute-start | bytes 620552 | tf_op jit(solution)/shard_map/ppermute | solution.py:489
  4.0 3.2 %collective-permute-start.1 = (f32[404,128]{1,0:T(8,128)}, f32[404,128]{1,0:T(8,128)}, u32[]{:S(2)}, u32[]{:S(2)}) collective-permute-start(f32[404,128]{1,0:T(8,128)} %get-tuple-element.21), channel_id=1, source_target_pairs={{16,32},{48,64},{80,96},{32,16},{64,48},{96,80},{17,33},{49,65},{8... | collective-permute-start | bytes 620552 | tf_op jit(solution)/shard_map/ppermute | solution.py:489
  7.2 6.0 %pack_strips.1 = f32[3328,128]{1,0:T(8,128)} custom-call(f32[3200,128]{1,0:T(8,128)} %bitcast.19, s32[8,128]{1,0:T(8,128)} %bitcast.28, s32[1024]{0:T(1024)} %picks.2, s32[1024]{0:T(1024)} %spots.2, s32[8,128]{1,0:T(8,128)} %bitcast.26), custom_call_target="tpu_custom_call" | custom-call | tf_op jit(solution)/shard_map/pack_strips/pallas_call | solution.py:548
  13.2 0.0 collective-permute-done.near
  13.2 0.0 collective-permute-done.1.far
  13.2 10.2 %all-to-all-start = ((f32[128,1,3328]{2,1,0:T(1,128)}), f32[128,1,3328]{2,1,0:T(1,128)}, u32[]{:S(2)}, u32[]{:S(2)}) async-start(f32[128,1,3328]{2,1,0:T(1,128)} %bitcast.22), calls=%async_computation | async-start | bytes 3407872 | tf_op jit(solution)/shard_map/all_to_all | solution.py:479
  23.5 3.6 %pack_rims.1 = (f32[160,128]{1,0:T(8,128)}, f32[160,128]{1,0:T(8,128)}, s32[8,128]{1,0:T(8,128)}) custom-call(s32[1]{0:T(128)} %bitcast.3.odd, f32[3200,128]{1,0:T(8,128)} %bitcast.20, f32[32,128]{1,0:T(8,128)} %metric.5, f32[404,128]{1,0:T(8,128)} %collective-permute-done.near, f32[404,128]{1,0:T(8,128)} %collective-permute-done.1.far, s32[8,128]{1,0:T(8,128)} %bitcast.29, ...), custom_call_target="tpu_custom_call" | custom-call | flops 3000000 | bytes 2000000 | tf_op jit(solution)/shard_map/pack_rims/pallas_call | solution.py:585
  27.1 1.3 %collective-permute-start.2 = (f32[160,128]{1,0:T(8,128)}, f32[160,128]{1,0:T(8,128)}, u32[]{:S(2)}, u32[]{:S(2)}) collective-permute-start(f32[160,128]{1,0:T(8,128)} %get-tuple-element.29), channel_id=1, source_target_pairs={{1,0},{2,1},{3,2},{4,3},{5,4},{6,5},{7,6},{8,7},{9,8},{10,9},{11,1... | collective-permute-start | bytes 245768 | tf_op jit(solution)/shard_map/ppermute | solution.py:496
  28.4 4.7 %collective-permute-start.3 = (f32[160,128]{1,0:T(8,128)}, f32[160,128]{1,0:T(8,128)}, u32[]{:S(2)}, u32[]{:S(2)}) collective-permute-start(f32[160,128]{1,0:T(8,128)} %get-tuple-element.30), channel_id=1, source_target_pairs={{0,1},{1,2},{2,3},{3,4},{4,5},{5,6},{6,7},{7,8},{8,9},{9,10},{10,1... | collective-permute-start | bytes 245768 | tf_op jit(solution)/shard_map/ppermute | solution.py:496
  33.1 11.8 %collective-permute-done.2.after_y = f32[160,128]{1,0:T(8,128)} collective-permute-done((f32[160,128]{1,0:T(8,128)}, f32[160,128]{1,0:T(8,128)}, u32[]{:S(2)}, u32[]{:S(2)}) %collective-permute-start.2) | collective-permute-done | bytes 81952 | tf_op jit(solution)/shard_map/ppermute | solution.py:496
  44.8 0.0 collective-permute-done.3.before_y
  44.8 3.7 %all-to-all-done = f32[128,1,3328]{2,1,0:T(1,128)} async-done(((f32[128,1,3328]{2,1,0:T(1,128)}), f32[128,1,3328]{2,1,0:T(1,128)}, u32[]{:S(2)}, u32[]{:S(2)}) %all-to-all-start) | async-done | bytes 1703968 | tf_op jit(solution)/shard_map/all_to_all | solution.py:479
  48.6 14.7 %step_nest.1 = (f32[2400,128]{1,0:T(8,128)}, f32[3328,128]{1,0:T(8,128)}) custom-call(f32[3328,128]{1,0:T(8,128)} %bitcast.6.moved, f32[2400,128]{1,0:T(8,128)} %bitcast.25, f32[24,128]{1,0:T(8,128)} %metric.4, f32[20]{0:T(128)} %buoyancy.3, s32[1024]{0:T(1024)} %picks.3, s32[1024]{0:T(1024)} %spots.3, s32[1024]{0:T(1024)} %bitcast.30), custom_call_target="tpu_custom_call" | custom-call | tf_op jit(solution)/shard_map/step_nest/pallas_call | solution.py:606
  63.2 6.6 %all-to-all-start.1 = ((f32[128,1,3328]{2,1,0:T(1,128)}), f32[128,1,3328]{2,1,0:T(1,128)}, u32[]{:S(2)}, u32[]{:S(2)}) async-start(f32[128,1,3328]{2,1,0:T(1,128)} %bitcast.23), calls=%async_computation.1 | async-start | bytes 3407872 | tf_op jit(solution)/shard_map/all_to_all | solution.py:479
  69.9 0.7 add_convert_fusion.edge
  70.5 9.8 %step_parent.1.parent = f32[3200,128]{1,0:T(8,128)} custom-call(s32[1]{0:T(128)} %bitcast.3.odd, s32[2]{0:T(128)} %add_convert_fusion.edge, f32[20]{0:T(128)} %buoyancy.3, f32[3200,128]{1,0:T(8,128)} %bitcast.21, f32[32,128]{1,0:T(8,128)} %metric.5, f32[404,128]{1,0:T(8,128)} %collective-permute-done.near, f32[404,128]{1,0:T(8,128)} %collective-permute-done.1.far, ...), custom_call_target="tpu_custom_call" | custom-call | flops 20000000 | bytes 8000000 | tf_op jit(solution)/shard_map/step_parent/pallas_call | solution.py:639
  80.3 14.7 %all-to-all-done.1 = f32[128,1,3328]{2,1,0:T(1,128)} async-done(((f32[128,1,3328]{2,1,0:T(1,128)}), f32[128,1,3328]{2,1,0:T(1,128)}, u32[]{:S(2)}, u32[]{:S(2)}) %all-to-all-start.1) | async-done | bytes 1703968 | tf_op jit(solution)/shard_map/all_to_all | solution.py:479
  95.0 12.9 %add_panels.1 = f32[100,32,128]{2,1,0:T(8,128)} custom-call(f32[3328,128]{1,0:T(8,128)} %bitcast.12.moved, f32[3200,128]{1,0:T(8,128)} %step_parent.1.parent), custom_call_target="tpu_custom_call" | custom-call | tf_op jit(solution)/shard_map/add_panels/pallas_call | solution.py:653
Async XLA Ops:
  2.6 10.6 %collective-permute-start = (f32[404,128]{1,0:T(8,128)}, f32[404,128]{1,0:T(8,128)}, u32[]{:S(2)}, u32[]{:S(2)}) collective-permute-start(f32[404,128]{1,0:T(8,128)} %get-tuple-element.20), channel_id=1, source_target_pairs={{0,16},{32,48},{64,80},{96,112},{16,0},{48,32},{80,64},{112,96},{1... | collective-permute-start | bytes 620552 | tf_op jit(solution)/shard_map/ppermute | solution.py:489
  4.0 9.2 %collective-permute-start.1 = (f32[404,128]{1,0:T(8,128)}, f32[404,128]{1,0:T(8,128)}, u32[]{:S(2)}, u32[]{:S(2)}) collective-permute-start(f32[404,128]{1,0:T(8,128)} %get-tuple-element.21), channel_id=1, source_target_pairs={{16,32},{48,64},{80,96},{32,16},{64,48},{96,80},{17,33},{49,65},{8... | collective-permute-start | bytes 620552 | tf_op jit(solution)/shard_map/ppermute | solution.py:489
  13.2 35.3 %all-to-all-start = ((f32[128,1,3328]{2,1,0:T(1,128)}), f32[128,1,3328]{2,1,0:T(1,128)}, u32[]{:S(2)}, u32[]{:S(2)}) async-start(f32[128,1,3328]{2,1,0:T(1,128)} %bitcast.22), calls=%async_computation | async-start | bytes 3407872 | tf_op jit(solution)/shard_map/all_to_all | solution.py:479
  27.1 17.7 %collective-permute-start.2 = (f32[160,128]{1,0:T(8,128)}, f32[160,128]{1,0:T(8,128)}, u32[]{:S(2)}, u32[]{:S(2)}) collective-permute-start(f32[160,128]{1,0:T(8,128)} %get-tuple-element.29), channel_id=1, source_target_pairs={{1,0},{2,1},{3,2},{4,3},{5,4},{6,5},{7,6},{8,7},{9,8},{10,9},{11,1... | collective-permute-start | bytes 245768 | tf_op jit(solution)/shard_map/ppermute | solution.py:496
  28.4 16.5 %collective-permute-start.3 = (f32[160,128]{1,0:T(8,128)}, f32[160,128]{1,0:T(8,128)}, u32[]{:S(2)}, u32[]{:S(2)}) collective-permute-start(f32[160,128]{1,0:T(8,128)} %get-tuple-element.30), channel_id=1, source_target_pairs={{0,1},{1,2},{2,3},{3,4},{4,5},{5,6},{6,7},{7,8},{8,9},{9,10},{10,1... | collective-permute-start | bytes 245768 | tf_op jit(solution)/shard_map/ppermute | solution.py:496
  63.2 31.8 %all-to-all-start.1 = ((f32[128,1,3328]{2,1,0:T(1,128)}), f32[128,1,3328]{2,1,0:T(1,128)}, u32[]{:S(2)}, u32[]{:S(2)}) async-start(f32[128,1,3328]{2,1,0:T(1,128)} %bitcast.23), calls=%async_computation.1 | async-start | bytes 3407872 | tf_op jit(solution)/shard_map/all_to_all | solution.py:479

commit v5 on v4

--- a/solution.py
+++ b/solution.py
@@ -22,7 +22,7 @@
 KEEP = 26
 REST = CAP - KEEP
 GROUP = 8
-STEP = 2
+STEP = 4
 MARGINS = (4, 8)
 VMEM_BYTES = 65500 * 1024
 
@@ -165,11 +165,12 @@
             mine = jnp.where(easts[t] == place, 1.0, 0.0).astype(jnp.bfloat16)
             parts.append((column * mine[None]).reshape(ROW, depth))
         where = pl.ds(pl.multiple_of(here * ROW, ROW), STEP * ROW)
-        sums[where, :] += jnp.dot(
+        both = jnp.dot(
             jnp.concatenate(parts, 0),
             weights[t * depth : (t + 1) * depth, :],
             preferred_element_type=jnp.float32,
         )
+        sums[where, :] += both[:, :ROW] + both[:, ROW:]
 
     low = [min(size_x, size_x // 2 + margin) for margin in MARGINS]
     widths = low + low[::-1]
@@ -209,7 +210,7 @@
 
 def relax(fields, sums, out, channels, size_x, i):
     block = slice(i * ROW, (i + 1) * ROW)
-    total = (sums[block, :ROW] + sums[block, ROW:]).T
+    total = sums[block, :].T
     share = 1.0 / (1.0 + total[TALLY : TALLY + 1])
     height = padded(channels)
     where = pl.ds(i, height, stride=size_x)
@@ -617,7 +618,7 @@
             index(pltpu.SMEM),
             index(pltpu.SMEM),
             pltpu.VMEM((padded(channels) * block_x, block_y), jnp.float32),
-            pltpu.VMEM((block_x * block_y, 2 * ROW), jnp.float32),
+            pltpu.VMEM((block_x * block_y, ROW), jnp.float32),
             pltpu.VMEM((block_x * block_y, ROW), jnp.float32),
             pltpu.VMEM((devices * CAP, ROW), jnp.float32),
         ]
@@ -659,7 +660,7 @@
             pltpu.VMEM(packed_shape, jnp.float32),
             pltpu.VMEM((padded(channels) * tile_x, tile_y), jnp.float32),
             pltpu.VMEM((padded(channels), tile_x, tile_y), jnp.float32),
-            pltpu.VMEM((tile_x * tile_y, 2 * ROW), jnp.float32),
+            pltpu.VMEM((tile_x * tile_y, ROW), jnp.float32),
         ]
         + add_scratch(devices)
         + [pltpu.SemaphoreType.DMA((1,)), pltpu.SemaphoreType.DMA((parts,))],

time: 108 us -> 107 us (level)
  Pallas kernels: 48.9 us -> 47.7 us
where the time goes in v5:
time: 107 us
  Pallas kernels  47.7 us (45%)
  waiting for transfers between devices  30.2 us (28%)
  starting transfers between devices  27.4 us (26%)
    all_to_all x2, waiting for transfers between devices, exchange(): lax.all_to_all(packed.reshape(devices, KEEP * ROW), ('gx', 'gy'), split_a...  18.4 us
    all_to_all x2, starting transfers between devices, exchange(): lax.all_to_all(packed.reshape(devices, KEEP * ROW), ('gx', 'gy'), split_a...  16.9 us
    pallas_call x1, Pallas kernels, on_device(): pl.pallas_call(functools.partial(nest_kernel, size_x=block_x), out_shape=...  14.1 us
    pallas_call x1, Pallas kernels, on_device(): pl.pallas_call(functools.partial(final_kernel, size_x=tile_x), out_shape=...  12.2 us
    ppermute x2, waiting for transfers between devices, shifted(): return (lax.ppermute(first, axis, down), lax.ppermute(last, axis, up))  11.8 us
    pallas_call x1, Pallas kernels, on_device(): pl.pallas_call(parent_kernel, out_shape=shape(*tile_shape), in_specs=[sme...  9.79 us
    pallas_call x1, Pallas kernels, on_device(): pl.pallas_call(functools.partial(strip_kernel, size_x=tile_x, cells=block...  6.02 us
    ppermute x2, starting transfers between devices, shifted(): return (lax.ppermute(first, axis, down), lax.ppermute(last, axis, up))  5.96 us
  transfers between devices with their start and end apart: 6, of which 3 were waited for; matrix products, arithmetic and copies ran while one was open for 1% of the time, Pallas kernels for 18%

profile of v5, /device:TPU:1, one launch (start us, length us, event | category | flops | bytes accessed | tf_op | source)
XLA Modules:
  0.0 106.8 jit_solution(11328097694334169615)
XLA Ops:
  0.6 2.0 %cut_rims.1 = (f32[404,128]{1,0:T(8,128)}, f32[404,128]{1,0:T(8,128)}) custom-call(s32[1]{0:T(128)} %bitcast.3.odd, f32[100,32,128]{2,1,0:T(8,128)} %bitcast.17, f32[100,32,128]{2,1,0:T(8,128)} %bitcast.18, f32[32,128]{1,0:T(8,128)} %metric.5), custom_call_target="tpu_custom_call" | custom-call | tf_op jit(solution)/shard_map/cut_rims/pallas_call | solution.py:539
  2.6 1.4 %collective-permute-start = (f32[404,128]{1,0:T(8,128)}, f32[404,128]{1,0:T(8,128)}, u32[]{:S(2)}, u32[]{:S(2)}) collective-permute-start(f32[404,128]{1,0:T(8,128)} %get-tuple-element.20), channel_id=1, source_target_pairs={{0,16},{32,48},{64,80},{96,112},{16,0},{48,32},{80,64},{112,96},{1... | collective-permute-start | bytes 620552 | tf_op jit(solution)/shard_map/ppermute | solution.py:490
  4.0 3.2 %collective-permute-start.1 = (f32[404,128]{1,0:T(8,128)}, f32[404,128]{1,0:T(8,128)}, u32[]{:S(2)}, u32[]{:S(2)}) collective-permute-start(f32[404,128]{1,0:T(8,128)} %get-tuple-element.21), channel_id=1, source_target_pairs={{16,32},{48,64},{80,96},{32,16},{64,48},{96,80},{17,33},{49,65},{8... | collective-permute-start | bytes 620552 | tf_op jit(solution)/shard_map/ppermute | solution.py:490
  7.2 6.0 %pack_strips.1 = f32[3328,128]{1,0:T(8,128)} custom-call(f32[3200,128]{1,0:T(8,128)} %bitcast.19, s32[8,128]{1,0:T(8,128)} %bitcast.28, s32[1024]{0:T(1024)} %picks.2, s32[1024]{0:T(1024)} %spots.2, s32[8,128]{1,0:T(8,128)} %bitcast.26), custom_call_target="tpu_custom_call" | custom-call | tf_op jit(solution)/shard_map/pack_strips/pallas_call | solution.py:549
  13.2 0.0 collective-permute-done.near
  13.2 0.0 collective-permute-done.1.far
  13.2 10.2 %all-to-all-start = ((f32[128,1,3328]{2,1,0:T(1,128)}), f32[128,1,3328]{2,1,0:T(1,128)}, u32[]{:S(2)}, u32[]{:S(2)}) async-start(f32[128,1,3328]{2,1,0:T(1,128)} %bitcast.22), calls=%async_computation | async-start | bytes 3407872 | tf_op jit(solution)/shard_map/all_to_all | solution.py:480
  23.5 3.6 %pack_rims.1 = (f32[160,128]{1,0:T(8,128)}, f32[160,128]{1,0:T(8,128)}, s32[8,128]{1,0:T(8,128)}) custom-call(s32[1]{0:T(128)} %bitcast.3.odd, f32[3200,128]{1,0:T(8,128)} %bitcast.20, f32[32,128]{1,0:T(8,128)} %metric.5, f32[404,128]{1,0:T(8,128)} %collective-permute-done.near, f32[404,128]{1,0:T(8,128)} %collective-permute-done.1.far, s32[8,128]{1,0:T(8,128)} %bitcast.29, ...), custom_call_target="tpu_custom_call" | custom-call | flops 3000000 | bytes 2000000 | tf_op jit(solution)/shard_map/pack_rims/pallas_call | solution.py:586
  27.1 1.3 %collective-permute-start.2 = (f32[160,128]{1,0:T(8,128)}, f32[160,128]{1,0:T(8,128)}, u32[]{:S(2)}, u32[]{:S(2)}) collective-permute-start(f32[160,128]{1,0:T(8,128)} %get-tuple-element.29), channel_id=1, source_target_pairs={{1,0},{2,1},{3,2},{4,3},{5,4},{6,5},{7,6},{8,7},{9,8},{10,9},{11,1... | collective-permute-start | bytes 245768 | tf_op jit(solution)/shard_map/ppermute | solution.py:497
  28.4 4.7 %collective-permute-start.3 = (f32[160,128]{1,0:T(8,128)}, f32[160,128]{1,0:T(8,128)}, u32[]{:S(2)}, u32[]{:S(2)}) collective-permute-start(f32[160,128]{1,0:T(8,128)} %get-tuple-element.30), channel_id=1, source_target_pairs={{0,1},{1,2},{2,3},{3,4},{4,5},{5,6},{6,7},{7,8},{8,9},{9,10},{10,1... | collective-permute-start | bytes 245768 | tf_op jit(solution)/shard_map/ppermute | solution.py:497
  33.1 11.8 %collective-permute-done.2.after_y = f32[160,128]{1,0:T(8,128)} collective-permute-done((f32[160,128]{1,0:T(8,128)}, f32[160,128]{1,0:T(8,128)}, u32[]{:S(2)}, u32[]{:S(2)}) %collective-permute-start.2) | collective-permute-done | bytes 81952 | tf_op jit(solution)/shard_map/ppermute | solution.py:497
  44.8 0.0 collective-permute-done.3.before_y
  44.8 3.7 %all-to-all-done = f32[128,1,3328]{2,1,0:T(1,128)} async-done(((f32[128,1,3328]{2,1,0:T(1,128)}), f32[128,1,3328]{2,1,0:T(1,128)}, u32[]{:S(2)}, u32[]{:S(2)}) %all-to-all-start) | async-done | bytes 1703968 | tf_op jit(solution)/shard_map/all_to_all | solution.py:480
  48.6 14.1 %step_nest.1 = (f32[2400,128]{1,0:T(8,128)}, f32[3328,128]{1,0:T(8,128)}) custom-call(f32[3328,128]{1,0:T(8,128)} %bitcast.6.moved, f32[2400,128]{1,0:T(8,128)} %bitcast.25, f32[24,128]{1,0:T(8,128)} %metric.4, f32[20]{0:T(128)} %buoyancy.3, s32[1024]{0:T(1024)} %picks.3, s32[1024]{0:T(1024)} %spots.3, s32[1024]{0:T(1024)} %bitcast.30), custom_call_target="tpu_custom_call" | custom-call | tf_op jit(solution)/shard_map/step_nest/pallas_call | solution.py:607
  62.7 6.6 %all-to-all-start.1 = ((f32[128,1,3328]{2,1,0:T(1,128)}), f32[128,1,3328]{2,1,0:T(1,128)}, u32[]{:S(2)}, u32[]{:S(2)}) async-start(f32[128,1,3328]{2,1,0:T(1,128)} %bitcast.23), calls=%async_computation.1 | async-start | bytes 3407872 | tf_op jit(solution)/shard_map/all_to_all | solution.py:480
  69.3 0.7 add_convert_fusion.edge
  70.0 9.8 %step_parent.1.parent = f32[3200,128]{1,0:T(8,128)} custom-call(s32[1]{0:T(128)} %bitcast.3.odd, s32[2]{0:T(128)} %add_convert_fusion.edge, f32[20]{0:T(128)} %buoyancy.3, f32[3200,128]{1,0:T(8,128)} %bitcast.21, f32[32,128]{1,0:T(8,128)} %metric.5, f32[404,128]{1,0:T(8,128)} %collective-permute-done.near, f32[404,128]{1,0:T(8,128)} %collective-permute-done.1.far, ...), custom_call_target="tpu_custom_call" | custom-call | flops 20000000 | bytes 8000000 | tf_op jit(solution)/shard_map/step_parent/pallas_call | solution.py:640
  79.7 14.7 %all-to-all-done.1 = f32[128,1,3328]{2,1,0:T(1,128)} async-done(((f32[128,1,3328]{2,1,0:T(1,128)}), f32[128,1,3328]{2,1,0:T(1,128)}, u32[]{:S(2)}, u32[]{:S(2)}) %all-to-all-start.1) | async-done | bytes 1703968 | tf_op jit(solution)/shard_map/all_to_all | solution.py:480
  94.4 12.2 %add_panels.1 = f32[100,32,128]{2,1,0:T(8,128)} custom-call(f32[3328,128]{1,0:T(8,128)} %bitcast.12.moved, f32[3200,128]{1,0:T(8,128)} %step_parent.1.parent), custom_call_target="tpu_custom_call" | custom-call | tf_op jit(solution)/shard_map/add_panels/pallas_call | solution.py:654
Async XLA Ops:
  2.6 10.6 %collective-permute-start = (f32[404,128]{1,0:T(8,128)}, f32[404,128]{1,0:T(8,128)}, u32[]{:S(2)}, u32[]{:S(2)}) collective-permute-start(f32[404,128]{1,0:T(8,128)} %get-tuple-element.20), channel_id=1, source_target_pairs={{0,16},{32,48},{64,80},{96,112},{16,0},{48,32},{80,64},{112,96},{1... | collective-permute-start | bytes 620552 | tf_op jit(solution)/shard_map/ppermute | solution.py:490
  4.0 9.2 %collective-permute-start.1 = (f32[404,128]{1,0:T(8,128)}, f32[404,128]{1,0:T(8,128)}, u32[]{:S(2)}, u32[]{:S(2)}) collective-permute-start(f32[404,128]{1,0:T(8,128)} %get-tuple-element.21), channel_id=1, source_target_pairs={{16,32},{48,64},{80,96},{32,16},{64,48},{96,80},{17,33},{49,65},{8... | collective-permute-start | bytes 620552 | tf_op jit(solution)/shard_map/ppermute | solution.py:490
  13.2 35.3 %all-to-all-start = ((f32[128,1,3328]{2,1,0:T(1,128)}), f32[128,1,3328]{2,1,0:T(1,128)}, u32[]{:S(2)}, u32[]{:S(2)}) async-start(f32[128,1,3328]{2,1,0:T(1,128)} %bitcast.22), calls=%async_computation | async-start | bytes 3407872 | tf_op jit(solution)/shard_map/all_to_all | solution.py:480
  27.1 17.7 %collective-permute-start.2 = (f32[160,128]{1,0:T(8,128)}, f32[160,128]{1,0:T(8,128)}, u32[]{:S(2)}, u32[]{:S(2)}) collective-permute-start(f32[160,128]{1,0:T(8,128)} %get-tuple-element.29), channel_id=1, source_target_pairs={{1,0},{2,1},{3,2},{4,3},{5,4},{6,5},{7,6},{8,7},{9,8},{10,9},{11,1... | collective-permute-start | bytes 245768 | tf_op jit(solution)/shard_map/ppermute | solution.py:497
  28.4 16.5 %collective-permute-start.3 = (f32[160,128]{1,0:T(8,128)}, f32[160,128]{1,0:T(8,128)}, u32[]{:S(2)}, u32[]{:S(2)}) collective-permute-start(f32[160,128]{1,0:T(8,128)} %get-tuple-element.30), channel_id=1, source_target_pairs={{0,1},{1,2},{2,3},{3,4},{4,5},{5,6},{6,7},{7,8},{8,9},{9,10},{10,1... | collective-permute-start | bytes 245768 | tf_op jit(solution)/shard_map/ppermute | solution.py:497
  62.7 31.8 %all-to-all-start.1 = ((f32[128,1,3328]{2,1,0:T(1,128)}), f32[128,1,3328]{2,1,0:T(1,128)}, u32[]{:S(2)}, u32[]{:S(2)}) async-start(f32[128,1,3328]{2,1,0:T(1,128)} %bitcast.23), calls=%async_computation.1 | async-start | bytes 3407872 | tf_op jit(solution)/shard_map/all_to_all | solution.py:480

commit v6 on v5

--- a/solution.py
+++ b/solution.py
@@ -519,7 +519,7 @@
     tile_shape = (channels * tile_x, tile_y)
     block_shape = (channels * block_x, block_y)
     packed_shape = (devices * KEEP, ROW)
-    parts = 4
+    parts = 2
 
     def shape(*dims, dtype=jnp.float32):
         return jax.ShapeDtypeStruct(dims, dtype)

time: 107 us -> 107 us (level)
  no operation moved by 1% of the time
where the time goes in v6:
time: 107 us
  Pallas kernels  47.6 us (44%)
  waiting for transfers between devices  30.2 us (28%)
  starting transfers between devices  27.4 us (26%)
    all_to_all x2, waiting for transfers between devices, exchange(): lax.all_to_all(packed.reshape(devices, KEEP * ROW), ('gx', 'gy'), split_a...  18.4 us
    all_to_all x2, starting transfers between devices, exchange(): lax.all_to_all(packed.reshape(devices, KEEP * ROW), ('gx', 'gy'), split_a...  16.9 us
    pallas_call x1, Pallas kernels, on_device(): pl.pallas_call(functools.partial(nest_kernel, size_x=block_x), out_shape=...  14 us
    pallas_call x1, Pallas kernels, on_device(): pl.pallas_call(functools.partial(final_kernel, size_x=tile_x), out_shape=...  12.2 us
    ppermute x2, waiting for transfers between devices, shifted(): return (lax.ppermute(first, axis, down), lax.ppermute(last, axis, up))  11.8 us
    pallas_call x1, Pallas kernels, on_device(): pl.pallas_call(parent_kernel, out_shape=shape(*tile_shape), in_specs=[sme...  9.79 us
    pallas_call x1, Pallas kernels, on_device(): pl.pallas_call(functools.partial(strip_kernel, size_x=tile_x, cells=block...  5.97 us
    ppermute x2, starting transfers between devices, shifted(): return (lax.ppermute(first, axis, down), lax.ppermute(last, axis, up))  5.96 us
  transfers between devices with their start and end apart: 6, of which 3 were waited for; matrix products, arithmetic and copies ran while one was open for 1% of the time, Pallas kernels for 18%

profile of v6, /device:TPU:1, one launch (start us, length us, event | category | flops | bytes accessed | tf_op | source)
XLA Modules:
  0.0 106.7 jit_solution(1734710959082779286)
XLA Ops:
  0.6 2.0 %cut_rims.1 = (f32[404,128]{1,0:T(8,128)}, f32[404,128]{1,0:T(8,128)}) custom-call(s32[1]{0:T(128)} %bitcast.3.odd, f32[100,32,128]{2,1,0:T(8,128)} %bitcast.17, f32[100,32,128]{2,1,0:T(8,128)} %bitcast.18, f32[32,128]{1,0:T(8,128)} %metric.5), custom_call_target="tpu_custom_call" | custom-call | tf_op jit(solution)/shard_map/cut_rims/pallas_call | solution.py:539
  2.6 1.4 %collective-permute-start = (f32[404,128]{1,0:T(8,128)}, f32[404,128]{1,0:T(8,128)}, u32[]{:S(2)}, u32[]{:S(2)}) collective-permute-start(f32[404,128]{1,0:T(8,128)} %get-tuple-element.20), channel_id=1, source_target_pairs={{0,16},{32,48},{64,80},{96,112},{16,0},{48,32},{80,64},{112,96},{1... | collective-permute-start | bytes 620552 | tf_op jit(solution)/shard_map/ppermute | solution.py:490
  4.0 3.2 %collective-permute-start.1 = (f32[404,128]{1,0:T(8,128)}, f32[404,128]{1,0:T(8,128)}, u32[]{:S(2)}, u32[]{:S(2)}) collective-permute-start(f32[404,128]{1,0:T(8,128)} %get-tuple-element.21), channel_id=1, source_target_pairs={{16,32},{48,64},{80,96},{32,16},{64,48},{96,80},{17,33},{49,65},{8... | collective-permute-start | bytes 620552 | tf_op jit(solution)/shard_map/ppermute | solution.py:490
  7.2 6.0 %pack_strips.1 = f32[3328,128]{1,0:T(8,128)} custom-call(f32[3200,128]{1,0:T(8,128)} %bitcast.19, s32[8,128]{1,0:T(8,128)} %bitcast.28, s32[1024]{0:T(1024)} %picks.2, s32[1024]{0:T(1024)} %spots.2, s32[8,128]{1,0:T(8,128)} %bitcast.26), custom_call_target="tpu_custom_call" | custom-call | tf_op jit(solution)/shard_map/pack_strips/pallas_call | solution.py:549
  13.2 0.0 collective-permute-done.near
  13.2 0.0 collective-permute-done.1.far
  13.2 10.2 %all-to-all-start = ((f32[128,1,3328]{2,1,0:T(1,128)}), f32[128,1,3328]{2,1,0:T(1,128)}, u32[]{:S(2)}, u32[]{:S(2)}) async-start(f32[128,1,3328]{2,1,0:T(1,128)} %bitcast.22), calls=%async_computation | async-start | bytes 3407872 | tf_op jit(solution)/shard_map/all_to_all | solution.py:480
  23.4 3.6 %pack_rims.1 = (f32[160,128]{1,0:T(8,128)}, f32[160,128]{1,0:T(8,128)}, s32[8,128]{1,0:T(8,128)}) custom-call(s32[1]{0:T(128)} %bitcast.3.odd, f32[3200,128]{1,0:T(8,128)} %bitcast.20, f32[32,128]{1,0:T(8,128)} %metric.5, f32[404,128]{1,0:T(8,128)} %collective-permute-done.near, f32[404,128]{1,0:T(8,128)} %collective-permute-done.1.far, s32[8,128]{1,0:T(8,128)} %bitcast.29, ...), custom_call_target="tpu_custom_call" | custom-call | flops 3000000 | bytes 2000000 | tf_op jit(solution)/shard_map/pack_rims/pallas_call | solution.py:586
  27.0 1.3 %collective-permute-start.2 = (f32[160,128]{1,0:T(8,128)}, f32[160,128]{1,0:T(8,128)}, u32[]{:S(2)}, u32[]{:S(2)}) collective-permute-start(f32[160,128]{1,0:T(8,128)} %get-tuple-element.29), channel_id=1, source_target_pairs={{1,0},{2,1},{3,2},{4,3},{5,4},{6,5},{7,6},{8,7},{9,8},{10,9},{11,1... | collective-permute-start | bytes 245768 | tf_op jit(solution)/shard_map/ppermute | solution.py:497
  28.3 4.7 %collective-permute-start.3 = (f32[160,128]{1,0:T(8,128)}, f32[160,128]{1,0:T(8,128)}, u32[]{:S(2)}, u32[]{:S(2)}) collective-permute-start(f32[160,128]{1,0:T(8,128)} %get-tuple-element.30), channel_id=1, source_target_pairs={{0,1},{1,2},{2,3},{3,4},{4,5},{5,6},{6,7},{7,8},{8,9},{9,10},{10,1... | collective-permute-start | bytes 245768 | tf_op jit(solution)/shard_map/ppermute | solution.py:497
  33.0 11.8 %collective-permute-done.2.after_y = f32[160,128]{1,0:T(8,128)} collective-permute-done((f32[160,128]{1,0:T(8,128)}, f32[160,128]{1,0:T(8,128)}, u32[]{:S(2)}, u32[]{:S(2)}) %collective-permute-start.2) | collective-permute-done | bytes 81952 | tf_op jit(solution)/shard_map/ppermute | solution.py:497
  44.8 0.0 collective-permute-done.3.before_y
  44.8 3.7 %all-to-all-done = f32[128,1,3328]{2,1,0:T(1,128)} async-done(((f32[128,1,3328]{2,1,0:T(1,128)}), f32[128,1,3328]{2,1,0:T(1,128)}, u32[]{:S(2)}, u32[]{:S(2)}) %all-to-all-start) | async-done | bytes 1703968 | tf_op jit(solution)/shard_map/all_to_all | solution.py:480
  48.5 14.0 %step_nest.1 = (f32[2400,128]{1,0:T(8,128)}, f32[3328,128]{1,0:T(8,128)}) custom-call(f32[3328,128]{1,0:T(8,128)} %bitcast.6.moved, f32[2400,128]{1,0:T(8,128)} %bitcast.25, f32[24,128]{1,0:T(8,128)} %metric.4, f32[20]{0:T(128)} %buoyancy.3, s32[1024]{0:T(1024)} %picks.3, s32[1024]{0:T(1024)} %spots.3, s32[1024]{0:T(1024)} %bitcast.30), custom_call_target="tpu_custom_call" | custom-call | tf_op jit(solution)/shard_map/step_nest/pallas_call | solution.py:607
  62.6 6.6 %all-to-all-start.1 = ((f32[128,1,3328]{2,1,0:T(1,128)}), f32[128,1,3328]{2,1,0:T(1,128)}, u32[]{:S(2)}, u32[]{:S(2)}) async-start(f32[128,1,3328]{2,1,0:T(1,128)} %bitcast.23), calls=%async_computation.1 | async-start | bytes 3407872 | tf_op jit(solution)/shard_map/all_to_all | solution.py:480
  69.2 0.7 add_convert_fusion.edge
  69.9 9.8 %step_parent.1.parent = f32[3200,128]{1,0:T(8,128)} custom-call(s32[1]{0:T(128)} %bitcast.3.odd, s32[2]{0:T(128)} %add_convert_fusion.edge, f32[20]{0:T(128)} %buoyancy.3, f32[3200,128]{1,0:T(8,128)} %bitcast.21, f32[32,128]{1,0:T(8,128)} %metric.5, f32[404,128]{1,0:T(8,128)} %collective-permute-done.near, f32[404,128]{1,0:T(8,128)} %collective-permute-done.1.far, ...), custom_call_target="tpu_custom_call" | custom-call | flops 20000000 | bytes 8000000 | tf_op jit(solution)/shard_map/step_parent/pallas_call | solution.py:640
  79.7 14.7 %all-to-all-done.1 = f32[128,1,3328]{2,1,0:T(1,128)} async-done(((f32[128,1,3328]{2,1,0:T(1,128)}), f32[128,1,3328]{2,1,0:T(1,128)}, u32[]{:S(2)}, u32[]{:S(2)}) %all-to-all-start.1) | async-done | bytes 1703968 | tf_op jit(solution)/shard_map/all_to_all | solution.py:480
  94.3 12.2 %add_panels.1 = f32[100,32,128]{2,1,0:T(8,128)} custom-call(f32[3328,128]{1,0:T(8,128)} %bitcast.12.moved, f32[3200,128]{1,0:T(8,128)} %step_parent.1.parent), custom_call_target="tpu_custom_call" | custom-call | tf_op jit(solution)/shard_map/add_panels/pallas_call | solution.py:654
Async XLA Ops:
  2.6 10.6 %collective-permute-start = (f32[404,128]{1,0:T(8,128)}, f32[404,128]{1,0:T(8,128)}, u32[]{:S(2)}, u32[]{:S(2)}) collective-permute-start(f32[404,128]{1,0:T(8,128)} %get-tuple-element.20), channel_id=1, source_target_pairs={{0,16},{32,48},{64,80},{96,112},{16,0},{48,32},{80,64},{112,96},{1... | collective-permute-start | bytes 620552 | tf_op jit(solution)/shard_map/ppermute | solution.py:490
  4.0 9.2 %collective-permute-start.1 = (f32[404,128]{1,0:T(8,128)}, f32[404,128]{1,0:T(8,128)}, u32[]{:S(2)}, u32[]{:S(2)}) collective-permute-start(f32[404,128]{1,0:T(8,128)} %get-tuple-element.21), channel_id=1, source_target_pairs={{16,32},{48,64},{80,96},{32,16},{64,48},{96,80},{17,33},{49,65},{8... | collective-permute-start | bytes 620552 | tf_op jit(solution)/shard_map/ppermute | solution.py:490
  13.2 35.3 %all-to-all-start = ((f32[128,1,3328]{2,1,0:T(1,128)}), f32[128,1,3328]{2,1,0:T(1,128)}, u32[]{:S(2)}, u32[]{:S(2)}) async-start(f32[128,1,3328]{2,1,0:T(1,128)} %bitcast.22), calls=%async_computation | async-start | bytes 3407872 | tf_op jit(solution)/shard_map/all_to_all | solution.py:480
  27.0 17.7 %collective-permute-start.2 = (f32[160,128]{1,0:T(8,128)}, f32[160,128]{1,0:T(8,128)}, u32[]{:S(2)}, u32[]{:S(2)}) collective-permute-start(f32[160,128]{1,0:T(8,128)} %get-tuple-element.29), channel_id=1, source_target_pairs={{1,0},{2,1},{3,2},{4,3},{5,4},{6,5},{7,6},{8,7},{9,8},{10,9},{11,1... | collective-permute-start | bytes 245768 | tf_op jit(solution)/shard_map/ppermute | solution.py:497
  28.3 16.5 %collective-permute-start.3 = (f32[160,128]{1,0:T(8,128)}, f32[160,128]{1,0:T(8,128)}, u32[]{:S(2)}, u32[]{:S(2)}) collective-permute-start(f32[160,128]{1,0:T(8,128)} %get-tuple-element.30), channel_id=1, source_target_pairs={{0,1},{1,2},{2,3},{3,4},{4,5},{5,6},{6,7},{7,8},{8,9},{9,10},{10,1... | collective-permute-start | bytes 245768 | tf_op jit(solution)/shard_map/ppermute | solution.py:497
  62.6 31.8 %all-to-all-start.1 = ((f32[128,1,3328]{2,1,0:T(1,128)}), f32[128,1,3328]{2,1,0:T(1,128)}, u32[]{:S(2)}, u32[]{:S(2)}) async-start(f32[128,1,3328]{2,1,0:T(1,128)} %bitcast.23), calls=%async_computation.1 | async-start | bytes 3407872 | tf_op jit(solution)/shard_map/all_to_all | solution.py:480

commit v7 on v5

--- a/solution.py
+++ b/solution.py
@@ -72,12 +72,18 @@
     staged[...] = jnp.broadcast_to(jnp.where(lane == SPOT, -1.0, 0.0), staged.shape)
 
 
+def spread_spots(spots, table):
+    for a in range(spots.shape[0]):
+        row = spots[a : a + 1, :].astype(jnp.float32)
+        table[a * ROW : (a + 1) * ROW, :] = jnp.broadcast_to(row, (ROW, ROW)).T
+
+
 def pack_rows(rows, picks, spots, slots, staged, packed, sems):
     lane = lax.broadcasted_iota(jnp.int32, (1, ROW), 1)
     devices = packed.shape[0] // KEEP
 
     def move(r, carry):
-        spot = jnp.full((1, ROW), spots[r], jnp.int32).astype(jnp.float32)
+        spot = spots[pl.ds(r, 1), :]
         row = rows[pl.ds(picks[r], 1), :]
         staged[pl.ds(slots[r], 1), :] = jnp.where(lane == SPOT, spot, row)
         return carry
@@ -268,13 +274,13 @@
 
 
 def strip_kernel(
-    parent, dest, picks, spots, spot_rows, packed,
-    tile, dest_v, picks_s, spots_s, spots_v, rows, staged, slots_v, slots, sems, slot_sems, out_sems,
+    parent, dest, picks, spots, packed,
+    tile, dest_v, picks_s, table, spots_v, rows, staged, slots_v, slots, sems, slot_sems, out_sems,
     *, size_x, cells
 ):
     channels = parent.shape[0] // size_x
     copies = fetch(
-        [(dest, dest_v), (spot_rows, spots_v), (picks, picks_s), (spots, spots_s)], sems
+        [(dest, dest_v), (spots, spots_v), (picks, picks_s)], sems
     )
     arrivals = fetch(split(parent, tile, out_sems.shape[0]), out_sems)
     clear_rows(staged)
@@ -284,30 +290,35 @@
     moves = fetch(
         [(slots_v.at[a], slots.at[pl.ds(a * ROW, ROW)]) for a in range(slots_v.shape[0])], slot_sems
     )
+    spread_spots(spots_v, table)
     for copy in arrivals:
         copy.wait()
     to_rows(tile, rows, channels, size_x)
     for copy in copies[2:] + moves:
         copy.wait()
-    for copy in pack_rows(rows, picks_s, spots_s, slots, staged, packed, out_sems):
+    for copy in pack_rows(rows, picks_s, table, slots, staged, packed, out_sems):
         copy.wait()
 
 
 def nest_kernel(
     moved, nest, metric, buoyancy, picks, spots, slots, out, packed,
-    came, tile, metric_v, buoyancy_s, picks_s, spots_s, slots_s, state, sums, rows, staged,
+    came, tile, metric_v, buoyancy_s, picks_s, spots_v, table, slots_s, state, sums, rows, staged,
     weights, columns, easts, sems, out_sems,
     *, size_x
 ):
     channels = nest.shape[0] // size_x
+    early = pltpu.make_async_copy(spots, spots_v, sems.at[5])
+    early.start()
     arrivals = fetch(split(moved, came, out_sems.shape[0]), out_sems)
     copies = planned(
         [(nest, tile.at[pl.ds(0, nest.shape[0])]), (metric, metric_v), (buoyancy, buoyancy_s)]
-        + [(picks, picks_s), (spots, spots_s), (slots, slots_s)],
+        + [(picks, picks_s), (slots, slots_s)],
         sems,
     )
     sums[...] = jnp.zeros(sums.shape, jnp.float32)
     clear_rows(staged)
+    early.wait()
+    spread_spots(spots_v, table)
     add_rows(came, arrivals, copies, sums, weights, columns, easts, size_x)
     for copy in copies:
         copy.wait()
@@ -322,7 +333,7 @@
     result = pltpu.make_async_copy(state.at[pl.ds(0, out.shape[0])], out, sems.at[0])
     result.start()
     to_rows(state, rows, channels, size_x)
-    for copy in pack_rows(rows, picks_s, spots_s, slots_s, staged, packed, out_sems):
+    for copy in pack_rows(rows, picks_s, table, slots_s, staged, packed, out_sems):
         copy.wait()
     result.wait()
 
@@ -549,13 +560,13 @@
     packed = pl.pallas_call(
         functools.partial(strip_kernel, size_x=tile_x, cells=block_x * block_y),
         out_shape=shape(*packed_shape),
-        in_specs=[anywhere()] * 5,
+        in_specs=[anywhere()] * 4,
         out_specs=anywhere(),
         scratch_shapes=[
             pltpu.VMEM((padded(channels) * tile_x, tile_y), jnp.float32),
             listed,
             index(pltpu.SMEM),
-            index(pltpu.SMEM),
+            pltpu.VMEM((slots, ROW), jnp.float32),
             listed,
             pltpu.VMEM((tile_x * tile_y, ROW), jnp.float32),
             pltpu.VMEM((devices * CAP, ROW), jnp.float32),
@@ -571,7 +582,6 @@
         parent.reshape(tile_shape),
         strip_dest.reshape(groups, ROW),
         strip_col,
-        strip_pos,
         strip_pos.reshape(groups, ROW),
     )
 
@@ -615,7 +625,8 @@
             pltpu.VMEM((block_x, block_y), jnp.float32),
             pltpu.SMEM(buoyancy.shape, jnp.float32),
             index(pltpu.SMEM),
-            index(pltpu.SMEM),
+            listed,
+            pltpu.VMEM((slots, ROW), jnp.float32),
             index(pltpu.SMEM),
             pltpu.VMEM((padded(channels) * block_x, block_y), jnp.float32),
             pltpu.VMEM((block_x * block_y, ROW), jnp.float32),
@@ -632,7 +643,7 @@
         nest_metric,
         buoyancy,
         panel_src,
-        panel_col,
+        panel_col.reshape(groups, ROW),
         panel_slots.reshape(slots),
     )
     moved = exchange(packed, devices)

time: 107 us -> 107 us (level)
  no operation moved by 1% of the time
where the time goes in v7:
time: 107 us
  Pallas kernels  47.5 us (44%)
  waiting for transfers between devices  30.2 us (28%)
  starting transfers between devices  27.4 us (26%)
    all_to_all x2, waiting for transfers between devices, exchange(): lax.all_to_all(packed.reshape(devices, KEEP * ROW), ('gx', 'gy'), split_a...  18.4 us
    all_to_all x2, starting transfers between devices, exchange(): lax.all_to_all(packed.reshape(devices, KEEP * ROW), ('gx', 'gy'), split_a...  16.9 us
    pallas_call x1, Pallas kernels, on_device(): pl.pallas_call(functools.partial(nest_kernel, size_x=block_x), out_shape=...  14 us
    pallas_call x1, Pallas kernels, on_device(): pl.pallas_call(functools.partial(final_kernel, size_x=tile_x), out_shape=...  12.2 us
    ppermute x2, waiting for transfers between devices, shifted(): return (lax.ppermute(first, axis, down), lax.ppermute(last, axis, up))  11.8 us
    pallas_call x1, Pallas kernels, on_device(): pl.pallas_call(parent_kernel, out_shape=shape(*tile_shape), in_specs=[sme...  9.79 us
    ppermute x2, starting transfers between devices, shifted(): return (lax.ppermute(first, axis, down), lax.ppermute(last, axis, up))  5.96 us
    pallas_call x1, Pallas kernels, on_device(): pl.pallas_call(functools.partial(strip_kernel, size_x=tile_x, cells=block...  5.89 us
  transfers between devices with their start and end apart: 6, of which 3 were waited for; matrix products, arithmetic and copies ran while one was open for 1% of the time, Pallas kernels for 18%

profile of v7, /device:TPU:1, one launch (start us, length us, event | category | flops | bytes accessed | tf_op | source)
XLA Modules:
  0.0 106.6 jit_solution(18177055874192282063)
XLA Ops:
  0.6 2.0 %cut_rims.1 = (f32[404,128]{1,0:T(8,128)}, f32[404,128]{1,0:T(8,128)}) custom-call(s32[1]{0:T(128)} %bitcast.3.odd, f32[100,32,128]{2,1,0:T(8,128)} %bitcast.18, f32[100,32,128]{2,1,0:T(8,128)} %bitcast.19, f32[32,128]{1,0:T(8,128)} %metric.5), custom_call_target="tpu_custom_call" | custom-call | tf_op jit(solution)/shard_map/cut_rims/pallas_call | solution.py:550
  2.6 1.4 %collective-permute-start = (f32[404,128]{1,0:T(8,128)}, f32[404,128]{1,0:T(8,128)}, u32[]{:S(2)}, u32[]{:S(2)}) collective-permute-start(f32[404,128]{1,0:T(8,128)} %get-tuple-element.20), channel_id=1, source_target_pairs={{0,16},{32,48},{64,80},{96,112},{16,0},{48,32},{80,64},{112,96},{1... | collective-permute-start | bytes 620552 | tf_op jit(solution)/shard_map/ppermute | solution.py:501
  4.0 3.2 %collective-permute-start.1 = (f32[404,128]{1,0:T(8,128)}, f32[404,128]{1,0:T(8,128)}, u32[]{:S(2)}, u32[]{:S(2)}) collective-permute-start(f32[404,128]{1,0:T(8,128)} %get-tuple-element.21), channel_id=1, source_target_pairs={{16,32},{48,64},{80,96},{32,16},{64,48},{96,80},{17,33},{49,65},{8... | collective-permute-start | bytes 620552 | tf_op jit(solution)/shard_map/ppermute | solution.py:501
  7.2 5.9 %pack_strips.1 = f32[3328,128]{1,0:T(8,128)} custom-call(f32[3200,128]{1,0:T(8,128)} %bitcast.20, s32[8,128]{1,0:T(8,128)} %bitcast.29, s32[1024]{0:T(1024)} %picks.2, s32[8,128]{1,0:T(8,128)} %bitcast.30), custom_call_target="tpu_custom_call" | custom-call | tf_op jit(solution)/shard_map/pack_strips/pallas_call | solution.py:560
  13.1 0.0 collective-permute-done.near
  13.1 0.0 collective-permute-done.1.far
  13.1 10.2 %all-to-all-start = ((f32[128,1,3328]{2,1,0:T(1,128)}), f32[128,1,3328]{2,1,0:T(1,128)}, u32[]{:S(2)}, u32[]{:S(2)}) async-start(f32[128,1,3328]{2,1,0:T(1,128)} %bitcast.23), calls=%async_computation | async-start | bytes 3407872 | tf_op jit(solution)/shard_map/all_to_all | solution.py:491
  23.3 3.6 %pack_rims.1 = (f32[160,128]{1,0:T(8,128)}, f32[160,128]{1,0:T(8,128)}, s32[8,128]{1,0:T(8,128)}) custom-call(s32[1]{0:T(128)} %bitcast.3.odd, f32[3200,128]{1,0:T(8,128)} %bitcast.21, f32[32,128]{1,0:T(8,128)} %metric.5, f32[404,128]{1,0:T(8,128)} %collective-permute-done.near, f32[404,128]{1,0:T(8,128)} %collective-permute-done.1.far, s32[8,128]{1,0:T(8,128)} %bitcast.31, ...), custom_call_target="tpu_custom_call" | custom-call | flops 3000000 | bytes 2000000 | tf_op jit(solution)/shard_map/pack_rims/pallas_call | solution.py:596
  27.0 1.3 %collective-permute-start.2 = (f32[160,128]{1,0:T(8,128)}, f32[160,128]{1,0:T(8,128)}, u32[]{:S(2)}, u32[]{:S(2)}) collective-permute-start(f32[160,128]{1,0:T(8,128)} %get-tuple-element.29), channel_id=1, source_target_pairs={{1,0},{2,1},{3,2},{4,3},{5,4},{6,5},{7,6},{8,7},{9,8},{10,9},{11,1... | collective-permute-start | bytes 245768 | tf_op jit(solution)/shard_map/ppermute | solution.py:508
  28.2 4.7 %collective-permute-start.3 = (f32[160,128]{1,0:T(8,128)}, f32[160,128]{1,0:T(8,128)}, u32[]{:S(2)}, u32[]{:S(2)}) collective-permute-start(f32[160,128]{1,0:T(8,128)} %get-tuple-element.30), channel_id=1, source_target_pairs={{0,1},{1,2},{2,3},{3,4},{4,5},{5,6},{6,7},{7,8},{8,9},{9,10},{10,1... | collective-permute-start | bytes 245768 | tf_op jit(solution)/shard_map/ppermute | solution.py:508
  32.9 11.8 %collective-permute-done.2.after_y = f32[160,128]{1,0:T(8,128)} collective-permute-done((f32[160,128]{1,0:T(8,128)}, f32[160,128]{1,0:T(8,128)}, u32[]{:S(2)}, u32[]{:S(2)}) %collective-permute-start.2) | collective-permute-done | bytes 81952 | tf_op jit(solution)/shard_map/ppermute | solution.py:508
  44.7 0.0 collective-permute-done.3.before_y
  44.7 3.7 %all-to-all-done = f32[128,1,3328]{2,1,0:T(1,128)} async-done(((f32[128,1,3328]{2,1,0:T(1,128)}), f32[128,1,3328]{2,1,0:T(1,128)}, u32[]{:S(2)}, u32[]{:S(2)}) %all-to-all-start) | async-done | bytes 1703968 | tf_op jit(solution)/shard_map/all_to_all | solution.py:491
  48.5 14.0 %step_nest.1 = (f32[2400,128]{1,0:T(8,128)}, f32[3328,128]{1,0:T(8,128)}) custom-call(f32[3328,128]{1,0:T(8,128)} %bitcast.6.moved, f32[2400,128]{1,0:T(8,128)} %bitcast.26, f32[24,128]{1,0:T(8,128)} %metric.4, f32[20]{0:T(128)} %buoyancy.3, s32[1024]{0:T(1024)} %picks.3, s32[8,128]{1,0:T(8,128)} %bitcast.28, s32[1024]{0:T(1024)} %bitcast.32), custom_call_target="tpu_custom_call" | custom-call | tf_op jit(solution)/shard_map/step_nest/pallas_call | solution.py:617
  62.5 6.6 %all-to-all-start.1 = ((f32[128,1,3328]{2,1,0:T(1,128)}), f32[128,1,3328]{2,1,0:T(1,128)}, u32[]{:S(2)}, u32[]{:S(2)}) async-start(f32[128,1,3328]{2,1,0:T(1,128)} %bitcast.24), calls=%async_computation.1 | async-start | bytes 3407872 | tf_op jit(solution)/shard_map/all_to_all | solution.py:491
  69.1 0.7 add_convert_fusion.edge
  69.8 9.8 %step_parent.1.parent = f32[3200,128]{1,0:T(8,128)} custom-call(s32[1]{0:T(128)} %bitcast.3.odd, s32[2]{0:T(128)} %add_convert_fusion.edge, f32[20]{0:T(128)} %buoyancy.3, f32[3200,128]{1,0:T(8,128)} %bitcast.22, f32[32,128]{1,0:T(8,128)} %metric.5, f32[404,128]{1,0:T(8,128)} %collective-permute-done.near, f32[404,128]{1,0:T(8,128)} %collective-permute-done.1.far, ...), custom_call_target="tpu_custom_call" | custom-call | flops 20000000 | bytes 8000000 | tf_op jit(solution)/shard_map/step_parent/pallas_call | solution.py:651
  79.6 14.7 %all-to-all-done.1 = f32[128,1,3328]{2,1,0:T(1,128)} async-done(((f32[128,1,3328]{2,1,0:T(1,128)}), f32[128,1,3328]{2,1,0:T(1,128)}, u32[]{:S(2)}, u32[]{:S(2)}) %all-to-all-start.1) | async-done | bytes 1703968 | tf_op jit(solution)/shard_map/all_to_all | solution.py:491
  94.2 12.2 %add_panels.1 = f32[100,32,128]{2,1,0:T(8,128)} custom-call(f32[3328,128]{1,0:T(8,128)} %bitcast.13.moved, f32[3200,128]{1,0:T(8,128)} %step_parent.1.parent), custom_call_target="tpu_custom_call" | custom-call | tf_op jit(solution)/shard_map/add_panels/pallas_call | solution.py:665
Async XLA Ops:
  2.6 10.5 %collective-permute-start = (f32[404,128]{1,0:T(8,128)}, f32[404,128]{1,0:T(8,128)}, u32[]{:S(2)}, u32[]{:S(2)}) collective-permute-start(f32[404,128]{1,0:T(8,128)} %get-tuple-element.20), channel_id=1, source_target_pairs={{0,16},{32,48},{64,80},{96,112},{16,0},{48,32},{80,64},{112,96},{1... | collective-permute-start | bytes 620552 | tf_op jit(solution)/shard_map/ppermute | solution.py:501
  4.0 9.1 %collective-permute-start.1 = (f32[404,128]{1,0:T(8,128)}, f32[404,128]{1,0:T(8,128)}, u32[]{:S(2)}, u32[]{:S(2)}) collective-permute-start(f32[404,128]{1,0:T(8,128)} %get-tuple-element.21), channel_id=1, source_target_pairs={{16,32},{48,64},{80,96},{32,16},{64,48},{96,80},{17,33},{49,65},{8... | collective-permute-start | bytes 620552 | tf_op jit(solution)/shard_map/ppermute | solution.py:501
  13.1 35.3 %all-to-all-start = ((f32[128,1,3328]{2,1,0:T(1,128)}), f32[128,1,3328]{2,1,0:T(1,128)}, u32[]{:S(2)}, u32[]{:S(2)}) async-start(f32[128,1,3328]{2,1,0:T(1,128)} %bitcast.23), calls=%async_computation | async-start | bytes 3407872 | tf_op jit(solution)/shard_map/all_to_all | solution.py:491
  27.0 17.7 %collective-permute-start.2 = (f32[160,128]{1,0:T(8,128)}, f32[160,128]{1,0:T(8,128)}, u32[]{:S(2)}, u32[]{:S(2)}) collective-permute-start(f32[160,128]{1,0:T(8,128)} %get-tuple-element.29), channel_id=1, source_target_pairs={{1,0},{2,1},{3,2},{4,3},{5,4},{6,5},{7,6},{8,7},{9,8},{10,9},{11,1... | collective-permute-start | bytes 245768 | tf_op jit(solution)/shard_map/ppermute | solution.py:508
  28.2 16.5 %collective-permute-start.3 = (f32[160,128]{1,0:T(8,128)}, f32[160,128]{1,0:T(8,128)}, u32[]{:S(2)}, u32[]{:S(2)}) collective-permute-start(f32[160,128]{1,0:T(8,128)} %get-tuple-element.30), channel_id=1, source_target_pairs={{0,1},{1,2},{2,3},{3,4},{4,5},{5,6},{6,7},{7,8},{8,9},{9,10},{10,1... | collective-permute-start | bytes 245768 | tf_op jit(solution)/shard_map/ppermute | solution.py:508
  62.5 31.8 %all-to-all-start.1 = ((f32[128,1,3328]{2,1,0:T(1,128)}), f32[128,1,3328]{2,1,0:T(1,128)}, u32[]{:S(2)}, u32[]{:S(2)}) async-start(f32[128,1,3328]{2,1,0:T(1,128)} %bitcast.24), calls=%async_computation.1 | async-start | bytes 3407872 | tf_op jit(solution)/shard_map/all_to_all | solution.py:491
